TPU v7x, 32 devices: a whole 2x2x4 slice. The times are simulated.
32 devices in a mesh: rows: 8 (over y, x, core), heads: 4 (over z).
Axes of the slice: x: 2, y: 2, z: 4, core: 2. Of those that a mesh axis runs over, the one named last changes fastest.
Arguments:
- images: bfloat16 [16, 64, 64, 512], P('heads', 'rows'), may hold values from -6 to 6
- image_sides: int32 [16], replicated, may hold values from 32 to 64, as said below
- labels: int32 [16], replicated, may hold values from 0 to 999
- timesteps: int32 [16], replicated, may hold values from 0 to 999
- cotangent: bfloat16 [16, 64, 64, 512], P('heads', 'rows'), may hold values from -6 to 6
- first_gain: bfloat16 [512], replicated, may hold values from 0.25 to 1.75
- first_bias: bfloat16 [512], replicated, may hold values from -3 to 3
- conv_one: bfloat16 [4608, 512], replicated, may hold values from -0.09375 to 0.09375
- time_proj: bfloat16 [1024, 512], replicated, may hold values from -0.5 to 0.5
- time_bias: bfloat16 [512], replicated, may hold values from -3 to 3
- second_gain: bfloat16 [512], replicated, may hold values from 0.25 to 1.75
- second_bias: bfloat16 [512], replicated, may hold values from -3 to 3
- conv_two: bfloat16 [4608, 512], replicated, may hold values from -0.09375 to 0.09375
- conv_bias: bfloat16 [512], replicated, may hold values from -3 to 3
- third_gain: bfloat16 [512], replicated, may hold values from 0.25 to 1.75
- third_bias: bfloat16 [512], replicated, may hold values from -3 to 3
- proj_in: bfloat16 [512, 512], replicated, may hold values from -0.25 to 0.25
- proj_in_bias: bfloat16 [512], replicated, may hold values from -3 to 3
- attn_gain: bfloat16 [512], replicated, may hold values from 0.25 to 1.75
- attn_bias: bfloat16 [512], replicated, may hold values from -3 to 3
- qkv_proj: bfloat16 [512, 1536], replicated, may hold values from -0.25 to 0.25
- attn_out: bfloat16 [512, 512], replicated, may hold values from -16 to 16
- attn_out_bias: bfloat16 [512], replicated, may hold values from -6 to 6
- class_table: bfloat16 [1000, 512], replicated, may hold values from -6 to 6
- cross_value: bfloat16 [512, 512], replicated, may hold values from -0.25 to 0.25
- cross_out: bfloat16 [512, 512], replicated, may hold values from -0.25 to 0.25
- feed_gain: bfloat16 [512], replicated, may hold values from 0.25 to 1.75
- feed_bias: bfloat16 [512], replicated, may hold values from -3 to 3
- geglu_proj: bfloat16 [512, 4096], replicated, may hold values from -0.25 to 0.25
- geglu_bias: bfloat16 [4096], replicated, may hold values from -3 to 3
- feed_out: bfloat16 [2048, 512], replicated, may hold values from -0.1875 to 0.1875
- feed_out_bias: bfloat16 [512], replicated, may hold values from -7 to 7
- proj_out: bfloat16 [512, 512], replicated, may hold values from -0.25 to 0.25
- proj_out_bias: bfloat16 [512], replicated, may hold values from -6 to 6
Outputs:
- output: bfloat16 [16, 64, 64, 512], P('heads', 'rows')
- grad_images: float32 [16, 64, 64, 512], P('heads', 'rows')
- grad_first_gain: float32 [512], P('rows')
- grad_first_bias: float32 [512], P('rows')
- grad_conv_one: float32 [4608, 512], P('rows')
- grad_time_proj: float32 [1024, 512], P('rows')
- grad_time_bias: float32 [512], P('rows')
- grad_second_gain: float32 [512], P('rows')
- grad_second_bias: float32 [512], P('rows')
- grad_conv_two: float32 [4608, 512], P('rows')
- grad_conv_bias: float32 [512], P('rows')
- grad_third_gain: float32 [512], P('rows')
- grad_third_bias: float32 [512], P('rows')
- grad_proj_in: float32 [512, 512], P('rows')
- grad_proj_in_bias: float32 [512], P('rows')
- grad_attn_gain: float32 [512], P('rows')
- grad_attn_bias: float32 [512], P('rows')
- grad_qkv_proj: float32 [512, 1536], P('rows')
- grad_attn_out: float32 [512, 512], P('rows')
- grad_attn_out_bias: float32 [512], P('rows')
- grad_class_table: float32 [1000, 512], P(None, 'rows')
- grad_cross_value: float32 [512, 512], P('rows')
- grad_cross_out: float32 [512, 512], P('rows')
- grad_feed_gain: float32 [512], P('rows')
- grad_feed_bias: float32 [512], P('rows')
- grad_geglu_proj: float32 [512, 4096], P('rows')
- grad_geglu_bias: float32 [4096], P('rows')
- grad_feed_out: float32 [2048, 512], P('rows')
- grad_feed_out_bias: float32 [512], P('rows')
- grad_proj_out: float32 [512, 512], P('rows')
- grad_proj_out_bias: float32 [512], P('rows')
Inputs may be any that keep to these rules, and one draw needn't show every extreme that they name: `image_sides`: each side is 64, 48 or 32; each block of 4 consecutive images holds at least one of side 64.
All inputs are finite; a program needn't handle non-finite values.
Results may differ from a plain program's by a relative error of at most 0.018.
Values may be sent and summed in bfloat16 or wider, within the bound.
A program may use at most 640 MiB of HBM per device.

v0:
```python
from functools import partial
import math

import jax
import jax.numpy as jnp
from jax import lax
from jax.sharding import PartitionSpec as P

HEADS = 8
GROUPS = 32


GN_EPS = 1e-06
LN_EPS = 1e-05
NEG_FILL = -1e30
HIGH = lax.Precision.HIGHEST


def extended(block, sides, width):
    for axis, dim in sides:
        count = lax.axis_size(axis)
        forward = [(i, i + 1) for i in range(count - 1)]
        backward = [(target, source) for source, target in forward]
        low = lax.ppermute(
            lax.slice_in_dim(block, block.shape[dim] - width, None, axis=dim), axis, forward
        )
        high = lax.ppermute(lax.slice_in_dim(block, 0, width, axis=dim), axis, backward)
        block = jnp.concatenate([low, block, high], axis=dim)
    return block


def rounded(field):
    return field.astype(jnp.bfloat16)


def pixel_mask(sides, row_first, row_count, row_width):
    row_ids = row_first + jnp.arange(row_count, dtype=jnp.int32)
    col_ids = jnp.arange(row_width, dtype=jnp.int32)
    limit = sides[:, None, None]
    within = (row_ids[None, :, None] < limit) & (col_ids[None, None, :] < limit)
    return within.astype(jnp.float32)[..., None]


def group_sums(first_term, second_term):
    shaped = (
        first_term.shape[0],
        first_term.shape[1] * first_term.shape[2],
        GROUPS,
        first_term.shape[3] // GROUPS,
    )
    return lax.psum(
        (
            jnp.sum(first_term.reshape(shaped), axis=(1, 3)),
            jnp.sum(second_term.reshape(shaped), axis=(1, 3)),
        ),
        "rows",
    )


def spread_groups(stat, channels):
    return jnp.repeat(stat, channels // GROUPS, axis=1)[:, None, None, :]


def norm_forward(field, inside, pixel_count, norm_gain, norm_bias):
    channels = field.shape[-1]
    masked = field * inside
    row_total, square = group_sums(masked, masked * field)
    group_mean = row_total / pixel_count
    inv_std = spread_groups(
        lax.rsqrt(square / pixel_count - group_mean * group_mean + GN_EPS), channels
    )
    normed = (field - spread_groups(group_mean, channels)) * inv_std
    return (normed * norm_gain + norm_bias, normed, inv_std)


def norm_backward(grad_norm, normed, inv_std, inside, pixel_count, norm_gain):
    channels = normed.shape[-1]
    grad_norm = grad_norm * inside
    scaled = grad_norm * norm_gain
    row_total, crossed = group_sums(scaled, scaled * normed)
    grad_field = (
        inside
        * inv_std
        * (
            scaled
            - spread_groups(row_total / pixel_count, channels)
            - normed * spread_groups(crossed / pixel_count, channels)
        )
    )
    return (
        grad_field,
        jnp.sum(grad_norm * normed, axis=(0, 1, 2)),
        jnp.sum(grad_norm, axis=(0, 1, 2)),
    )


def layer_norm(field, norm_gain, norm_bias):
    centre = jnp.mean(field, axis=-1, keepdims=True)
    centred = field - centre
    spread = jnp.mean(centred * centred, axis=-1, keepdims=True)
    return centred * lax.rsqrt(spread + LN_EPS) * norm_gain + norm_bias


def geglu_act(gate_pair):
    half_dim = gate_pair.shape[-1] // 2
    return gate_pair[..., :half_dim] * jax.nn.gelu(gate_pair[..., half_dim:], approximate=False)


def conv_taps(field, flipped):
    padded = extended(field, (("rows", 1),), 1)
    padded = jnp.pad(padded, ((0, 0), (0, 0), (1, 1), (0, 0)))
    band_rows, row_width = (field.shape[1], field.shape[2])
    offsets = [
        (2 - row_off, 2 - col_off) if flipped else (row_off, col_off)
        for row_off in range(3)
        for col_off in range(3)
    ]
    return jnp.stack(
        [
            padded[:, top_row : top_row + band_rows, left_col : left_col + row_width, :]
            for top_row, left_col in offsets
        ],
        axis=3,
    )


def conv_apply(tap_stack, weight):
    channels = tap_stack.shape[-1]
    return jnp.einsum(
        "brwtc,tco->brwo",
        tap_stack,
        weight.reshape(9, channels, -1),
        preferred_element_type=jnp.float32,
    )


def conv_weight_grad(tap_stack, grads_low):
    channels = tap_stack.shape[-1]
    return jnp.einsum(
        "brwtc,brwo->tco", tap_stack, grads_low, preferred_element_type=jnp.float32
    ).reshape(9 * channels, -1)


def conv_back(grads_low, weight):
    channels = grads_low.shape[-1]
    return jnp.einsum(
        "brwtc,tic->brwi",
        conv_taps(grads_low, True),
        weight.reshape(9, channels, channels),
        preferred_element_type=jnp.float32,
    )


def tokens_dot(inputs_low, weight):
    return jnp.einsum("blc,co->blo", inputs_low, weight, preferred_element_type=jnp.float32)


def weight_grad(inputs_low, grads_low):
    return jnp.einsum("blc,blo->co", inputs_low, grads_low, preferred_element_type=jnp.float32)


def back_dot(grads_low, weight):
    return jnp.einsum("blo,co->blc", grads_low, weight, preferred_element_type=jnp.float32)


def time_features(time_steps, dims):
    half_dim = dims // 2
    frequency = jnp.exp(-math.log(10000.0) * jnp.arange(half_dim, dtype=jnp.float32) / half_dim)
    angles = time_steps.astype(jnp.float32)[:, None] * frequency[None, :]
    return jnp.concatenate([jnp.cos(angles), jnp.sin(angles)], axis=-1)


def to_heads(field):
    return lax.all_to_all(field, "heads", split_axis=3, concat_axis=0, tiled=True)


def from_heads(field):
    return lax.all_to_all(field, "heads", split_axis=0, concat_axis=3, tiled=True)


def masked_scores(queries, keys_all, key_valid, score_scale):
    scores = (
        jnp.einsum("gqhd,gkhd->ghqk", queries, keys_all, preferred_element_type=jnp.float32)
        * score_scale
    )
    return jnp.where(key_valid[:, None, None, :] > 0, scores, NEG_FILL)


def attend(pieces, score_scale):
    queries, keys_all, values_all, key_valid = pieces
    scores = masked_scores(queries, keys_all, key_valid, score_scale)
    row_max = jnp.max(scores, axis=-1, keepdims=True)
    raw_weights = jnp.exp(scores - row_max)
    row_total = jnp.sum(raw_weights, axis=-1, keepdims=True)
    prob_low = rounded(raw_weights / row_total)
    mixed_out = jnp.einsum(
        "ghqk,gkhd->gqhd", prob_low, values_all, preferred_element_type=jnp.float32
    )
    return (rounded(mixed_out), (row_max + jnp.log(row_total))[..., 0])


def attend_back(pieces, score_scale, with_keys):
    queries, keys_all, values_all, key_valid, grad_mixed, log_total = pieces
    scores = masked_scores(queries, keys_all, key_valid, score_scale)
    probs = jnp.exp(scores - log_total[..., None])
    grad_probs = jnp.einsum(
        "gqhd,gkhd->ghqk", grad_mixed, values_all, preferred_element_type=jnp.float32
    )
    row_delta = jnp.sum(probs * grad_probs, axis=-1, keepdims=True)
    grad_scores = rounded(probs * (grad_probs - row_delta))
    grad_queries = (
        jnp.einsum("ghqk,gkhd->gqhd", grad_scores, keys_all, preferred_element_type=jnp.float32)
        * score_scale
    )
    grad_keys = (
        jnp.einsum("ghqk,gqhd->gkhd", grad_scores, queries, preferred_element_type=jnp.float32)
        * score_scale
    )
    grad_values = jnp.einsum(
        "ghqk,gqhd->gkhd", rounded(probs), grad_mixed, preferred_element_type=jnp.float32
    )
    return (grad_queries, grad_keys, grad_values)


def per_device(
    images,
    image_sides,
    labels,
    timesteps,
    cotangent,
    first_gain,
    first_bias,
    conv_one,
    time_proj,
    time_bias,
    second_gain,
    second_bias,
    conv_two,
    conv_bias,
    third_gain,
    third_bias,
    proj_in,
    proj_in_bias,
    attn_gain,
    attn_bias,
    qkv_proj,
    attn_out,
    attn_out_bias,
    class_table,
    cross_value,
    cross_out,
    feed_gain,
    feed_bias,
    geglu_proj,
    geglu_bias,
    feed_out,
    feed_out_bias,
    proj_out,
    proj_out_bias,
):
    image_count, band_rows, row_width, channels = images.shape
    tokens = band_rows * row_width
    head_dim = channels // HEADS
    score_scale = head_dim ** (-0.5)
    first_image = lax.axis_index("heads") * image_count
    first_row = lax.axis_index("rows") * band_rows
    own_sides = lax.dynamic_slice_in_dim(image_sides, first_image, image_count)
    own_labels = lax.dynamic_slice_in_dim(labels, first_image, image_count)
    own_steps = lax.dynamic_slice_in_dim(timesteps, first_image, image_count)
    inside = pixel_mask(own_sides, first_row, band_rows, row_width)
    pixel_count = (own_sides * own_sides * (channels // GROUPS)).astype(jnp.float32)[:, None]
    start = images.astype(jnp.float32) * inside
    norm_one, normed_one, std_one = norm_forward(start, inside, pixel_count, first_gain, first_bias)
    act_one = rounded(jax.nn.silu(norm_one) * inside)
    taps_one = conv_taps(act_one, False)
    time_embed = rounded(jax.nn.silu(time_features(own_steps, time_proj.shape[0])))
    time_shift = jnp.dot(time_embed, time_proj, preferred_element_type=jnp.float32)
    hidden_one = conv_apply(taps_one, conv_one) + time_shift[:, None, None, :] + time_bias
    norm_two, normed_two, std_two = norm_forward(
        hidden_one, inside, pixel_count, second_gain, second_bias
    )
    act_two = rounded(jax.nn.silu(norm_two) * inside)
    taps_two = conv_taps(act_two, False)
    residual = start + conv_apply(taps_two, conv_two) + conv_bias
    norm_three, normed_three, std_three = norm_forward(
        residual, inside, pixel_count, third_gain, third_bias
    )
    flat_in = rounded(norm_three.reshape(image_count, tokens, channels))
    stream = tokens_dot(flat_in, proj_in) + proj_in_bias
    attn_in = rounded(layer_norm(stream, attn_gain, attn_bias))
    qkv_rows = rounded(tokens_dot(attn_in, qkv_proj)).reshape(
        image_count, tokens, 3, HEADS, head_dim
    )
    qkv_rows = to_heads(qkv_rows)
    item_count = qkv_rows.shape[0]
    group_size = HEADS // qkv_rows.shape[3]
    queries, keys_own, values_own = (qkv_rows[:, :, 0], qkv_rows[:, :, 1], qkv_rows[:, :, 2])
    keys_all, values_all = (
        lax.all_gather(keys_own, "rows", axis=1, tiled=True),
        lax.all_gather(values_own, "rows", axis=1, tiled=True),
    )
    full_rows = keys_all.shape[1] // row_width
    key_valid = pixel_mask(image_sides, 0, full_rows, row_width)[..., 0].reshape(item_count, -1)

    def grouped(field):
        return field.reshape((field.shape[0] // group_size, group_size) + field.shape[1:])

    def ungrouped(field):
        return field.reshape((-1,) + field.shape[2:])

    mixed_out, log_total = lax.map(
        partial(attend, score_scale=score_scale),
        (grouped(queries), grouped(keys_all), grouped(values_all), grouped(key_valid)),
    )
    mixed_out = ungrouped(mixed_out)[:, :, None]
    log_total = ungrouped(log_total)
    mixed_out = from_heads(mixed_out)
    mixed_out = mixed_out.reshape(image_count, tokens, channels)
    stream_two = stream + tokens_dot(mixed_out, attn_out) + attn_out_bias
    one_hot = rounded(
        (own_labels[:, None] == jnp.arange(class_table.shape[0], dtype=jnp.int32)[None, :]).astype(
            jnp.float32
        )
    )
    context = jnp.dot(one_hot, class_table, preferred_element_type=jnp.float32)
    value_vec = jnp.dot(rounded(context), cross_value, preferred_element_type=jnp.float32)
    value_low = rounded(value_vec)
    cross_term = jnp.dot(value_low, cross_out, preferred_element_type=jnp.float32)
    stream_three = stream_two + cross_term[:, None, :]
    feed_in = rounded(layer_norm(stream_three, feed_gain, feed_bias))
    gate_pair = tokens_dot(feed_in, geglu_proj) + geglu_bias
    gated_hidden = rounded(geglu_act(gate_pair))
    stream_four = stream_three + tokens_dot(gated_hidden, feed_out) + feed_out_bias
    last_in = rounded(stream_four)
    branch = tokens_dot(last_in, proj_out) + proj_out_bias
    output = (residual + branch.reshape(images.shape)) * inside
    grad_out = cotangent.astype(jnp.float32) * inside
    grad_branch = grad_out.reshape(image_count, tokens, channels)
    grad_proj_out_bias = jnp.sum(grad_branch, axis=(0, 1))
    low_branch = rounded(grad_branch)
    grad_proj_out = weight_grad(last_in, low_branch)
    grad_four = back_dot(low_branch, proj_out)
    grad_feed_out_bias = jnp.sum(grad_four, axis=(0, 1))
    low_feed = rounded(grad_four)
    grad_feed_out = weight_grad(gated_hidden, low_feed)
    grad_gated = back_dot(low_feed, feed_out)
    geglu_value, geglu_pull = jax.vjp(geglu_act, gate_pair)
    grad_pair = geglu_pull(grad_gated)[0]
    grad_geglu_bias = jnp.sum(grad_pair, axis=(0, 1))
    low_pair = rounded(grad_pair)
    grad_geglu_proj = weight_grad(feed_in, low_pair)
    feed_value, feed_pull = jax.vjp(
        layer_norm, stream_three, feed_gain.astype(jnp.float32), feed_bias.astype(jnp.float32)
    )
    norm_part, grad_feed_gain, grad_feed_bias = feed_pull(back_dot(low_pair, geglu_proj))
    grad_three = grad_four + norm_part
    grad_cross = jnp.sum(grad_three, axis=1)
    grad_cross_out = jnp.dot(value_low.astype(jnp.float32).T, grad_cross, precision=HIGH)
    grad_value = jnp.dot(grad_cross, cross_out.astype(jnp.float32).T, precision=HIGH)
    grad_cross_value = jnp.dot(context.T, grad_value, precision=HIGH)
    grad_context = jnp.dot(grad_value, cross_value.astype(jnp.float32).T, precision=HIGH)
    grad_class_table = jnp.dot(one_hot.astype(jnp.float32).T, grad_context, precision=HIGH)
    grad_attn_out_bias = jnp.sum(grad_three, axis=(0, 1))
    low_attn = rounded(grad_three)
    grad_attn_out = weight_grad(mixed_out, low_attn)
    grad_mixed = rounded(back_dot(low_attn, attn_out)).reshape(
        image_count, tokens, 1, HEADS, head_dim
    )
    grad_mixed = to_heads(grad_mixed)
    grad_mixed = grad_mixed[:, :, 0]
    grad_queries, grad_keys_all, grad_values_all = lax.map(
        partial(attend_back, score_scale=score_scale, with_keys=True),
        (
            grouped(queries),
            grouped(keys_all),
            grouped(values_all),
            grouped(key_valid),
            grouped(grad_mixed),
            grouped(log_total),
        ),
    )
    grad_keys, grad_values = (
        lax.psum_scatter(
            ungrouped(grad_keys_all).astype(jnp.bfloat16), "rows", scatter_dimension=1, tiled=True
        ).astype(jnp.float32),
        lax.psum_scatter(
            ungrouped(grad_values_all).astype(jnp.bfloat16), "rows", scatter_dimension=1, tiled=True
        ).astype(jnp.float32),
    )
    grad_queries = ungrouped(grad_queries)
    grad_qkv = rounded(jnp.stack([grad_queries, grad_keys, grad_values], axis=2))
    grad_qkv = from_heads(grad_qkv)
    grad_qkv = grad_qkv.reshape(image_count, tokens, 3 * channels)
    grad_qkv_proj = weight_grad(attn_in, grad_qkv)
    attn_value, attn_pull = jax.vjp(
        layer_norm, stream, attn_gain.astype(jnp.float32), attn_bias.astype(jnp.float32)
    )
    norm_part, grad_attn_gain, grad_attn_bias = attn_pull(back_dot(grad_qkv, qkv_proj))
    grad_stream = grad_three + norm_part
    grad_proj_in_bias = jnp.sum(grad_stream, axis=(0, 1))
    low_in = rounded(grad_stream)
    grad_proj_in = weight_grad(flat_in, low_in)
    grad_norm_three = back_dot(low_in, proj_in).reshape(images.shape)
    resid_part, grad_third_gain, grad_third_bias = norm_backward(
        grad_norm_three, normed_three, std_three, inside, pixel_count, third_gain
    )
    grad_residual = grad_out + resid_part
    grad_conv_bias = jnp.sum(grad_residual, axis=(0, 1, 2))
    low_two = rounded(grad_residual)
    grad_conv_two = conv_weight_grad(taps_two, low_two)
    grad_act_two = conv_back(low_two, conv_two)
    silu_two, silu_pull_two = jax.vjp(jax.nn.silu, norm_two)
    grad_norm_two = silu_pull_two(grad_act_two * inside)[0]
    grad_hidden, grad_second_gain, grad_second_bias = norm_backward(
        grad_norm_two, normed_two, std_two, inside, pixel_count, second_gain
    )
    grad_time_bias = jnp.sum(grad_hidden, axis=(0, 1, 2))
    grad_shift = jnp.sum(grad_hidden, axis=(1, 2))
    grad_time_proj = jnp.dot(time_embed.astype(jnp.float32).T, grad_shift, precision=HIGH)
    low_one = rounded(grad_hidden)
    grad_conv_one = conv_weight_grad(taps_one, low_one)
    grad_act_one = conv_back(low_one, conv_one)
    silu_one, silu_pull_one = jax.vjp(jax.nn.silu, norm_one)
    grad_norm_one = silu_pull_one(grad_act_one * inside)[0]
    start_part, grad_first_gain, grad_first_bias = norm_backward(
        grad_norm_one, normed_one, std_one, inside, pixel_count, first_gain
    )
    grad_images = (grad_residual + start_part) * inside
    summed = (
        lax.psum_scatter(
            grad_first_gain.astype(jnp.bfloat16), "rows", scatter_dimension=0, tiled=True
        ).astype(jnp.float32),
        lax.psum_scatter(
            grad_first_bias.astype(jnp.bfloat16), "rows", scatter_dimension=0, tiled=True
        ).astype(jnp.float32),
        lax.psum_scatter(
            grad_conv_one.astype(jnp.bfloat16), "rows", scatter_dimension=0, tiled=True
        ).astype(jnp.float32),
        lax.psum_scatter(
            grad_time_proj.astype(jnp.bfloat16), "rows", scatter_dimension=0, tiled=True
        ).astype(jnp.float32),
        lax.psum_scatter(
            grad_time_bias.astype(jnp.bfloat16), "rows", scatter_dimension=0, tiled=True
        ).astype(jnp.float32),
        lax.psum_scatter(
            grad_second_gain.astype(jnp.bfloat16), "rows", scatter_dimension=0, tiled=True
        ).astype(jnp.float32),
        lax.psum_scatter(
            grad_second_bias.astype(jnp.bfloat16), "rows", scatter_dimension=0, tiled=True
        ).astype(jnp.float32),
        lax.psum_scatter(
            grad_conv_two.astype(jnp.bfloat16), "rows", scatter_dimension=0, tiled=True
        ).astype(jnp.float32),
        lax.psum_scatter(
            grad_conv_bias.astype(jnp.bfloat16), "rows", scatter_dimension=0, tiled=True
        ).astype(jnp.float32),
        lax.psum_scatter(
            grad_third_gain.astype(jnp.bfloat16), "rows", scatter_dimension=0, tiled=True
        ).astype(jnp.float32),
        lax.psum_scatter(
            grad_third_bias.astype(jnp.bfloat16), "rows", scatter_dimension=0, tiled=True
        ).astype(jnp.float32),
        lax.psum_scatter(
            grad_proj_in.astype(jnp.bfloat16), "rows", scatter_dimension=0, tiled=True
        ).astype(jnp.float32),
        lax.psum_scatter(
            grad_proj_in_bias.astype(jnp.bfloat16), "rows", scatter_dimension=0, tiled=True
        ).astype(jnp.float32),
        lax.psum_scatter(
            grad_attn_gain.astype(jnp.bfloat16), "rows", scatter_dimension=0, tiled=True
        ).astype(jnp.float32),
        lax.psum_scatter(
            grad_attn_bias.astype(jnp.bfloat16), "rows", scatter_dimension=0, tiled=True
        ).astype(jnp.float32),
        lax.psum_scatter(
            grad_qkv_proj.astype(jnp.bfloat16), "rows", scatter_dimension=0, tiled=True
        ).astype(jnp.float32),
        lax.psum_scatter(
            grad_attn_out.astype(jnp.bfloat16), "rows", scatter_dimension=0, tiled=True
        ).astype(jnp.float32),
        lax.psum_scatter(
            grad_attn_out_bias.astype(jnp.bfloat16), "rows", scatter_dimension=0, tiled=True
        ).astype(jnp.float32),
        lax.psum_scatter(
            grad_class_table.astype(jnp.bfloat16), "rows", scatter_dimension=1, tiled=True
        ).astype(jnp.float32),
        lax.psum_scatter(
            grad_cross_value.astype(jnp.bfloat16), "rows", scatter_dimension=0, tiled=True
        ).astype(jnp.float32),
        lax.psum_scatter(
            grad_cross_out.astype(jnp.bfloat16), "rows", scatter_dimension=0, tiled=True
        ).astype(jnp.float32),
        lax.psum_scatter(
            grad_feed_gain.astype(jnp.bfloat16), "rows", scatter_dimension=0, tiled=True
        ).astype(jnp.float32),
        lax.psum_scatter(
            grad_feed_bias.astype(jnp.bfloat16), "rows", scatter_dimension=0, tiled=True
        ).astype(jnp.float32),
        lax.psum_scatter(
            grad_geglu_proj.astype(jnp.bfloat16), "rows", scatter_dimension=0, tiled=True
        ).astype(jnp.float32),
        lax.psum_scatter(
            grad_geglu_bias.astype(jnp.bfloat16), "rows", scatter_dimension=0, tiled=True
        ).astype(jnp.float32),
        lax.psum_scatter(
            grad_feed_out.astype(jnp.bfloat16), "rows", scatter_dimension=0, tiled=True
        ).astype(jnp.float32),
        lax.psum_scatter(
            grad_feed_out_bias.astype(jnp.bfloat16), "rows", scatter_dimension=0, tiled=True
        ).astype(jnp.float32),
        lax.psum_scatter(
            grad_proj_out.astype(jnp.bfloat16), "rows", scatter_dimension=0, tiled=True
        ).astype(jnp.float32),
        lax.psum_scatter(
            grad_proj_out_bias.astype(jnp.bfloat16), "rows", scatter_dimension=0, tiled=True
        ).astype(jnp.float32),
    )
    (
        s01,
        s02,
        s03,
        s04,
        s05,
        s06,
        s07,
        s08,
        s09,
        s10,
        s11,
        s12,
        s13,
        s14,
        s15,
        s16,
        s17,
        s18,
        s19,
        s20,
        s21,
        s22,
        s23,
        s24,
        s25,
        s26,
        s27,
        s28,
        s29,
    ) = summed
    reduced = (
        lax.psum(s01.astype(jnp.bfloat16), "heads").astype(jnp.float32),
        lax.psum(s02.astype(jnp.bfloat16), "heads").astype(jnp.float32),
        lax.psum(s03.astype(jnp.bfloat16), "heads").astype(jnp.float32),
        lax.psum(s04.astype(jnp.bfloat16), "heads").astype(jnp.float32),
        lax.psum(s05.astype(jnp.bfloat16), "heads").astype(jnp.float32),
        lax.psum(s06.astype(jnp.bfloat16), "heads").astype(jnp.float32),
        lax.psum(s07.astype(jnp.bfloat16), "heads").astype(jnp.float32),
        lax.psum(s08.astype(jnp.bfloat16), "heads").astype(jnp.float32),
        lax.psum(s09.astype(jnp.bfloat16), "heads").astype(jnp.float32),
        lax.psum(s10.astype(jnp.bfloat16), "heads").astype(jnp.float32),
        lax.psum(s11.astype(jnp.bfloat16), "heads").astype(jnp.float32),
        lax.psum(s12.astype(jnp.bfloat16), "heads").astype(jnp.float32),
        lax.psum(s13.astype(jnp.bfloat16), "heads").astype(jnp.float32),
        lax.psum(s14.astype(jnp.bfloat16), "heads").astype(jnp.float32),
        lax.psum(s15.astype(jnp.bfloat16), "heads").astype(jnp.float32),
        lax.psum(s16.astype(jnp.bfloat16), "heads").astype(jnp.float32),
        lax.psum(s17.astype(jnp.bfloat16), "heads").astype(jnp.float32),
        lax.psum(s18.astype(jnp.bfloat16), "heads").astype(jnp.float32),
        lax.psum(s19.astype(jnp.bfloat16), "heads").astype(jnp.float32),
        lax.psum(s20.astype(jnp.bfloat16), "heads").astype(jnp.float32),
        lax.psum(s21.astype(jnp.bfloat16), "heads").astype(jnp.float32),
        lax.psum(s22.astype(jnp.bfloat16), "heads").astype(jnp.float32),
        lax.psum(s23.astype(jnp.bfloat16), "heads").astype(jnp.float32),
        lax.psum(s24.astype(jnp.bfloat16), "heads").astype(jnp.float32),
        lax.psum(s25.astype(jnp.bfloat16), "heads").astype(jnp.float32),
        lax.psum(s26.astype(jnp.bfloat16), "heads").astype(jnp.float32),
        lax.psum(s27.astype(jnp.bfloat16), "heads").astype(jnp.float32),
        lax.psum(s28.astype(jnp.bfloat16), "heads").astype(jnp.float32),
        lax.psum(s29.astype(jnp.bfloat16), "heads").astype(jnp.float32),
    )
    return (rounded(output), grad_images) + tuple(reduced)


def solution(mesh):
    return jax.shard_map(
        per_device,
        mesh=mesh,
        in_specs=(
            P("heads", "rows", None, None),
            P(),
            P(),
            P(),
            P("heads", "rows", None, None),
            P(),
            P(),
            P(),
            P(),
            P(),
            P(),
            P(),
            P(),
            P(),
            P(),
            P(),
            P(),
            P(),
            P(),
            P(),
            P(),
            P(),
            P(),
            P(),
            P(),
            P(),
            P(),
            P(),
            P(),
            P(),
            P(),
            P(),
            P(),
            P(),
        ),
        out_specs=(
            P("heads", "rows", None, None),
            P("heads", "rows", None, None),
            P("rows"),
            P("rows"),
            P("rows", None),
            P("rows", None),
            P("rows"),
            P("rows"),
            P("rows"),
            P("rows", None),
            P("rows"),
            P("rows"),
            P("rows"),
            P("rows", None),
            P("rows"),
            P("rows"),
            P("rows"),
            P("rows", None),
            P("rows", None),
            P("rows"),
            P(None, "rows"),
            P("rows", None),
            P("rows", None),
            P("rows"),
            P("rows"),
            P("rows", None),
            P("rows"),
            P("rows", None),
            P("rows"),
            P("rows", None),
            P("rows"),
        ),
        check_vma=False,
    )
```

profile of v0, /device:TPU:0, one launch (start us, length us, event | category | flops | bytes accessed | tf_op | source)
XLA Modules:
  0.0 2720.8 jit_solution(1642076416042184390)
XLA Ops:
  164.1 141.6 %all_to_all.63 = bf16[4,512,3,8,64]{1,4,2,0,3:T(8,128)(2,1)S(1)} all-to-all(bf16[4,512,3,8,64]{1,4,2,0,3:T(8,128)(2,1)S(1)} %copy.221), channel_id=1, replica_groups=mesh['rows'=8,'heads'=4] {'heads'}, dimensions={3} | all-to-all | bytes 12582912 | tf_op jit(solution)/shard_map/all_to_all | solution.py:174
  310.6 91.8 %all-gather.7.cloned.1.call-done = bf16[16,4096,1,2,64]{1,4,3,2,0:T(8,128)(2,1)} async-done(((bf16[16,512,1,2,64]{1,4,3,2,0:T(8,128)(2,1)}), bf16[16,4096,1,2,64]{1,4,3,2,0:T(8,128)(2,1)}) %all-gather.7.cloned.1.call-update) | async-done | bytes 16777232 | tf_op jit(solution)/shard_map/all_gather | solution.py:299
  402.4 95.0 %all-gather.5.cloned.1.call-done = bf16[16,4096,1,2,64]{1,4,3,2,0:T(8,128)(2,1)} async-done(((bf16[16,512,1,2,64]{1,4,3,2,0:T(8,128)(2,1)}), bf16[16,4096,1,2,64]{1,4,3,2,0:T(8,128)(2,1)}) %all-gather.5.cloned.1.call-update) | async-done | bytes 16777232 | tf_op jit(solution)/shard_map/all_gather | solution.py:300
  497.4 301.1 %while.26 = (s32[]{:T(128)}, bf16[4,4,512,2,64]{2,4,3,1,0:T(8,128)(2,1)}, f32[4,4,2,512]{3,2,1,0:T(2,128)}, bf16[4,4,4096,2,64]{2,4,3,1,0:T(8,128)(2,1)}, f32[4,...) while((s32[]{:T(128)}, ...), condition=%wide.region_23.24_spmd, body=%wide.region_20.23_spmd.sunk | while | flops 4496568320 | bytes 211028080 | solution.py:311
  497.5 26.6 fusion.261
  545.5 26.6 fusion.263
  572.8 26.6 fusion.261
  620.8 26.6 fusion.263
  648.0 26.6 fusion.261
  696.1 26.6 fusion.263
  723.3 26.6 fusion.261
  771.3 26.6 fusion.263
  816.9 35.5 %all-to-all-done.1 = bf16[16,512,1,2,64]{1,4,3,2,0:T(8,128)(2,1)} async-done(((bf16[16,512,1,2,64]{1,4,3,2,0:T(8,128)(2,1)}), bf16[16,512,1,2,64]{1,4,3,2,0:T(8,128)(2,1)}, u32[]{:S(2)}, u32[]{:S(2)}) %all-to-all-start.1) | async-done | bytes 2097184 | tf_op jit(solution)/shard_map/all_to_all | solution.py:178
  877.2 47.2 %multiply_add_fusion = (f32[4,512,2048]{2,1,0:T(8,128)}, f32[4,512,2048]{2,1,0:T(8,128)}, f32[4,512,2048]{2,1,0:T(8,128)}) fusion(f32[4,512,4096]{2,1,0:T(8,128)} %broadcast_add_fusion, bf16[2048,512]{1,0:T(8,128)(2,1)S(1)} %copy-done, f32[4,512,512]{2,1,0:T(8,128)S(1)} %copy-done.19), kind=kOutput, calls=%fused_computation.65 | convolution fusion | flops 4598005760 | bytes 90177536 | tf_op jit(solution)/shard_map/blo,co->blc/dot_general | solution.py:163
  924.4 32.5 %fusion.70 = (f32[4,512,2048]{2,1,0:T(8,128)}, bf16[4,512,2048]{2,1,0:T(8,128)(2,1)}) fusion(f32[4,512,2048]{2,1,0:T(8,128)} %get-tuple-element.342, f32[4,512,2048]{2,1,0:T(8,128)} %get-tuple-element.296, f32[4,512,4096]{2,1,0:T(8,128)} %broadcast_add_fusion), kind=kLoop, calls=%fused_computation.100 | loop fusion | flops 20971520 | bytes 92274688 | tf_op jit(solution)/shard_map/transpose(jvp())/mul | solution.py:106
  1000.1 47.9 %all-to-all-done.2 = bf16[4,512,1,8,64]{1,4,0,2,3:T(8,128)(2,1)} async-done(((bf16[4,512,1,8,64]{1,4,0,2,3:T(8,128)(2,1)}), bf16[4,512,1,8,64]{1,4,0,2,3:T(8,128)(2,1)}, u32[]{:S(2)}, u32[]{:S(2)}) %all-to-all-start.2) | async-done | bytes 2097184 | tf_op jit(solution)/shard_map/all_to_all | solution.py:174
  1047.9 749.5 %while.27 = (s32[]{:T(128)}, bf16[4,4,512,2,64]{2,4,3,1,0:T(8,128)(2,1)}, bf16[4,4,4096,2,64]{2,4,3,1,0:T(8,128)(2,1)}, bf16[4,4,4096,2,64]{2,4,3,1,0:T(8,128)(2...) while((s32[]{:T(128)}, ...), condition=%wide.region_30.31_spmd, body=%wide.region_28.30_spmd.sunk | while | flops 10890784768 | bytes 536007776 | solution.py:371
  1075.8 46.6 %multiply_reduce_fusion.21 = (f32[4,2,512]{2,1,0:T(2,128)S(1)}, f32[4,2,512,4096]{3,2,1,0:T(8,128)}) fusion(f32[4,2,512,4096]{3,2,1,0:T(8,128)} %fusion.270, f32[4,2,512]{2,1,0:T(2,128)S(1)} %dynamic-slice_bitcast_fusion.2, bf16[4,4,4096,2,64]{2,4,3,1,0:T(8,128)(2,1)} %get-tuple-element.516, s32[]{:T(128)S(6)} %copy.344, ...), kind=kOutput, calls=%fused_computation.24.clone.3 | convolution fusion | flops 2231365632 | bytes 138986496 | tf_op jit(solution)/shard_map/while/body/eval_jaxpr/gqhd,gkhd->ghqk/dot_general | solution.py:183
  1122.3 53.0 %multiply_convert_fusion.7 = bf16[4,2,512,4096]{3,2,1,0:T(8,128)(2,1)} fusion(f32[4,2,512,4096]{3,2,1,0:T(8,128)} %get-tuple-element.464, f32[4,2,512,4096]{3,2,1,0:T(8,128)} %fusion.270, f32[4,2,512]{2,1,0:T(2,128)S(1)} %get-tuple-element.465), kind=kLoop, calls=%fused_computation.23.clone.1 | loop fusion | flops 50331648 | bytes 167788544 | tf_op jit(solution)/shard_map/while/body/eval_jaxpr/convert_element_type | solution.py:33
  1263.2 46.6 %multiply_reduce_fusion.21 = (f32[4,2,512]{2,1,0:T(2,128)S(1)}, f32[4,2,512,4096]{3,2,1,0:T(8,128)}) fusion(f32[4,2,512,4096]{3,2,1,0:T(8,128)} %fusion.270, f32[4,2,512]{2,1,0:T(2,128)S(1)} %dynamic-slice_bitcast_fusion.2, bf16[4,4,4096,2,64]{2,4,3,1,0:T(8,128)(2,1)} %get-tuple-element.516, s32[]{:T(128)S(6)} %copy.344, ...), kind=kOutput, calls=%fused_computation.24.clone.3 | convolution fusion | flops 2231365632 | bytes 138986496 | tf_op jit(solution)/shard_map/while/body/eval_jaxpr/gqhd,gkhd->ghqk/dot_general | solution.py:183
  1309.8 53.0 %multiply_convert_fusion.7 = bf16[4,2,512,4096]{3,2,1,0:T(8,128)(2,1)} fusion(f32[4,2,512,4096]{3,2,1,0:T(8,128)} %get-tuple-element.464, f32[4,2,512,4096]{3,2,1,0:T(8,128)} %fusion.270, f32[4,2,512]{2,1,0:T(2,128)S(1)} %get-tuple-element.465), kind=kLoop, calls=%fused_computation.23.clone.1 | loop fusion | flops 50331648 | bytes 167788544 | tf_op jit(solution)/shard_map/while/body/eval_jaxpr/convert_element_type | solution.py:33
  1424.4 26.1 fusion.270
  1450.5 46.6 %multiply_reduce_fusion.21 = (f32[4,2,512]{2,1,0:T(2,128)S(1)}, f32[4,2,512,4096]{3,2,1,0:T(8,128)}) fusion(f32[4,2,512,4096]{3,2,1,0:T(8,128)} %fusion.270, f32[4,2,512]{2,1,0:T(2,128)S(1)} %dynamic-slice_bitcast_fusion.2, bf16[4,4,4096,2,64]{2,4,3,1,0:T(8,128)(2,1)} %get-tuple-element.516, s32[]{:T(128)S(6)} %copy.344, ...), kind=kOutput, calls=%fused_computation.24.clone.3 | convolution fusion | flops 2231365632 | bytes 138986496 | tf_op jit(solution)/shard_map/while/body/eval_jaxpr/gqhd,gkhd->ghqk/dot_general | solution.py:183
  1497.0 53.0 %multiply_convert_fusion.7 = bf16[4,2,512,4096]{3,2,1,0:T(8,128)(2,1)} fusion(f32[4,2,512,4096]{3,2,1,0:T(8,128)} %get-tuple-element.464, f32[4,2,512,4096]{3,2,1,0:T(8,128)} %fusion.270, f32[4,2,512]{2,1,0:T(2,128)S(1)} %get-tuple-element.465), kind=kLoop, calls=%fused_computation.23.clone.1 | loop fusion | flops 50331648 | bytes 167788544 | tf_op jit(solution)/shard_map/while/body/eval_jaxpr/convert_element_type | solution.py:33
  1637.7 46.6 %multiply_reduce_fusion.21 = (f32[4,2,512]{2,1,0:T(2,128)S(1)}, f32[4,2,512,4096]{3,2,1,0:T(8,128)}) fusion(f32[4,2,512,4096]{3,2,1,0:T(8,128)} %fusion.270, f32[4,2,512]{2,1,0:T(2,128)S(1)} %dynamic-slice_bitcast_fusion.2, bf16[4,4,4096,2,64]{2,4,3,1,0:T(8,128)(2,1)} %get-tuple-element.516, s32[]{:T(128)S(6)} %copy.344, ...), kind=kOutput, calls=%fused_computation.24.clone.3 | convolution fusion | flops 2231365632 | bytes 138986496 | tf_op jit(solution)/shard_map/while/body/eval_jaxpr/gqhd,gkhd->ghqk/dot_general | solution.py:183
  1684.2 53.0 %multiply_convert_fusion.7 = bf16[4,2,512,4096]{3,2,1,0:T(8,128)(2,1)} fusion(f32[4,2,512,4096]{3,2,1,0:T(8,128)} %get-tuple-element.464, f32[4,2,512,4096]{3,2,1,0:T(8,128)} %fusion.270, f32[4,2,512]{2,1,0:T(2,128)S(1)} %get-tuple-element.465), kind=kLoop, calls=%fused_computation.23.clone.1 | loop fusion | flops 50331648 | bytes 167788544 | tf_op jit(solution)/shard_map/while/body/eval_jaxpr/convert_element_type | solution.py:33
  1798.2 113.5 %reduce-scatter.17.cloned.1.call-done = bf16[16,512,2,64]{1,3,2,0:T(8,128)(2,1)} async-done(((bf16[16,4096,2,64]{1,3,2,0:T(8,128)(2,1)}), bf16[16,512,2,64]{1,3,2,0:T(8,128)(2,1)}) %reduce-scatter.17.cloned.1.call-update) | async-done | bytes 2097168 | tf_op jit(solution)/shard_map/reduce_scatter | solution.py:386
  1911.7 119.4 %reduce-scatter.15.cloned.1.call-done = bf16[16,512,2,64]{1,3,2,0:T(8,128)(2,1)} async-done(((bf16[16,4096,2,64]{1,3,2,0:T(8,128)(2,1)}), bf16[16,512,2,64]{1,3,2,0:T(8,128)(2,1)}) %reduce-scatter.15.cloned.1.call-update) | async-done | bytes 2097168 | tf_op jit(solution)/shard_map/reduce_scatter | solution.py:383
  2095.2 85.7 %all-to-all-done.3 = bf16[16,512,3,2,64]{1,4,3,2,0:T(8,128)(2,1)} async-done(((bf16[16,512,3,2,64]{1,4,3,2,0:T(8,128)(2,1)}), bf16[16,512,3,2,64]{1,4,3,2,0:T(8,128)(2,1)}, u32[]{:S(2)}, u32[]{:S(2)}) %all-to-all-start.3) | async-done | bytes 6291488 | tf_op jit(solution)/shard_map/all_to_all | solution.py:178
  2421.0 42.5 %reduce-scatter.27.cloned.1.call-done = bf16[64,1536]{1,0:T(8,128)(2,1)} async-done(((bf16[512,1536]{1,0:T(8,128)(2,1)}), bf16[64,1536]{1,0:T(8,128)(2,1)}) %reduce-scatter.27.cloned.1.call-update) | async-done | bytes 196624 | tf_op jit(solution)/shard_map/reduce_scatter | solution.py:475
  2463.6 57.6 %reduce-scatter.23.cloned.1.call-done = bf16[576,512]{1,0:T(8,128)(2,1)} async-done(((bf16[4608,512]{1,0:T(8,128)(2,1)}), bf16[576,512]{1,0:T(8,128)(2,1)}) %reduce-scatter.23.cloned.1.call-update) | async-done | bytes 589840 | tf_op jit(solution)/shard_map/reduce_scatter | solution.py:451
  2521.2 57.2 %reduce-scatter.19.cloned.1.call-done = bf16[576,512]{1,0:T(8,128)(2,1)} async-done(((bf16[4608,512]{1,0:T(8,128)(2,1)}), bf16[576,512]{1,0:T(8,128)(2,1)}) %reduce-scatter.19.cloned.1.call-update) | async-done | bytes 589840 | tf_op jit(solution)/shard_map/reduce_scatter | solution.py:436
  (634 shorter events, 1098.2 us)
Async XLA Ops:
  7.2 870.0 %copy-start = (bf16[2048,512]{1,0:T(8,128)(2,1)S(1)}, bf16[2048,512]{1,0:T(8,128)(2,1)}, u32[]{:S(2)}) copy-start(bf16[2048,512]{1,0:T(8,128)(2,1)} %param.68) | copy-start | bytes 6291460
  7.3 395.2 %all-gather.7.cloned.1.call-start = ((), (), s32[]{:S(2)}) async-start(), calls=%async_computation.33 | async-start | bytes 18874368 | tf_op jit(solution)/shard_map/all_gather | solution.py:299
  8.2 130.3 %copy-start.93 = (f32[4]{0:T(128)}, f32[4]{0:T(128)S(1)}, u32[]{:S(2)}) copy-start(f32[4]{0:T(128)S(1)} %get-tuple-element.298) | copy-start | bytes 52
  9.8 106.1 %copy-start.23 = (f32[4,8,64]{2,1,0:T(8,128)}, f32[4,8,64]{2,1,0:T(8,128)S(1)}, u32[]{:S(2)}) copy-start(f32[4,8,64]{2,1,0:T(8,128)S(1)} %and_convert_fusion.1) | copy-start | bytes 24580
  31.5 3.3 collective-permute-start
  32.8 3.4 collective-permute-start.1
  84.6 2.8 collective-permute-start.2
  85.9 4.5 collective-permute-start.3
  87.2 57.8 %copy-start.85 = (f32[512]{0:T(512)}, f32[512]{0:T(512)S(1)}, u32[]{:S(2)}) copy-start(f32[512]{0:T(512)S(1)} %convert_element_type.455) | copy-start | bytes 6148
  309.3 188.1 %all-gather.5.cloned.1.call-start = ((), (), s32[]{:S(2)}) async-start(), calls=%async_computation.32 | async-start | bytes 18874368 | tf_op jit(solution)/shard_map/all_gather | solution.py:300
  798.7 53.7 %all-to-all-start.1 = ((bf16[16,512,1,2,64]{1,4,3,2,0:T(8,128)(2,1)}), bf16[16,512,1,2,64]{1,4,3,2,0:T(8,128)(2,1)}, u32[]{:S(2)}, u32[]{:S(2)}) async-start(bf16[16,512,1,2,64]{1,4,3,2,0:T(8,128)(2,1)} %bitcast.497), calls=%async_computation.1 | async-start | bytes 4194304 | tf_op jit(solution)/shard_map/all_to_all | solution.py:178
  995.6 52.4 %all-to-all-start.2 = ((bf16[4,512,1,8,64]{1,4,0,2,3:T(8,128)(2,1)}), bf16[4,512,1,8,64]{1,4,0,2,3:T(8,128)(2,1)}, u32[]{:S(2)}, u32[]{:S(2)}) async-start(bf16[4,512,1,8,64]{1,4,0,2,3:T(8,128)(2,1)} %copy.233), calls=%async_computation.2 | async-start | bytes 4194304 | tf_op jit(solution)/shard_map/all_to_all | solution.py:174
  1000.0 911.8 %reduce-scatter.17.cloned.1.call-start = ((), (), s32[]{:S(2)}) async-start(), calls=%async_computation.19 | async-start | bytes 18874368 | tf_op jit(solution)/shard_map/reduce_scatter | solution.py:386
  1797.5 233.6 %reduce-scatter.15.cloned.1.call-start = ((), (), s32[]{:S(2)}) async-start(), calls=%async_computation.18 | async-start | bytes 18874368 | tf_op jit(solution)/shard_map/reduce_scatter | solution.py:383
  2037.3 143.6 %all-to-all-start.3 = ((bf16[16,512,3,2,64]{1,4,3,2,0:T(8,128)(2,1)}), bf16[16,512,3,2,64]{1,4,3,2,0:T(8,128)(2,1)}, u32[]{:S(2)}, u32[]{:S(2)}) async-start(bf16[16,512,3,2,64]{1,4,3,2,0:T(8,128)(2,1)} %pad_maximum_fusion), calls=%async_computation.5 | async-start | bytes 12582912 | tf_op jit(solution)/shard_map/all_to_all | solution.py:178
  2042.6 358.7 %reduce-scatter.41.cloned.1.call-start = ((), (), s32[]{:S(2)}) async-start(), calls=%async_computation.31 | async-start | bytes 589824 | tf_op jit(solution)/shard_map/reduce_scatter | solution.py:511
  2055.1 346.2 %reduce-scatter.29.cloned.1.call-start = ((), (), s32[]{:S(2)}) async-start(), calls=%async_computation.25 | async-start | bytes 589824 | tf_op jit(solution)/shard_map/reduce_scatter | solution.py:478
  2060.1 341.2 %reduce-scatter.39.cloned.1.call-start = ((), (), s32[]{:S(2)}) async-start(), calls=%async_computation.30 | async-start | bytes 2359296 | tf_op jit(solution)/shard_map/reduce_scatter | solution.py:505
  2070.8 330.5 %reduce-scatter.37.cloned.1.call-start = ((), (), s32[]{:S(2)}) async-start(), calls=%async_computation.29 | async-start | bytes 4718592 | tf_op jit(solution)/shard_map/reduce_scatter | solution.py:499
  2089.3 312.0 %reduce-scatter.25.cloned.1.call-start = ((), (), s32[]{:S(2)}) async-start(), calls=%async_computation.23 | async-start | bytes 589824 | tf_op jit(solution)/shard_map/reduce_scatter | solution.py:463
  2210.0 191.4 %reduce-scatter.33.cloned.1.call-start = ((), (), s32[]{:S(2)}) async-start(), calls=%async_computation.27 | async-start | bytes 589824 | tf_op jit(solution)/shard_map/reduce_scatter | solution.py:487
  2218.6 182.8 %reduce-scatter.35.cloned.1.call-start = ((), (), s32[]{:S(2)}) async-start(), calls=%async_computation.28 | async-start | bytes 589824 | tf_op jit(solution)/shard_map/reduce_scatter | solution.py:490
  2239.5 161.9 %reduce-scatter.31.cloned.1.call-start = ((), (), s32[]{:S(2)}) async-start(), calls=%async_computation.26 | async-start | bytes 1179648 | tf_op jit(solution)/shard_map/reduce_scatter | solution.py:484
  2249.4 6.1 collective-permute-start.4
  2251.2 4.2 collective-permute-start.5
  2255.1 165.9 %reduce-scatter.21.cloned.1.call-start = ((), (), s32[]{:S(2)}) async-start(), calls=%async_computation.21 | async-start | bytes 1179648 | tf_op jit(solution)/shard_map/reduce_scatter | solution.py:439
  2323.6 140.0 %reduce-scatter.27.cloned.1.call-start = ((), (), s32[]{:S(2)}) async-start(), calls=%async_computation.24 | async-start | bytes 1769472 | tf_op jit(solution)/shard_map/reduce_scatter | solution.py:475
  2333.0 188.2 %reduce-scatter.23.cloned.1.call-start = ((), (), s32[]{:S(2)}) async-start(), calls=%async_computation.22 | async-start | bytes 5308416 | tf_op jit(solution)/shard_map/reduce_scatter | solution.py:451
  2349.0 229.4 %reduce-scatter.19.cloned.1.call-start = ((), (), s32[]{:S(2)}) async-start(), calls=%async_computation.20 | async-start | bytes 5308416 | tf_op jit(solution)/shard_map/reduce_scatter | solution.py:436
  2365.3 330.0 %all-reduce.34.cloned.1.call-start = ((), (), s32[]{:S(2)}) async-start(), calls=%async_computation.34 | async-start | bytes 5505024 | tf_op jit(solution)/shard_map/psum | solution.py:552
  2368.9 14.7 collective-permute-start.6
  2370.4 13.2 collective-permute-start.7
  (134 other events, 1629.5 us)
Sparse Core Ops, SparseCore 0:
  309.5 92.9 all-gather.6
  404.3 93.1 all-gather.4
  1797.6 114.0 reduce-scatter.16
  1915.2 115.9 reduce-scatter.14
  2055.2 34.4 reduce-scatter.40
  2093.5 34.1 reduce-scatter.28
  2131.0 41.1 reduce-scatter.38
  2176.0 51.3 reduce-scatter.36
  2231.0 34.6 reduce-scatter.24
  2269.0 34.1 reduce-scatter.32
  2306.2 34.1 reduce-scatter.34
  2344.4 37.1 reduce-scatter.30
  2385.7 35.3 reduce-scatter.20
  2425.1 38.4 reduce-scatter.26
  2467.3 53.8 reduce-scatter.22
  2524.5 53.8 reduce-scatter.18
  2582.0 113.2 all-reduce.33
where the time goes:
time: 2730 us; the launch traced here: 2720 us
  matrix products  1020 us (37%)
  waiting for transfers between devices  797 us (29%)
  other arithmetic  479 us (18%)
  blocking collectives  272 us (10%)
  local copies, waits for them, and re-layouts  105 us (4%)
  starting transfers between devices  28 us (1%)
    dot_general x8, matrix products, masked_scores(): jnp.einsum('gqhd,gkhd->ghqk', queries, keys_all, preferred_element_type=j...  293 us
    convert_element_type x8, other arithmetic, rounded(): return field.astype(jnp.bfloat16)  231 us
    all_to_all x1, blocking collectives, to_heads(): lax.all_to_all(field, 'heads', split_axis=3, concat_axis=0, tiled=True)  142 us
    all_to_all x2, waiting for transfers between devices, from_heads(): lax.all_to_all(field, 'heads', split_axis=0, concat_axis=3, tiled=True)  121 us
    reduce_scatter x1, waiting for transfers between devices, per_device(): lax.psum_scatter(ungrouped(grad_keys_all).astype(jnp.bfloat16), 'rows', s...  119 us
    reduce_scatter x1, waiting for transfers between devices, per_device(): lax.psum_scatter(ungrouped(grad_values_all).astype(jnp.bfloat16), 'rows',...  114 us
    dot_general x4, matrix products, attend(): jnp.einsum('ghqk,gkhd->gqhd', prob_low, values_all, preferred_element_typ...  106 us
    dot_general x4, matrix products, attend_back(): jnp.einsum('gqhd,gkhd->ghqk', grad_mixed, values_all, preferred_element_t...  104 us
  transfers between devices with their start and end apart: 28, of which 14 were waited for; matrix products, arithmetic and copies ran while one was open for 10% of the time, Pallas kernels for 0%

commit v1 on v0

v1 whole, which is shorter than its diff:
```python
from functools import partial
import math

import jax
import jax.numpy as jnp
from jax import lax
from jax.experimental import pallas as pl
from jax.experimental.pallas import tpu as pltpu
from jax.sharding import PartitionSpec as P

HEADS = 8
GROUPS = 32


GN_EPS = 1e-06
LN_EPS = 1e-05
HIGH = lax.Precision.HIGHEST


LOG2E = math.log2(math.e)
BF = jnp.bfloat16
F32 = jnp.float32

def dot_nt(lhs, rhs):
    return lax.dot_general(lhs, rhs, (((1,), (1,)), ((), ())), preferred_element_type=F32)


def dot_nn(lhs, rhs):
    return lax.dot_general(lhs, rhs, (((1,), (0,)), ((), ())), preferred_element_type=F32)


def lane_ids(rows):
    return lax.broadcasted_iota(jnp.int32, (rows, 128), 1)


def swap_halves(field):
    return pltpu.roll(field, 64, 1)


def pieces_of(column):
    top = column.astype(BF).astype(F32)
    rest = column - top
    mid = rest.astype(BF).astype(F32)
    return (top, mid, rest - mid)


def extras(column, lanes, first):
    top, mid, low = pieces_of(column)
    return jnp.where(
        lanes == first, top, jnp.where(lanes == first + 1, mid, jnp.where(lanes == first + 2, low, 0.0))
    )


def block_of(count, pref):
    for size in pref:
        if count % size == 0:
            return size
    return count


def crop(field, width, side):
    rows = field.shape[0] // width
    if side == width:
        return field
    return field.reshape(rows, width, 128)[:, :side].reshape(rows * side, 128)


def uncrop(field, width, side):
    if side == width:
        return field
    rows = field.shape[0] // side
    spread = field.reshape(rows, side, 128)
    return jnp.concatenate(
        [spread, jnp.zeros((rows, width - side, 128), field.dtype)], axis=1
    ).reshape(rows * width, 128)


def unpack_pairs(pairs):
    return jnp.concatenate([pairs, swap_halves(pairs)], axis=0)


def pack_pairs(field, lanes):
    half = field.shape[0] // 2
    return jnp.where(lanes[:half] < 64, field[:half], swap_halves(field[half:]))


def attend_kernel(width, scale, side_ref, qkv_ref, out_ref, norm_ref, q_s, k_s, v_s, vt_s, top_s, safe_s):
    bands, packed, _ = qkv_ref.shape
    band_tokens = packed * 2 // 3
    band_rows = band_tokens // width
    side_now = side_ref[0]

    def variant(side):
        tokens = side * side
        used = side // band_rows
        own = band_rows * side
        lanes = lane_ids(own)
        low = lanes < 64
        row_ids = lax.broadcasted_iota(jnp.int32, (128, 128), 0)
        col_ids = lax.broadcasted_iota(jnp.int32, (128, 128), 1)
        picks = jnp.where((row_ids < 64) == (col_ids < 64), 1.0, 0.0).astype(BF)

        def gather_band(band, norms):
            pairs = crop(qkv_ref[band, band_tokens:, :].astype(F32), width, side)
            keys = crop(qkv_ref[band, :band_tokens, :].astype(F32), width, side)
            queries = unpack_pairs(pairs) * (scale * LOG2E)
            head = queries.astype(BF).astype(F32)
            turned = swap_halves(keys)
            rows = pl.ds(pl.multiple_of(band * own, 16), own)
            q_s[rows, :] = jnp.where(low, head, swap_halves(queries - head)).astype(BF)
            k_s[rows, :] = jnp.where(low, keys, turned).astype(BF)
            v_s[rows, :] = jnp.where(low, turned, jnp.where(lanes == 64, 1.0, 0.0)).astype(BF)
            joint = jnp.where(low, queries, turned)
            sums = dot_nn((joint * joint).astype(BF), picks)
            return jnp.maximum(norms, jnp.max(sums, axis=0, keepdims=True))

        norms = lax.fori_loop(0, used, gather_band, jnp.zeros((1, 128), F32))
        step = block_of(tokens, (512, 256))
        for first in range(0, tokens, step):
            vt_s[:, first : first + step] = v_s[first : first + step, :].T
        first_lanes = lane_ids(1) < 64
        query_top = jnp.max(jnp.where(first_lanes, norms, 0.0))
        key_top = jnp.max(jnp.where(first_lanes, 0.0, norms))
        safe = query_top * key_top * 1.05 <= 100.0 * 100.0
        bq = block_of(tokens, (512, 768, 256))
        bk = block_of(tokens, (512, 768, 256))

        @pl.when(safe)
        def _():
            top_s[...] = jnp.zeros_like(top_s)

        @pl.when(jnp.logical_not(safe))
        def _():
            def tops(qi, _):
                cols = pl.ds(pl.multiple_of(qi * bq, 256), bq)
                queries = q_s[cols, :]

                def more(ki, top):
                    scores = dot_nt(k_s[pl.ds(pl.multiple_of(ki * bk, 256), bk), :], queries)
                    return jnp.maximum(top, jnp.max(scores, axis=0, keepdims=True))

                top = lax.fori_loop(0, tokens // bk, more, jnp.full((1, bq), -jnp.inf, F32))
                top_s[:, cols] = jnp.broadcast_to(top, (8, bq))
                return 0

            lax.fori_loop(0, tokens // bq, tops, 0)

        def main(qi, _):
            cols = pl.ds(pl.multiple_of(qi * bq, 256), bq)
            queries = q_s[cols, :]
            top = top_s[0:1, cols]
            total = jnp.zeros((80, bq), F32)
            for first in range(0, tokens, bk):
                scores = dot_nt(k_s[first : first + bk, :], queries)
                weights = jnp.exp2(scores - top).astype(BF)
                total = total + dot_nn(vt_s[0:80, first : first + bk], weights)
            row_total = total[64:65]
            mixed = total[:64] / row_total
            log_total = jnp.broadcast_to(top + jnp.log2(row_total), (64, bq))
            norm_ref[cols, :] = jnp.concatenate([mixed, log_total], axis=0).T
            return 0

        lax.fori_loop(0, tokens // bq, main, 0)

        def spread_band(band, _):
            rows = pl.ds(pl.multiple_of(band * own, 16), own)
            pairs = pack_pairs(norm_ref[rows, :], lanes)
            out_ref[band] = uncrop(pairs, width, side).astype(BF)
            return 0

        lax.fori_loop(0, used, spread_band, 0)
        if used < bands:
            out_ref[used:] = jnp.zeros((bands - used,) + out_ref.shape[1:], BF)

    for side in (width, width * 3 // 4, width // 2):
        pl.when(side_now == side)(partial(variant, side))


def attend(side, qkv, width, scale):
    bands, packed, _ = qkv.shape
    tokens = bands * packed * 2 // 3
    vm = pl.BlockSpec(memory_space=pltpu.VMEM)
    return pl.pallas_call(
        partial(attend_kernel, width, scale),
        out_shape=(
            jax.ShapeDtypeStruct((bands, packed // 3, 128), BF),
            jax.ShapeDtypeStruct((tokens, 128), F32),
        ),
        in_specs=[pl.BlockSpec(memory_space=pltpu.SMEM), vm],
        out_specs=(vm, vm),
        scratch_shapes=[
            pltpu.VMEM((tokens, 128), BF),
            pltpu.VMEM((tokens, 128), BF),
            pltpu.VMEM((tokens, 128), BF),
            pltpu.VMEM((128, tokens), BF),
            pltpu.VMEM((8, tokens), F32),
            pltpu.SMEM((1,), jnp.int32),
        ],
        compiler_params=pltpu.CompilerParams(vmem_limit_bytes=48 << 20),
        cost_estimate=pl.CostEstimate(
            flops=4 * 256 * tokens * tokens, bytes_accessed=8 << 20, transcendentals=tokens * tokens
        ),
        name="attend",
    )(side, qkv)


def attend_back_kernel(width, scale, side_ref, qkv_ref, grad_ref, norm_ref, out_ref,
                       q_s, k_s, kn_s, g_s, v_s, qt_s, gt_s, dq_s, dkv_s):
    bands, packed, _ = qkv_ref.shape
    band_tokens = packed * 2 // 3
    band_rows = band_tokens // width
    side_now = side_ref[0]

    def variant(side):
        tokens = side * side
        used = side // band_rows
        own = band_rows * side
        lanes = lane_ids(own)
        low = lanes < 64
        ones_high = jnp.where((lanes >= 64) & (lanes < 67), 1.0, 0.0)
        ones_low = jnp.where(lanes < 3, 1.0, 0.0).astype(BF)

        def gather_band(band, _):
            queries = unpack_pairs(crop(qkv_ref[band, band_tokens:, :].astype(F32), width, side))
            keys = crop(qkv_ref[band, :band_tokens, :].astype(F32), width, side)
            grads = unpack_pairs(crop(grad_ref[band].astype(F32), width, side))
            rows = pl.ds(pl.multiple_of(band * own, 16), own)
            mixed = norm_ref[rows, :]
            delta = jnp.sum(jnp.where(low, grads * mixed, 0.0), axis=1, keepdims=True)
            log_total = mixed[:, 64:65]
            scaled = queries * (scale * LOG2E)
            head = scaled.astype(BF).astype(F32)
            turned = swap_halves(keys)
            q_s[rows, :128] = jnp.where(low, head, swap_halves(scaled - head)).astype(BF)
            q_s[rows, 128:] = extras(-log_total, lanes, 0).astype(BF)
            k_s[rows, :128] = jnp.where(low, keys, turned).astype(BF)
            k_s[rows, 128:] = ones_low
            kn_s[rows, :] = jnp.where(low, keys, 0.0).astype(BF)
            g_s[rows, :] = jnp.where(low, grads, extras(-delta, lanes, 64)).astype(BF)
            v_s[rows, :] = jnp.where(low, turned, ones_high).astype(BF)
            dq_s[rows, :] = jnp.where(low, queries, swap_halves(grads))
            return 0

        lax.fori_loop(0, used, gather_band, 0)
        step = block_of(tokens, (512, 256))
        for first in range(0, tokens, step):
            turned = dq_s[first : first + step, :].T.astype(BF)
            qt_s[:, first : first + step] = turned[:64]
            gt_s[:, first : first + step] = turned[64:]
        dkv_s[...] = jnp.zeros_like(dkv_s)
        bq = block_of(tokens, (512, 768, 256))
        bk = block_of(tokens, (512, 768, 256))

        def main(qi, _):
            rows = pl.ds(pl.multiple_of(qi * bq, 256), bq)
            queries = q_s[rows, :]
            grads = g_s[rows, :]
            grads_t = gt_s[:, rows]
            queries_t = qt_s[:, rows]
            total = jnp.zeros((bq, 128), F32)
            for first in range(0, tokens, bk):
                probs = jnp.exp2(dot_nt(queries, k_s[first : first + bk, :]))
                slopes = dot_nt(grads, v_s[first : first + bk, :])
                grad_scores = (probs * slopes).astype(BF)
                dkv_s[64:, first : first + bk] += dot_nn(grads_t, probs.astype(BF))
                dkv_s[:64, first : first + bk] += dot_nn(queries_t, grad_scores)
                total = total + dot_nn(grad_scores, kn_s[first : first + bk, :])
            dq_s[rows, :] = total
            return 0

        lax.fori_loop(0, tokens // bq, main, 0)
        for first in range(0, tokens, step):
            turned = dkv_s[:, first : first + step].T
            k_s[first : first + step, :128] = jnp.where(
                lane_ids(step) < 64, turned * scale, turned
            ).astype(BF)

        def spread_band(band, _):
            rows = pl.ds(pl.multiple_of(band * own, 16), own)
            out_ref[band, :band_tokens] = uncrop(k_s[rows, :128], width, side)
            pairs = pack_pairs(dq_s[rows, :] * scale, lanes)
            out_ref[band, band_tokens:] = uncrop(pairs, width, side).astype(BF)
            return 0

        lax.fori_loop(0, used, spread_band, 0)
        if used < bands:
            out_ref[used:] = jnp.zeros((bands - used,) + out_ref.shape[1:], BF)

    for side in (width, width * 3 // 4, width // 2):
        pl.when(side_now == side)(partial(variant, side))


def attend_back(side, qkv, grads, norms, width, scale):
    bands, packed, _ = qkv.shape
    tokens = bands * packed * 2 // 3
    vm = pl.BlockSpec(memory_space=pltpu.VMEM)
    return pl.pallas_call(
        partial(attend_back_kernel, width, scale),
        out_shape=jax.ShapeDtypeStruct((bands, packed, 128), BF),
        in_specs=[pl.BlockSpec(memory_space=pltpu.SMEM), vm, vm, vm],
        out_specs=vm,
        scratch_shapes=[
            pltpu.VMEM((tokens, 256), BF),
            pltpu.VMEM((tokens, 256), BF),
            pltpu.VMEM((tokens, 128), BF),
            pltpu.VMEM((tokens, 128), BF),
            pltpu.VMEM((tokens, 128), BF),
            pltpu.VMEM((64, tokens), BF),
            pltpu.VMEM((64, tokens), BF),
            pltpu.VMEM((tokens, 128), F32),
            pltpu.VMEM((128, tokens), F32),
        ],
        compiler_params=pltpu.CompilerParams(vmem_limit_bytes=56 << 20),
        cost_estimate=pl.CostEstimate(
            flops=10 * 256 * tokens * tokens, bytes_accessed=10 << 20, transcendentals=tokens * tokens
        ),
        name="attend_back",
    )(side, qkv, grads, norms)


def extended(block, sides, width):
    for axis, dim in sides:
        count = lax.axis_size(axis)
        forward = [(i, i + 1) for i in range(count - 1)]
        backward = [(target, source) for source, target in forward]
        low = lax.ppermute(
            lax.slice_in_dim(block, block.shape[dim] - width, None, axis=dim), axis, forward
        )
        high = lax.ppermute(lax.slice_in_dim(block, 0, width, axis=dim), axis, backward)
        block = jnp.concatenate([low, block, high], axis=dim)
    return block


def rounded(field):
    return field.astype(jnp.bfloat16)


def pixel_mask(sides, row_first, row_count, row_width):
    row_ids = row_first + jnp.arange(row_count, dtype=jnp.int32)
    col_ids = jnp.arange(row_width, dtype=jnp.int32)
    limit = sides[:, None, None]
    within = (row_ids[None, :, None] < limit) & (col_ids[None, None, :] < limit)
    return within.astype(jnp.float32)[..., None]


def group_sums(first_term, second_term):
    shaped = (
        first_term.shape[0],
        first_term.shape[1] * first_term.shape[2],
        GROUPS,
        first_term.shape[3] // GROUPS,
    )
    return lax.psum(
        (
            jnp.sum(first_term.reshape(shaped), axis=(1, 3)),
            jnp.sum(second_term.reshape(shaped), axis=(1, 3)),
        ),
        "rows",
    )


def spread_groups(stat, channels):
    return jnp.repeat(stat, channels // GROUPS, axis=1)[:, None, None, :]


def norm_forward(field, inside, pixel_count, norm_gain, norm_bias):
    channels = field.shape[-1]
    masked = field * inside
    row_total, square = group_sums(masked, masked * field)
    group_mean = row_total / pixel_count
    inv_std = spread_groups(
        lax.rsqrt(square / pixel_count - group_mean * group_mean + GN_EPS), channels
    )
    normed = (field - spread_groups(group_mean, channels)) * inv_std
    return (normed * norm_gain + norm_bias, normed, inv_std)


def norm_backward(grad_norm, normed, inv_std, inside, pixel_count, norm_gain):
    channels = normed.shape[-1]
    grad_norm = grad_norm * inside
    scaled = grad_norm * norm_gain
    row_total, crossed = group_sums(scaled, scaled * normed)
    grad_field = (
        inside
        * inv_std
        * (
            scaled
            - spread_groups(row_total / pixel_count, channels)
            - normed * spread_groups(crossed / pixel_count, channels)
        )
    )
    return (
        grad_field,
        jnp.sum(grad_norm * normed, axis=(0, 1, 2)),
        jnp.sum(grad_norm, axis=(0, 1, 2)),
    )


def layer_norm(field, norm_gain, norm_bias):
    centre = jnp.mean(field, axis=-1, keepdims=True)
    centred = field - centre
    spread = jnp.mean(centred * centred, axis=-1, keepdims=True)
    return centred * lax.rsqrt(spread + LN_EPS) * norm_gain + norm_bias


def geglu_act(gate_pair):
    half_dim = gate_pair.shape[-1] // 2
    return gate_pair[..., :half_dim] * jax.nn.gelu(gate_pair[..., half_dim:], approximate=False)


def conv_taps(field, flipped):
    padded = extended(field, (("rows", 1),), 1)
    padded = jnp.pad(padded, ((0, 0), (0, 0), (1, 1), (0, 0)))
    band_rows, row_width = (field.shape[1], field.shape[2])
    offsets = [
        (2 - row_off, 2 - col_off) if flipped else (row_off, col_off)
        for row_off in range(3)
        for col_off in range(3)
    ]
    return jnp.stack(
        [
            padded[:, top_row : top_row + band_rows, left_col : left_col + row_width, :]
            for top_row, left_col in offsets
        ],
        axis=3,
    )


def conv_apply(tap_stack, weight):
    channels = tap_stack.shape[-1]
    return jnp.einsum(
        "brwtc,tco->brwo",
        tap_stack,
        weight.reshape(9, channels, -1),
        preferred_element_type=jnp.float32,
    )


def conv_weight_grad(tap_stack, grads_low):
    channels = tap_stack.shape[-1]
    return jnp.einsum(
        "brwtc,brwo->tco", tap_stack, grads_low, preferred_element_type=jnp.float32
    ).reshape(9 * channels, -1)


def conv_back(grads_low, weight):
    channels = grads_low.shape[-1]
    return jnp.einsum(
        "brwtc,tic->brwi",
        conv_taps(grads_low, True),
        weight.reshape(9, channels, channels),
        preferred_element_type=jnp.float32,
    )


def tokens_dot(inputs_low, weight):
    return jnp.einsum("blc,co->blo", inputs_low, weight, preferred_element_type=jnp.float32)


def weight_grad(inputs_low, grads_low):
    return jnp.einsum("blc,blo->co", inputs_low, grads_low, preferred_element_type=jnp.float32)


def back_dot(grads_low, weight):
    return jnp.einsum("blo,co->blc", grads_low, weight, preferred_element_type=jnp.float32)


def time_features(time_steps, dims):
    half_dim = dims // 2
    frequency = jnp.exp(-math.log(10000.0) * jnp.arange(half_dim, dtype=jnp.float32) / half_dim)
    angles = time_steps.astype(jnp.float32)[:, None] * frequency[None, :]
    return jnp.concatenate([jnp.cos(angles), jnp.sin(angles)], axis=-1)


def pack_tokens(field):
    turned = jnp.transpose(field, (2, 0, 1, 3))
    half = turned.shape[2] // 2
    return jnp.concatenate([turned[:, :, :half], turned[:, :, half:]], axis=-1)


def pack_rows(queries, keys, values):
    joint = jnp.transpose(jnp.concatenate([keys, values], axis=-1), (2, 0, 1, 3))
    return jnp.concatenate([joint, pack_tokens(queries)], axis=2)


def unpack_tokens(pairs):
    heads, images, half, _ = pairs.shape
    joint = jnp.concatenate([pairs[..., :64], pairs[..., 64:]], axis=2)
    return jnp.transpose(joint, (1, 2, 0, 3)).reshape(images, 2 * half, heads * 64)


def to_items(sent, bands):
    heads, images, packed, lanes = sent.shape
    per_band = heads * images // bands
    items = sent.reshape(bands, per_band, packed, lanes)
    chunks = [
        lax.all_to_all(items[:, at], "rows", split_axis=0, concat_axis=0, tiled=True)
        for at in range(per_band)
    ]
    return chunks, lax.axis_index("rows") * per_band


def from_items(results, images):
    bands = results[0].shape[0]
    back = [
        lax.all_to_all(result, "rows", split_axis=0, concat_axis=0, tiled=True)
        for result in results
    ]
    joint = jnp.stack(back, axis=1)
    return joint.reshape((HEADS, images) + joint.shape[2:])


def per_device(
    images,
    image_sides,
    labels,
    timesteps,
    cotangent,
    first_gain,
    first_bias,
    conv_one,
    time_proj,
    time_bias,
    second_gain,
    second_bias,
    conv_two,
    conv_bias,
    third_gain,
    third_bias,
    proj_in,
    proj_in_bias,
    attn_gain,
    attn_bias,
    qkv_proj,
    attn_out,
    attn_out_bias,
    class_table,
    cross_value,
    cross_out,
    feed_gain,
    feed_bias,
    geglu_proj,
    geglu_bias,
    feed_out,
    feed_out_bias,
    proj_out,
    proj_out_bias,
):
    image_count, band_rows, row_width, channels = images.shape
    tokens = band_rows * row_width
    head_dim = channels // HEADS
    score_scale = head_dim ** (-0.5)
    first_image = lax.axis_index("heads") * image_count
    first_row = lax.axis_index("rows") * band_rows
    own_sides = lax.dynamic_slice_in_dim(image_sides, first_image, image_count)
    own_labels = lax.dynamic_slice_in_dim(labels, first_image, image_count)
    own_steps = lax.dynamic_slice_in_dim(timesteps, first_image, image_count)
    inside = pixel_mask(own_sides, first_row, band_rows, row_width)
    pixel_count = (own_sides * own_sides * (channels // GROUPS)).astype(jnp.float32)[:, None]
    start = images.astype(jnp.float32) * inside
    norm_one, normed_one, std_one = norm_forward(start, inside, pixel_count, first_gain, first_bias)
    act_one = rounded(jax.nn.silu(norm_one) * inside)
    taps_one = conv_taps(act_one, False)
    time_embed = rounded(jax.nn.silu(time_features(own_steps, time_proj.shape[0])))
    time_shift = jnp.dot(time_embed, time_proj, preferred_element_type=jnp.float32)
    hidden_one = conv_apply(taps_one, conv_one) + time_shift[:, None, None, :] + time_bias
    norm_two, normed_two, std_two = norm_forward(
        hidden_one, inside, pixel_count, second_gain, second_bias
    )
    act_two = rounded(jax.nn.silu(norm_two) * inside)
    taps_two = conv_taps(act_two, False)
    residual = start + conv_apply(taps_two, conv_two) + conv_bias
    norm_three, normed_three, std_three = norm_forward(
        residual, inside, pixel_count, third_gain, third_bias
    )
    flat_in = rounded(norm_three.reshape(image_count, tokens, channels))
    stream = tokens_dot(flat_in, proj_in) + proj_in_bias
    attn_in = rounded(layer_norm(stream, attn_gain, attn_bias))
    bands = lax.axis_size("rows")
    qkv_rows = rounded(tokens_dot(attn_in, qkv_proj)).reshape(
        image_count, tokens, 3, HEADS, head_dim
    )
    sent = pack_rows(qkv_rows[:, :, 0], qkv_rows[:, :, 1], qkv_rows[:, :, 2])
    chunks, first_item = to_items(sent, bands)
    item_sides = [
        lax.dynamic_slice_in_dim(own_sides, lax.rem(first_item + at, image_count), 1)
        for at in range(len(chunks))
    ]
    attended = [
        attend(side, chunk, row_width, score_scale) for side, chunk in zip(item_sides, chunks)
    ]
    mixed_out = from_items([pairs for pairs, _ in attended], image_count)
    mixed_out = unpack_tokens(mixed_out)
    stream_two = stream + tokens_dot(mixed_out, attn_out) + attn_out_bias
    one_hot = rounded(
        (own_labels[:, None] == jnp.arange(class_table.shape[0], dtype=jnp.int32)[None, :]).astype(
            jnp.float32
        )
    )
    context = jnp.dot(one_hot, class_table, preferred_element_type=jnp.float32)
    value_vec = jnp.dot(rounded(context), cross_value, preferred_element_type=jnp.float32)
    value_low = rounded(value_vec)
    cross_term = jnp.dot(value_low, cross_out, preferred_element_type=jnp.float32)
    stream_three = stream_two + cross_term[:, None, :]
    feed_in = rounded(layer_norm(stream_three, feed_gain, feed_bias))
    gate_pair = tokens_dot(feed_in, geglu_proj) + geglu_bias
    gated_hidden = rounded(geglu_act(gate_pair))
    stream_four = stream_three + tokens_dot(gated_hidden, feed_out) + feed_out_bias
    last_in = rounded(stream_four)
    branch = tokens_dot(last_in, proj_out) + proj_out_bias
    output = (residual + branch.reshape(images.shape)) * inside
    grad_out = cotangent.astype(jnp.float32) * inside
    grad_branch = grad_out.reshape(image_count, tokens, channels)
    grad_proj_out_bias = jnp.sum(grad_branch, axis=(0, 1))
    low_branch = rounded(grad_branch)
    grad_proj_out = weight_grad(last_in, low_branch)
    grad_four = back_dot(low_branch, proj_out)
    grad_feed_out_bias = jnp.sum(grad_four, axis=(0, 1))
    low_feed = rounded(grad_four)
    grad_feed_out = weight_grad(gated_hidden, low_feed)
    grad_gated = back_dot(low_feed, feed_out)
    geglu_value, geglu_pull = jax.vjp(geglu_act, gate_pair)
    grad_pair = geglu_pull(grad_gated)[0]
    grad_geglu_bias = jnp.sum(grad_pair, axis=(0, 1))
    low_pair = rounded(grad_pair)
    grad_geglu_proj = weight_grad(feed_in, low_pair)
    feed_value, feed_pull = jax.vjp(
        layer_norm, stream_three, feed_gain.astype(jnp.float32), feed_bias.astype(jnp.float32)
    )
    norm_part, grad_feed_gain, grad_feed_bias = feed_pull(back_dot(low_pair, geglu_proj))
    grad_three = grad_four + norm_part
    grad_cross = jnp.sum(grad_three, axis=1)
    grad_attn_out_bias = jnp.sum(grad_three, axis=(0, 1))
    low_attn = rounded(grad_three)
    grad_attn_out = weight_grad(mixed_out, low_attn)
    grad_mixed = rounded(back_dot(low_attn, attn_out)).reshape(
        image_count, tokens, HEADS, head_dim
    )
    grad_chunks, _ = to_items(pack_tokens(grad_mixed), bands)
    grad_qkv = from_items(
        [
            attend_back(side, chunk, grad_chunk, norms, row_width, score_scale)
            for side, chunk, grad_chunk, (_, norms) in zip(
                item_sides, chunks, grad_chunks, attended
            )
        ],
        image_count,
    )
    grad_queries = unpack_tokens(grad_qkv[:, :, tokens:])
    grad_keys = jnp.transpose(grad_qkv[:, :, :tokens, :64], (1, 2, 0, 3)).reshape(
        image_count, tokens, channels
    )
    grad_values = jnp.transpose(grad_qkv[:, :, :tokens, 64:], (1, 2, 0, 3)).reshape(
        image_count, tokens, channels
    )
    grad_qkv = jnp.concatenate([grad_queries, grad_keys, grad_values], axis=-1)
    grad_qkv_proj = weight_grad(attn_in, grad_qkv)
    attn_value, attn_pull = jax.vjp(
        layer_norm, stream, attn_gain.astype(jnp.float32), attn_bias.astype(jnp.float32)
    )
    norm_part, grad_attn_gain, grad_attn_bias = attn_pull(back_dot(grad_qkv, qkv_proj))
    grad_stream = grad_three + norm_part
    grad_proj_in_bias = jnp.sum(grad_stream, axis=(0, 1))
    low_in = rounded(grad_stream)
    grad_proj_in = weight_grad(flat_in, low_in)
    grad_norm_three = back_dot(low_in, proj_in).reshape(images.shape)
    resid_part, grad_third_gain, grad_third_bias = norm_backward(
        grad_norm_three, normed_three, std_three, inside, pixel_count, third_gain
    )
    grad_residual = grad_out + resid_part
    grad_conv_bias = jnp.sum(grad_residual, axis=(0, 1, 2))
    low_two = rounded(grad_residual)
    grad_conv_two = conv_weight_grad(taps_two, low_two)
    grad_act_two = conv_back(low_two, conv_two)
    silu_two, silu_pull_two = jax.vjp(jax.nn.silu, norm_two)
    grad_norm_two = silu_pull_two(grad_act_two * inside)[0]
    grad_hidden, grad_second_gain, grad_second_bias = norm_backward(
        grad_norm_two, normed_two, std_two, inside, pixel_count, second_gain
    )
    grad_shift = jnp.sum(grad_hidden, axis=(1, 2))
    low_one = rounded(grad_hidden)
    grad_conv_one = conv_weight_grad(taps_one, low_one)
    grad_act_one = conv_back(low_one, conv_one)
    silu_one, silu_pull_one = jax.vjp(jax.nn.silu, norm_one)
    grad_norm_one = silu_pull_one(grad_act_one * inside)[0]
    start_part, grad_first_gain, grad_first_bias = norm_backward(
        grad_norm_one, normed_one, std_one, inside, pixel_count, first_gain
    )
    grad_images = (grad_residual + start_part) * inside
    me = lax.axis_index("rows")

    def own(field, axis=0):
        size = field.shape[axis] // bands
        return lax.dynamic_slice_in_dim(field, me * size, size, axis)

    per_image = lax.psum(jnp.stack([grad_cross, grad_shift]), "rows")
    per_image = lax.all_gather(per_image, "heads", axis=1, tiled=True)
    all_cross, all_shift = per_image[0], per_image[1]
    all_hot = rounded(
        (labels[:, None] == jnp.arange(class_table.shape[0], dtype=jnp.int32)[None, :]).astype(
            jnp.float32
        )
    )
    all_context = jnp.dot(all_hot, class_table, preferred_element_type=jnp.float32)
    all_value = rounded(
        jnp.dot(rounded(all_context), cross_value, preferred_element_type=jnp.float32)
    ).astype(jnp.float32)
    all_embed = rounded(jax.nn.silu(time_features(timesteps, time_proj.shape[0])))
    grad_cross_out = jnp.dot(own(all_value, 1).T, all_cross, precision=HIGH)
    grad_value = jnp.dot(all_cross, cross_out.astype(jnp.float32).T, precision=HIGH)
    grad_cross_value = jnp.dot(own(all_context, 1).T, grad_value, precision=HIGH)
    grad_context = jnp.dot(grad_value, own(cross_value).astype(jnp.float32).T, precision=HIGH)
    grad_class_table = jnp.dot(all_hot.astype(jnp.float32).T, grad_context, precision=HIGH)
    grad_time_proj = jnp.dot(
        own(all_embed.astype(jnp.float32), 1).T, all_shift, precision=HIGH
    )
    vectors = [
        grad_first_gain,
        grad_first_bias,
        grad_second_gain,
        grad_second_bias,
        grad_conv_bias,
        grad_third_gain,
        grad_third_bias,
        grad_proj_in_bias,
        grad_attn_gain,
        grad_attn_bias,
        grad_attn_out_bias,
        grad_feed_gain,
        grad_feed_bias,
        grad_feed_out_bias,
        grad_proj_out_bias,
    ]
    joint = lax.psum(
        jnp.concatenate([v.reshape(-1, channels) for v in vectors + [grad_geglu_bias]]),
        ("rows", "heads"),
    )
    (
        grad_first_gain,
        grad_first_bias,
        grad_second_gain,
        grad_second_bias,
        grad_conv_bias,
        grad_third_gain,
        grad_third_bias,
        grad_proj_in_bias,
        grad_attn_gain,
        grad_attn_bias,
        grad_attn_out_bias,
        grad_feed_gain,
        grad_feed_bias,
        grad_feed_out_bias,
        grad_proj_out_bias,
    ) = [own(joint[at]) for at in range(len(vectors))]
    grad_geglu_bias = own(joint[len(vectors) :].reshape(-1))

    def reduced(field):
        part = lax.psum_scatter(rounded(field), "rows", scatter_dimension=0, tiled=True)
        return lax.psum(part, "heads").astype(jnp.float32)

    return (
        rounded(output),
        grad_images,
        grad_first_gain,
        grad_first_bias,
        reduced(grad_conv_one),
        grad_time_proj,
        own(jnp.sum(all_shift, axis=0)),
        grad_second_gain,
        grad_second_bias,
        reduced(grad_conv_two),
        grad_conv_bias,
        grad_third_gain,
        grad_third_bias,
        reduced(grad_proj_in),
        grad_proj_in_bias,
        grad_attn_gain,
        grad_attn_bias,
        reduced(grad_qkv_proj),
        reduced(grad_attn_out),
        grad_attn_out_bias,
        grad_class_table,
        grad_cross_value,
        grad_cross_out,
        grad_feed_gain,
        grad_feed_bias,
        reduced(grad_geglu_proj),
        grad_geglu_bias,
        reduced(grad_feed_out),
        grad_feed_out_bias,
        reduced(grad_proj_out),
        grad_proj_out_bias,
    )


def solution(mesh):
    return jax.shard_map(
        per_device,
        mesh=mesh,
        in_specs=(
            P("heads", "rows", None, None),
            P(),
            P(),
            P(),
            P("heads", "rows", None, None),
            P(),
            P(),
            P(),
            P(),
            P(),
            P(),
            P(),
            P(),
            P(),
            P(),
            P(),
            P(),
            P(),
            P(),
            P(),
            P(),
            P(),
            P(),
            P(),
            P(),
            P(),
            P(),
            P(),
            P(),
            P(),
            P(),
            P(),
            P(),
            P(),
        ),
        out_specs=(
            P("heads", "rows", None, None),
            P("heads", "rows", None, None),
            P("rows"),
            P("rows"),
            P("rows", None),
            P("rows", None),
            P("rows"),
            P("rows"),
            P("rows"),
            P("rows", None),
            P("rows"),
            P("rows"),
            P("rows"),
            P("rows", None),
            P("rows"),
            P("rows"),
            P("rows"),
            P("rows", None),
            P("rows", None),
            P("rows"),
            P(None, "rows"),
            P("rows", None),
            P("rows", None),
            P("rows"),
            P("rows"),
            P("rows", None),
            P("rows"),
            P("rows", None),
            P("rows"),
            P("rows", None),
            P("rows"),
        ),
        check_vma=False,
    )
```

time: 2730 us -> 1310 us (0.48)
  matrix products: 1020 us -> 281 us
  waiting for transfers between devices: 797 us -> 150 us
  other arithmetic: 479 us -> 173 us
  Pallas kernels: 0 us -> 166 us
  local copies, waits for them, and re-layouts: 105 us -> 181 us
  starting transfers between devices: 28 us -> 64.8 us
    dot_general x35 -> x8, matrix products: 754 us -> 9.09 us  [the longest x1 1.83 us: per_device(): jnp.dot(rounded(all_context), cross_value, preferred_element_type=jnp.flo...]
    reduce_scatter x14 -> x8, waiting for transfers between devices: 410 us -> 0.08 us  [reduced(): lax.psum_scatter(rounded(field), 'rows', scatter_dimension=0, tiled=True)]
    convert_element_type x8 -> x5, other arithmetic: 231 us -> 21.9 us  [rounded(): return field.astype(jnp.bfloat16)]
    all_gather x2 -> x0, waiting for transfers between devices: 187 us -> none  [the longest x1 95 us: per_device(): lax.all_gather(values_own, 'rows', axis=1, tiled=True)]
    pallas_call x0 -> x8, Pallas kernels: none -> 166 us  [the longest x4 113 us: attend_back(): pl.pallas_call(partial(attend_back_kernel, width, scale), out_shape=jax.S...]
    all_to_all x3 -> x13, waiting for transfers between devices: 169 us -> 58.6 us  [the longest x5 41.6 us: to_items(): lax.all_to_all(items[:, at], 'rows', split_axis=0, concat_axis=0, tiled=T...]
    reduce_sum x5 -> x0, other arithmetic: 91.3 us -> none  [the longest x4 85.8 us: attend(): row_total = jnp.sum(raw_weights, axis=-1, keepdims=True)]
    psum x1, blocking collectives: 12.8 us -> 96 us  [per_device(): lax.psum(jnp.concatenate([v.reshape(-1, channels) for v in vectors + [gra...]
  transfers between devices with their start and end apart: 28 -> 30, of which waited for: 14 -> 10; matrix products, arithmetic and copies ran while one was open for 10% -> 23% of each run, Pallas kernels for 0% -> 13%
where the time goes in v1:
time: 1310 us
  matrix products  281 us (21%)
  blocking collectives  276 us (21%)
  local copies, waits for them, and re-layouts  181 us (14%)
  other arithmetic  173 us (13%)
  Pallas kernels  166 us (13%)
  waiting for transfers between devices  150 us (11%)
  starting transfers between devices  64.8 us (5%)
  between operations  16.6 us (1%)
    pallas_call x4, Pallas kernels, attend_back(): pl.pallas_call(partial(attend_back_kernel, width, scale), out_shape=jax.S...  113 us
    psum x6, blocking collectives, group_sums(): lax.psum((jnp.sum(first_term.reshape(shaped), axis=(1, 3)), jnp.sum(secon...  103 us
    psum x1, blocking collectives, per_device(): lax.psum(jnp.concatenate([v.reshape(-1, channels) for v in vectors + [gra...  96 us
    dot_general x6, matrix products, back_dot(): jnp.einsum('blo,co->blc', grads_low, weight, preferred_element_type=jnp.f...  88 us
    psum x1, waiting for transfers between devices, reduced(): return lax.psum(part, 'heads').astype(jnp.float32)  87.4 us
    unnamed x337, local copies, waits for them, and re-layouts  79.2 us
    all_to_all x3, blocking collectives, to_items(): lax.all_to_all(items[:, at], 'rows', split_axis=0, concat_axis=0, tiled=T...  63.6 us
    pallas_call x4, Pallas kernels, attend(): pl.pallas_call(partial(attend_kernel, width, scale), out_shape=(jax.Shape...  53.3 us
  transfers between devices with their start and end apart: 30, of which 10 were waited for; matrix products, arithmetic and copies ran while one was open for 23% of the time, Pallas kernels for 13%

profile of v1, /device:TPU:0, one launch (start us, length us, event | category | flops | bytes accessed | tf_op | source)
XLA Modules:
  0.0 1308.2 jit_solution(10918033901215020539)
XLA Ops:
  11.3 15.1 %all-reduce.11 = (f32[4,32]{1,0:T(4,128)S(1)}, f32[4,32]{1,0:T(4,128)S(1)}) all-reduce(f32[4,32]{1,0:T(4,128)S(1)} %reduce_sum.488, f32[4,32]{1,0:T(4,128)S(1)} %reduce_sum.485), channel_id=1, replica_groups=mesh['rows'=8,'heads'=4] {'rows'}, use_global_device_ids=true, to_apply=%region_5.6 | all-reduce | flops 256 | bytes 2048 | tf_op jit(solution)/shard_map/psum | solution.py:353
  55.8 15.9 %multiply_reduce_fusion.1 = (f32[4,512]{1,0:T(4,128)S(1)}, f32[4,512]{1,0:T(4,128)S(1)}, bf16[4,8,64,512]{3,2,1,0:T(8,128)(2,1)}, f32[4,8,64,512,1]{3,2,4,1,0:T(8,128)}) fusion(f32[512]{0:T(512)S(1)} %convert_element_type.243, f32[4,512]{1,0:T(4,128)S(1)} %fusion.146, f32[4,8,64]{2,1,0:T(8,128)S(1)} %and_convert_fusion, ...), kind=kOutput, calls=%fused_computation.44 | convolution fusion | flops 9673109504 | bytes 32016384 | tf_op jit(solution)/shard_map/brwtc,tco->brwo/dot_general | solution.py:431
  72.1 17.5 %all-reduce.10 = (f32[4,32]{1,0:T(4,128)S(1)}, f32[4,32]{1,0:T(4,128)S(1)}) all-reduce(f32[4,32]{1,0:T(4,128)S(1)} %reduce_sum.494, f32[4,32]{1,0:T(4,128)S(1)} %reduce_sum.491), channel_id=1, replica_groups=mesh['rows'=8,'heads'=4] {'rows'}, use_global_device_ids=true, to_apply=%region_11.12 | all-reduce | flops 256 | bytes 2048 | tf_op jit(solution)/shard_map/psum | solution.py:353
  114.4 13.0 fusion.42
  130.5 19.6 %all-reduce.9 = (f32[4,32]{1,0:T(4,128)S(1)}, f32[4,32]{1,0:T(4,128)S(1)}) all-reduce(f32[4,32]{1,0:T(4,128)S(1)} %reduce_sum.500, f32[4,32]{1,0:T(4,128)S(1)} %reduce_sum.497), channel_id=1, replica_groups=mesh['rows'=8,'heads'=4] {'rows'}, use_global_device_ids=true, to_apply=%region_17.18 | all-reduce | flops 256 | bytes 2048 | tf_op jit(solution)/shard_map/psum | solution.py:353
  207.3 25.7 %all_to_all.80.qkv_ref = bf16[8,768,128]{2,1,0:T(8,128)(2,1)} all-to-all(bf16[8,768,128]{2,1,0:T(8,128)(2,1)S(1)} %get-tuple-element.116), channel_id=1, replica_groups=mesh['rows'=8,'heads'=4] {'rows'}, dimensions={0} | all-to-all | bytes 3145728 | tf_op jit(solution)/shard_map/all_to_all | solution.py:497
  233.0 24.1 %all_to_all.81.qkv_ref = bf16[8,768,128]{2,1,0:T(8,128)(2,1)} all-to-all(bf16[8,768,128]{2,1,0:T(8,128)(2,1)S(1)} %get-tuple-element.119), channel_id=1, replica_groups=mesh['rows'=8,'heads'=4] {'rows'}, dimensions={0} | all-to-all | bytes 3145728 | tf_op jit(solution)/shard_map/all_to_all | solution.py:497
  263.6 18.8 %all-to-all-done.4.qkv_ref = bf16[8,768,128]{2,1,0:T(8,128)(2,1)} async-done(((bf16[8,768,128]{2,1,0:T(8,128)(2,1)}), bf16[8,768,128]{2,1,0:T(8,128)(2,1)}, u32[]{:S(2)}, u32[]{:S(2)}) %all-to-all-start.4) | async-done | bytes 1572896 | tf_op jit(solution)/shard_map/all_to_all | solution.py:497
  324.4 28.7 %attend.6 = (bf16[8,256,128]{2,1,0:T(8,128)(2,1)}, f32[4096,128]{1,0:T(8,128)S(1)}) custom-call(s32[1]{0:T(128)} %get-tuple-element.182.side_ref, bf16[8,768,128]{2,1,0:T(8,128)(2,1)} %all-to-all-done.4.qkv_ref), custom_call_target="tpu_custom_call" | custom-call | flops 17179869184 | bytes 8388608 | tf_op jit(solution)/shard_map/attend/pallas_call | solution.py:183
  358.7 10.6 attend.7
  403.0 18.0 %broadcast_add_fusion = f32[4,512,4096]{2,1,0:T(8,128)} fusion(f32[4096]{0:T(1024)S(1)} %convert_element_type.265, bf16[512,4096]{1,0:T(8,128)(2,1)} %param.62, f32[4,512,512]{1,2,0:T(8,128)S(1)} %get-tuple-element.187, f32[512]{0:T(512)S(1)} %convert_element_type.263, f32[512]{0:T(512)S(1)} %convert_element_type.262, f32[4,512]{1,0:T(4,128)S(1)} %fusion.155, ...), kind=kOutput, calls=%fused_computation.25 | convolution fusion | flops 8603566080 | bytes 41979904 | tf_op jit(solution)/shard_map/blc,co->blo/dot_general | solution.py:457
  421.1 47.4 %multiply_add_fusion = (f32[4,512,2048]{2,1,0:T(8,128)}, f32[4,512,2048]{2,1,0:T(8,128)}, f32[4,512,2048]{2,1,0:T(8,128)}) fusion(f32[4,512,4096]{2,1,0:T(8,128)} %broadcast_add_fusion, bf16[2048,512]{1,0:T(8,128)(2,1)S(1)} %copy-done, f32[4,512,512]{2,1,0:T(8,128)S(1)} %copy-done.31), kind=kOutput, calls=%fused_computation.11 | convolution fusion | flops 4598005760 | bytes 90177536 | tf_op jit(solution)/shard_map/blo,co->blc/dot_general | solution.py:465
  468.5 32.2 %fusion.16 = (f32[4,512,2048]{2,1,0:T(8,128)}, bf16[4,512,2048]{2,1,0:T(8,128)(2,1)}) fusion(f32[4,512,2048]{2,1,0:T(8,128)} %get-tuple-element.188, f32[4,512,2048]{2,1,0:T(8,128)} %get-tuple-element.105, f32[4,512,4096]{2,1,0:T(8,128)} %broadcast_add_fusion), kind=kLoop, calls=%fused_computation.48 | loop fusion | flops 20971520 | bytes 92274688 | tf_op jit(solution)/shard_map/transpose(jvp())/mul | solution.py:408
  500.7 18.6 %fusion.205 = (f32[512]{0:T(512)}, f32[4,512,512]{2,1,0:T(8,128)}) fusion(bf16[512,4096]{1,0:T(8,128)(2,1)} %param.62, f32[4,512,2048]{2,1,0:T(8,128)} %get-tuple-element.109, f32[4,512,2048]{2,1,0:T(8,128)} %get-tuple-element.104), kind=kOutput, calls=%fused_computation.396 | convolution fusion | flops 8607760384 | bytes 41945088 | tf_op jit(solution)/shard_map/blo,co->blc/dot_general | solution.py:465
  549.4 13.8 %all_to_all.82.grad_ref = bf16[8,256,128]{2,1,0:T(8,128)(2,1)} all-to-all(bf16[8,256,128]{2,1,0:T(8,128)(2,1)S(1)} %get-tuple-element.126), channel_id=1, replica_groups=mesh['rows'=8,'heads'=4] {'rows'}, dimensions={0} | all-to-all | bytes 1048576 | tf_op jit(solution)/shard_map/all_to_all | solution.py:497
  593.1 21.5 %attend_back.4 = bf16[8,768,128]{2,1,0:T(8,128)(2,1)} custom-call(s32[1]{0:T(128)} %get-tuple-element.179.side_ref, bf16[8,768,128]{2,1,0:T(8,128)(2,1)} %all_to_all.80.qkv_ref, bf16[8,256,128]{2,1,0:T(8,128)(2,1)} %all_to_all.82.grad_ref, f32[4096,128]{1,0:T(8,128)} %copy-done.6), custom_call_target="tpu_custom_call" | custom-call | flops 42949672960 | bytes 10485760 | tf_op jit(solution)/shard_map/attend_back/pallas_call | solution.py:297
  618.9 16.3 %attend_back.5 = bf16[8,768,128]{2,1,0:T(8,128)(2,1)} custom-call(s32[1]{0:T(128)} %get-tuple-element.180.side_ref, bf16[8,768,128]{2,1,0:T(8,128)(2,1)} %all_to_all.81.qkv_ref, bf16[8,256,128]{2,1,0:T(8,128)(2,1)} %copy-done.48, f32[4096,128]{1,0:T(8,128)} %copy-done.5), custom_call_target="tpu_custom_call" | custom-call | flops 42949672960 | bytes 10485760 | tf_op jit(solution)/shard_map/attend_back/pallas_call | solution.py:297
  645.7 53.3 %attend_back.6 = bf16[8,768,128]{2,1,0:T(8,128)(2,1)} custom-call(s32[1]{0:T(128)} %get-tuple-element.182.side_ref, bf16[8,768,128]{2,1,0:T(8,128)(2,1)} %all-to-all-done.4.qkv_ref, bf16[8,256,128]{2,1,0:T(8,128)(2,1)} %copy-done.47, f32[4096,128]{1,0:T(8,128)} %copy-done.4), custom_call_target="tpu_custom_call" | custom-call | flops 42949672960 | bytes 10485760 | tf_op jit(solution)/shard_map/attend_back/pallas_call | solution.py:297
  703.4 21.6 %attend_back.7 = bf16[8,768,128]{2,1,0:T(8,128)(2,1)} custom-call(s32[1]{0:T(128)} %get-tuple-element.181.side_ref, bf16[8,768,128]{2,1,0:T(8,128)(2,1)} %all-to-all-done.6.qkv_ref, bf16[8,256,128]{2,1,0:T(8,128)(2,1)} %copy-done.49, f32[4096,128]{1,0:T(8,128)} %copy-done.3), custom_call_target="tpu_custom_call" | custom-call | flops 42949672960 | bytes 10485760 | tf_op jit(solution)/shard_map/attend_back/pallas_call | solution.py:297
  817.9 10.6 bitcast_convert_fusion.3
  841.3 11.8 fusion
  853.2 17.0 %bitcast_convert_fusion.2 = bf16[512,4096]{1,0:T(8,128)(2,1)} fusion(f32[4,512,2048]{2,1,0:T(8,128)} %get-tuple-element.109, f32[4,512,2048]{2,1,0:T(8,128)} %get-tuple-element.104, f32[4,512,512]{1,2,0:T(8,128)S(1)} %copy-done.15, f32[512]{0:T(512)S(1)} %copy-done.131, f32[512]{0:T(512)S(1)} %copy-done.105, f32[4,512]{1,0:T(4,128)S(1)} %copy-done.86, ...), kind=kOutput, calls=%fused_computation.33 | convolution fusion | flops 8614051840 | bytes 41963520 | tf_op jit(solution)/shard_map/blc,blo->co/dot_general | solution.py:461
  883.5 11.8 all-reduce.8
  907.6 15.3 %bitcast_convert_fusion = bf16[9,512,512]{2,1,0:T(8,128)(2,1)} fusion(bf16[4,8,64,9,512]{4,2,1,0,3:T(8,128)(2,1)} %copy-done.59, bf16[4,8,64,512]{3,2,1,0:T(8,128)(2,1)S(1)} %get-tuple-element.100), kind=kOutput, calls=%fused_computation.29 | convolution fusion | flops 9666035712 | bytes 25690112 | tf_op jit(solution)/shard_map/brwtc,brwo->tco/dot_general | solution.py:441
  942.0 16.7 %fusion.45 = f32[4,8,64,512]{3,2,0,1:T(8,128)} fusion(bf16[9,512,512,1,1]{2,1,3,4,0:T(8,128)(2,1)} %bitcast.464, bf16[4,8,64,9,512]{4,2,1,0,3:T(8,128)(2,1)} %fusion.61), kind=kOutput, calls=%fused_computation.131 | convolution fusion | flops 9663676416 | bytes 27787264 | tf_op jit(solution)/shard_map/brwtc,tic->brwi/dot_general | solution.py:448
  965.6 13.2 %all-reduce.7 = (f32[4,32]{1,0:T(4,128)S(1)}, f32[4,32]{1,0:T(4,128)S(1)}) all-reduce(f32[4,32]{1,0:T(4,128)S(1)} %reduce_sum.520, f32[4,32]{1,0:T(4,128)S(1)} %reduce_sum.517), channel_id=1, replica_groups=mesh['rows'=8,'heads'=4] {'rows'}, use_global_device_ids=true, to_apply=%region_37.38 | all-reduce | flops 256 | bytes 2048 | tf_op jit(solution)/shard_map/psum | solution.py:353
  987.0 15.4 %bitcast_convert_fusion.1 = bf16[9,512,512]{2,1,0:T(8,128)(2,1)} fusion(bf16[4,8,64,9,512]{4,2,3,1,0:T(8,128)(2,1)} %fusion.81, bf16[4,8,64,512]{3,2,1,0:T(8,128)(2,1)S(1)} %fusion.111), kind=kOutput, calls=%fused_computation.30 | convolution fusion | flops 9666035712 | bytes 25690112 | tf_op jit(solution)/shard_map/brwtc,brwo->tco/dot_general | solution.py:441
  1016.7 16.7 %fusion.48 = f32[4,8,64,512]{3,2,0,1:T(8,128)} fusion(bf16[9,512,512,1,1]{2,1,3,4,0:T(8,128)(2,1)} %bitcast.468, bf16[4,8,64,9,512]{4,2,1,0,3:T(8,128)(2,1)} %copy-done.60), kind=kOutput, calls=%fused_computation.132 | convolution fusion | flops 9663676416 | bytes 27787264 | tf_op jit(solution)/shard_map/brwtc,tic->brwi/dot_general | solution.py:448
  1043.3 26.1 %all-reduce.6 = (f32[4,32]{1,0:T(4,128)S(1)}, f32[4,32]{1,0:T(4,128)S(1)}, f32[2,4,512]{2,0,1:T(2,128)S(1)}) all-reduce(f32[4,32]{1,0:T(4,128)S(1)} %reduce_sum.526, f32[4,32]{1,0:T(4,128)S(1)} %reduce_sum.523, f32[2,4,512]{2,0,1:T(2,128)S(1)} %pad_maximum_fusion.15), channel_id=1, replica_groups=mesh['rows'=8,'heads'=4] {'rows'}, use_global_device_ids=true, to_apply=%region_43.44 | all-reduce | flops 4352 | bytes 34816 | tf_op jit(solution)/shard_map/psum | solution.py:353
  1077.4 96.0 %psum.166 = f32[23,512]{1,0:T(8,128)S(1)} all-reduce(f32[23,512]{1,0:T(8,128)S(1)} %concatenate.86), channel_id=1, replica_groups=mesh['rows'=8,'heads'=4] {'rows','heads'}, use_global_device_ids=true, to_apply=%region_60.61 | all-reduce | flops 11776 | bytes 94208 | tf_op jit(solution)/shard_map/psum | solution.py:734
  1174.2 13.1 %all_gather.3 = f32[2,16,512]{2,0,1:T(2,128)S(1)} all-gather(f32[2,4,512]{2,0,1:T(2,128)S(1)} %get-tuple-element.79), channel_id=1, replica_groups=mesh['rows'=8,'heads'=4] {'heads'}, dimensions={1}, use_global_device_ids=true | all-gather | bytes 81920 | tf_op jit(solution)/shard_map/all_gather | solution.py:697
  1203.8 87.4 %all-reduce.15.cloned.1.call-done = (bf16[576,512]{1,0:T(8,128)(2,1)}, bf16[576,512]{1,0:T(8,128)(2,1)}, bf16[64,512]{1,0:T(8,128)(2,1)}, bf16[64,1536]{1,0:T(8,...) async-done(((bf16[576,512]{1,0:T(8,128)(2,1)}, bf16[576,512]{1,0:T(8,128)(2,1)}, ...) | async-done | bytes 2359312 | tf_op jit(solution)/shard_map/psum | solution.py:759
  (622 shorter events, 508.6 us)
Async XLA Ops:
  7.2 413.9 %copy-start = (bf16[2048,512]{1,0:T(8,128)(2,1)S(1)}, bf16[2048,512]{1,0:T(8,128)(2,1)}, u32[]{:S(2)}) copy-start(bf16[2048,512]{1,0:T(8,128)(2,1)} %param.64) | copy-start | bytes 6291460
  31.4 3.5 collective-permute-start
  32.8 3.4 collective-permute-start.1
  93.6 2.8 collective-permute-start.2
  94.9 4.5 collective-permute-start.3
  96.3 300.7 %copy-start.101 = (f32[512]{0:T(512)}, f32[512]{0:T(512)S(1)}, u32[]{:S(2)}) copy-start(f32[512]{0:T(512)S(1)} %convert_element_type.252) | copy-start | bytes 6148
  257.1 25.3 %all-to-all-start.4 = ((bf16[8,768,128]{2,1,0:T(8,128)(2,1)}), bf16[8,768,128]{2,1,0:T(8,128)(2,1)}, u32[]{:S(2)}, u32[]{:S(2)}) async-start(bf16[8,768,128]{2,1,0:T(8,128)(2,1)} %get-tuple-element.118), calls=%async_computation.4 | async-start | bytes 3145728 | tf_op jit(solution)/shard_map/all_to_all | solution.py:497
  282.4 25.3 %all-to-all-start.6 = ((bf16[8,768,128]{2,1,0:T(8,128)(2,1)}), bf16[8,768,128]{2,1,0:T(8,128)(2,1)}, u32[]{:S(2)}, u32[]{:S(2)}) async-start(bf16[8,768,128]{2,1,0:T(8,128)(2,1)} %get-tuple-element.117), calls=%async_computation.6 | async-start | bytes 3145728 | tf_op jit(solution)/shard_map/all_to_all | solution.py:497
  307.8 13.2 %all-to-all-start.1 = ((bf16[8,256,128]{2,1,0:T(8,128)(2,1)}), bf16[8,256,128]{2,1,0:T(8,128)(2,1)S(1)}, u32[]{:S(2)}, u32[]{:S(2)}) async-start(bf16[8,256,128]{2,1,0:T(8,128)(2,1)} %get-tuple-element.39), calls=%async_computation.1 | async-start | bytes 1048576 | tf_op jit(solution)/shard_map/all_to_all | solution.py:506
  320.9 33.5 %all-to-all-start.3 = ((bf16[8,256,128]{2,1,0:T(8,128)(2,1)}), bf16[8,256,128]{2,1,0:T(8,128)(2,1)S(1)}, u32[]{:S(2)}, u32[]{:S(2)}) async-start(bf16[8,256,128]{2,1,0:T(8,128)(2,1)} %get-tuple-element.40), calls=%async_computation.3 | async-start | bytes 1048576 | tf_op jit(solution)/shard_map/all_to_all | solution.py:506
  354.4 16.2 %all-to-all-start.5 = ((bf16[8,256,128]{2,1,0:T(8,128)(2,1)}), bf16[8,256,128]{2,1,0:T(8,128)(2,1)}, u32[]{:S(2)}, u32[]{:S(2)}) async-start(bf16[8,256,128]{2,1,0:T(8,128)(2,1)} %get-tuple-element.41), calls=%async_computation.5 | async-start | bytes 1048576 | tf_op jit(solution)/shard_map/all_to_all | solution.py:506
  370.7 15.8 %all-to-all-start.7 = ((bf16[8,256,128]{2,1,0:T(8,128)(2,1)}), bf16[8,256,128]{2,1,0:T(8,128)(2,1)}, u32[]{:S(2)}, u32[]{:S(2)}) async-start(bf16[8,256,128]{2,1,0:T(8,128)(2,1)} %get-tuple-element.42), calls=%async_computation.7 | async-start | bytes 1048576 | tf_op jit(solution)/shard_map/all_to_all | solution.py:506
  563.3 13.2 %all-to-all-start.10 = ((bf16[8,256,128]{2,1,0:T(8,128)(2,1)}), bf16[8,256,128]{2,1,0:T(8,128)(2,1)S(1)}, u32[]{:S(2)}, u32[]{:S(2)}) async-start(bf16[8,256,128]{2,1,0:T(8,128)(2,1)} %get-tuple-element.127), calls=%async_computation.10 | async-start | bytes 1048576 | tf_op jit(solution)/shard_map/all_to_all | solution.py:497
  576.4 13.2 %all-to-all-start.12 = ((bf16[8,256,128]{2,1,0:T(8,128)(2,1)}), bf16[8,256,128]{2,1,0:T(8,128)(2,1)S(1)}, u32[]{:S(2)}, u32[]{:S(2)}) async-start(bf16[8,256,128]{2,1,0:T(8,128)(2,1)} %get-tuple-element.129), calls=%async_computation.12 | async-start | bytes 1048576 | tf_op jit(solution)/shard_map/all_to_all | solution.py:497
  579.9 611.5 %reduce-scatter.17.cloned.1.call-start = ((), (), s32[]{:S(2)}) async-start(), calls=%async_computation.28 | async-start | bytes 589824 | tf_op jit(solution)/shard_map/reduce_scatter | solution.py:758
  589.6 25.0 %all-to-all-start.14 = ((bf16[8,256,128]{2,1,0:T(8,128)(2,1)}), bf16[8,256,128]{2,1,0:T(8,128)(2,1)S(1)}, u32[]{:S(2)}, u32[]{:S(2)}) async-start(bf16[8,256,128]{2,1,0:T(8,128)(2,1)} %get-tuple-element.128), calls=%async_computation.14 | async-start | bytes 1048576 | tf_op jit(solution)/shard_map/all_to_all | solution.py:497
  614.6 26.8 %all-to-all-start.9 = ((bf16[8,768,128]{2,1,0:T(8,128)(2,1)}), bf16[8,768,128]{2,1,0:T(8,128)(2,1)}, u32[]{:S(2)}, u32[]{:S(2)}) async-start(bf16[8,768,128]{2,1,0:T(8,128)(2,1)} %attend_back.4), calls=%async_computation.9 | async-start | bytes 3145728 | tf_op jit(solution)/shard_map/all_to_all | solution.py:506
  641.4 57.7 %all-to-all-start.11 = ((bf16[8,768,128]{2,1,0:T(8,128)(2,1)}), bf16[8,768,128]{2,1,0:T(8,128)(2,1)}, u32[]{:S(2)}, u32[]{:S(2)}) async-start(bf16[8,768,128]{2,1,0:T(8,128)(2,1)} %attend_back.5), calls=%async_computation.11 | async-start | bytes 3145728 | tf_op jit(solution)/shard_map/all_to_all | solution.py:506
  699.0 25.9 %all-to-all-start.13 = ((bf16[8,768,128]{2,1,0:T(8,128)(2,1)}), bf16[8,768,128]{2,1,0:T(8,128)(2,1)}, u32[]{:S(2)}, u32[]{:S(2)}) async-start(bf16[8,768,128]{2,1,0:T(8,128)(2,1)} %attend_back.6), calls=%async_computation.13 | async-start | bytes 3145728 | tf_op jit(solution)/shard_map/all_to_all | solution.py:506
  724.9 25.3 %all-to-all-start.15 = ((bf16[8,768,128]{2,1,0:T(8,128)(2,1)}), bf16[8,768,128]{2,1,0:T(8,128)(2,1)}, u32[]{:S(2)}, u32[]{:S(2)}) async-start(bf16[8,768,128]{2,1,0:T(8,128)(2,1)} %attend_back.7), calls=%async_computation.15 | async-start | bytes 3145728 | tf_op jit(solution)/shard_map/all_to_all | solution.py:506
  729.2 462.2 %reduce-scatter.23.cloned.1.call-start = ((), (), s32[]{:S(2)}) async-start(), calls=%async_computation.31 | async-start | bytes 589824 | tf_op jit(solution)/shard_map/reduce_scatter | solution.py:758
  741.7 449.8 %reduce-scatter.13.cloned.1.call-start = ((), (), s32[]{:S(2)}) async-start(), calls=%async_computation.26 | async-start | bytes 589824 | tf_op jit(solution)/shard_map/reduce_scatter | solution.py:758
  817.8 373.7 %reduce-scatter.21.cloned.1.call-start = ((), (), s32[]{:S(2)}) async-start(), calls=%async_computation.30 | async-start | bytes 2359296 | tf_op jit(solution)/shard_map/reduce_scatter | solution.py:758
  828.5 363.0 %reduce-scatter.15.cloned.1.call-start = ((), (), s32[]{:S(2)}) async-start(), calls=%async_computation.27 | async-start | bytes 1769472 | tf_op jit(solution)/shard_map/reduce_scatter | solution.py:758
  841.2 350.3 %reduce-scatter.19.cloned.1.call-start = ((), (), s32[]{:S(2)}) async-start(), calls=%async_computation.29 | async-start | bytes 4718592 | tf_op jit(solution)/shard_map/reduce_scatter | solution.py:758
  870.2 321.3 %reduce-scatter.11.cloned.1.call-start = ((), (), s32[]{:S(2)}) async-start(), calls=%async_computation.25 | async-start | bytes 5308416 | tf_op jit(solution)/shard_map/reduce_scatter | solution.py:758
  904.0 19.0 %collective-permute-start.4 = (bf16[4,1,64,512]{3,2,1,0:T(8,128)(2,1)S(1)}, bf16[4,1,64,512]{3,2,1,0:T(8,128)(2,1)S(1)}, u32[]{:S(2)}, u32[]{:S(2)}) collective-permute-start(bf16[4,1,64,512]{3,2,1,0:T(8,128)(2,1)S(1)} %get-tuple-element.136), channel_id=1, source_target_pairs={{0,4},{4,8},{8,12},{12,16},{16,20},{20,24},{24,28},{1,5},{5,9},{9,... | collective-permute-start | bytes 786440 | tf_op jit(solution)/shard_map/ppermute | solution.py:326
  905.9 17.1 %collective-permute-start.5 = (bf16[4,1,64,512]{3,2,1,0:T(8,128)(2,1)S(1)}, bf16[4,1,64,512]{3,2,1,0:T(8,128)(2,1)S(1)}, u32[]{:S(2)}, u32[]{:S(2)}) collective-permute-start(bf16[4,1,64,512]{3,2,1,0:T(8,128)(2,1)S(1)} %get-tuple-element.137), channel_id=1, source_target_pairs={{4,0},{8,4},{12,8},{16,12},{20,16},{24,20},{28,24},{5,1},{9,5},{13... | collective-permute-start | bytes 786440 | tf_op jit(solution)/shard_map/ppermute | solution.py:329
  922.9 268.6 %reduce-scatter.9.cloned.1.call-start = ((), (), s32[]{:S(2)}) async-start(), calls=%async_computation.24 | async-start | bytes 5308416 | tf_op jit(solution)/shard_map/reduce_scatter | solution.py:758
  983.5 19.0 %collective-permute-start.6 = (bf16[4,1,64,512]{3,2,1,0:T(8,128)(2,1)S(1)}, bf16[4,1,64,512]{3,2,1,0:T(8,128)(2,1)S(1)}, u32[]{:S(2)}, u32[]{:S(2)}) collective-permute-start(bf16[4,1,64,512]{3,2,1,0:T(8,128)(2,1)S(1)} %get-tuple-element.134), channel_id=1, source_target_pairs={{0,4},{4,8},{8,12},{12,16},{16,20},{20,24},{24,28},{1,5},{5,9},{9,... | collective-permute-start | bytes 786440 | tf_op jit(solution)/shard_map/ppermute | solution.py:326
  985.5 17.0 %collective-permute-start.7 = (bf16[4,1,64,512]{3,2,1,0:T(8,128)(2,1)S(1)}, bf16[4,1,64,512]{3,2,1,0:T(8,128)(2,1)S(1)}, u32[]{:S(2)}, u32[]{:S(2)}) collective-permute-start(bf16[4,1,64,512]{3,2,1,0:T(8,128)(2,1)S(1)} %get-tuple-element.135), channel_id=1, source_target_pairs={{4,0},{8,4},{12,8},{16,12},{20,16},{24,20},{28,24},{5,1},{9,5},{13... | collective-permute-start | bytes 786440 | tf_op jit(solution)/shard_map/ppermute | solution.py:329
  1002.4 288.8 %all-reduce.15.cloned.1.call-start = ((), (), s32[]{:S(2)}) async-start(), calls=%async_computation.32 | async-start | bytes 4718592 | tf_op jit(solution)/shard_map/psum | solution.py:759
  (153 other events, 2849.0 us)
Sparse Core Ops, SparseCore 0:
  585.1 59.3 reduce-scatter.16
  741.8 87.4 reduce-scatter.22
  833.0 70.1 reduce-scatter.12
  906.6 41.2 reduce-scatter.20
  951.0 38.6 reduce-scatter.14
  992.9 51.3 reduce-scatter.18
  1048.2 53.9 reduce-scatter.10
  1105.6 54.4 reduce-scatter.8
  1191.7 99.4 all-reduce.14

commit v2 on v1

v2 whole, which is shorter than its diff:
```python
from functools import partial
import math

import jax
import jax.numpy as jnp
from jax import lax
from jax.experimental import pallas as pl
from jax.experimental.pallas import tpu as pltpu
from jax.sharding import PartitionSpec as P

HEADS = 8
GROUPS = 32
GN_EPS = 1e-06
LN_EPS = 1e-05
HIGH = lax.Precision.HIGHEST
LOG2E = math.log2(math.e)
BF = jnp.bfloat16
F32 = jnp.float32

def dot_nt(lhs, rhs):
    return lax.dot_general(lhs, rhs, (((1,), (1,)), ((), ())), preferred_element_type=F32)


def dot_nn(lhs, rhs):
    return lax.dot_general(lhs, rhs, (((1,), (0,)), ((), ())), preferred_element_type=F32)


def lane_ids(rows):
    return lax.broadcasted_iota(jnp.int32, (rows, 128), 1)


def swap_halves(field):
    return pltpu.roll(field, 64, 1)


def pieces_of(column):
    top = column.astype(BF).astype(F32)
    rest = column - top
    mid = rest.astype(BF).astype(F32)
    return (top, mid, rest - mid)


def extras(column, lanes, first):
    top, mid, low = pieces_of(column)
    return jnp.where(
        lanes == first, top, jnp.where(lanes == first + 1, mid, jnp.where(lanes == first + 2, low, 0.0))
    )


def block_of(count, pref):
    for size in pref:
        if count % size == 0:
            return size
    return count


def crop(field, width, side):
    rows = field.shape[0] // width
    if side == width:
        return field
    return field.reshape(rows, width, 128)[:, :side].reshape(rows * side, 128)


def uncrop(field, width, side):
    if side == width:
        return field
    rows = field.shape[0] // side
    spread = field.reshape(rows, side, 128)
    return jnp.concatenate(
        [spread, jnp.zeros((rows, width - side, 128), field.dtype)], axis=1
    ).reshape(rows * width, 128)


def unpack_pairs(pairs):
    return jnp.concatenate([pairs, swap_halves(pairs)], axis=0)


def pack_pairs(field, lanes):
    half = field.shape[0] // 2
    return jnp.where(lanes[:half] < 64, field[:half], swap_halves(field[half:]))


def attend_kernel(width, scale, side_ref, qkv_ref, out_ref, norm_ref, q_s, k_s, v_s, vt_s, top_s, safe_s):
    bands, packed, _ = qkv_ref.shape
    band_tokens = packed * 2 // 3
    band_rows = band_tokens // width
    side_now = side_ref[0]

    def variant(side):
        tokens = side * side
        used = side // band_rows
        own = band_rows * side
        lanes = lane_ids(own)
        low = lanes < 64
        row_ids = lax.broadcasted_iota(jnp.int32, (128, 128), 0)
        col_ids = lax.broadcasted_iota(jnp.int32, (128, 128), 1)
        picks = jnp.where((row_ids < 64) == (col_ids < 64), 1.0, 0.0).astype(BF)

        def gather_band(band, norms):
            pairs = crop(qkv_ref[band, band_tokens:, :].astype(F32), width, side)
            keys = crop(qkv_ref[band, :band_tokens, :].astype(F32), width, side)
            queries = unpack_pairs(pairs) * (scale * LOG2E)
            head = queries.astype(BF).astype(F32)
            turned = swap_halves(keys)
            rows = pl.ds(pl.multiple_of(band * own, 16), own)
            q_s[rows, :] = jnp.where(low, head, swap_halves(queries - head)).astype(BF)
            k_s[rows, :] = jnp.where(low, keys, turned).astype(BF)
            v_s[rows, :] = jnp.where(low, turned, jnp.where(lanes == 64, 1.0, 0.0)).astype(BF)
            joint = jnp.where(low, queries, turned)
            sums = dot_nn((joint * joint).astype(BF), picks)
            return jnp.maximum(norms, jnp.max(sums, axis=0, keepdims=True))

        norms = lax.fori_loop(0, used, gather_band, jnp.zeros((1, 128), F32))
        step = block_of(tokens, (512, 256))
        for first in range(0, tokens, step):
            vt_s[:, first : first + step] = v_s[first : first + step, :].T
        first_lanes = lane_ids(1) < 64
        query_top = jnp.max(jnp.where(first_lanes, norms, 0.0))
        key_top = jnp.max(jnp.where(first_lanes, 0.0, norms))
        safe = query_top * key_top * 1.05 <= 100.0 * 100.0
        bq = block_of(tokens, (512, 768, 256))
        bk = block_of(tokens, (512, 768, 256))

        @pl.when(safe)
        def _():
            top_s[...] = jnp.zeros_like(top_s)

        @pl.when(jnp.logical_not(safe))
        def _():
            def tops(qi, _):
                cols = pl.ds(pl.multiple_of(qi * bq, 256), bq)
                queries = q_s[cols, :]

                def more(ki, top):
                    scores = dot_nt(k_s[pl.ds(pl.multiple_of(ki * bk, 256), bk), :], queries)
                    return jnp.maximum(top, jnp.max(scores, axis=0, keepdims=True))

                top = lax.fori_loop(0, tokens // bk, more, jnp.full((1, bq), -jnp.inf, F32))
                top_s[:, cols] = jnp.broadcast_to(top, (8, bq))
                return 0

            lax.fori_loop(0, tokens // bq, tops, 0)

        def main(qi, _):
            cols = pl.ds(pl.multiple_of(qi * bq, 256), bq)
            queries = q_s[cols, :]
            top = top_s[0:1, cols]
            total = jnp.zeros((80, bq), F32)
            for first in range(0, tokens, bk):
                scores = dot_nt(k_s[first : first + bk, :], queries)
                weights = jnp.exp2(scores - top).astype(BF)
                total = total + dot_nn(vt_s[0:80, first : first + bk], weights)
            row_total = total[64:65]
            mixed = total[:64] / row_total
            log_total = jnp.broadcast_to(top + jnp.log2(row_total), (64, bq))
            norm_ref[cols, :] = jnp.concatenate([mixed, log_total], axis=0).T
            return 0

        lax.fori_loop(0, tokens // bq, main, 0)

        def spread_band(band, _):
            rows = pl.ds(pl.multiple_of(band * own, 16), own)
            pairs = pack_pairs(norm_ref[rows, :], lanes)
            out_ref[band] = uncrop(pairs, width, side).astype(BF)
            return 0

        lax.fori_loop(0, used, spread_band, 0)
        if used < bands:
            out_ref[used:] = jnp.zeros((bands - used,) + out_ref.shape[1:], BF)

    for side in (width, width * 3 // 4, width // 2):
        pl.when(side_now == side)(partial(variant, side))


def attend(side, qkv, width, scale):
    bands, packed, _ = qkv.shape
    tokens = bands * packed * 2 // 3
    vm = pl.BlockSpec(memory_space=pltpu.VMEM)
    return pl.pallas_call(
        partial(attend_kernel, width, scale),
        out_shape=(
            jax.ShapeDtypeStruct((bands, packed // 3, 128), BF),
            jax.ShapeDtypeStruct((tokens, 128), F32),
        ),
        in_specs=[pl.BlockSpec(memory_space=pltpu.SMEM), vm],
        out_specs=(vm, vm),
        scratch_shapes=[
            pltpu.VMEM((tokens, 128), BF),
            pltpu.VMEM((tokens, 128), BF),
            pltpu.VMEM((tokens, 128), BF),
            pltpu.VMEM((128, tokens), BF),
            pltpu.VMEM((8, tokens), F32),
            pltpu.SMEM((1,), jnp.int32),
        ],
        compiler_params=pltpu.CompilerParams(vmem_limit_bytes=48 << 20),
        cost_estimate=pl.CostEstimate(
            flops=4 * 256 * tokens * tokens, bytes_accessed=8 << 20, transcendentals=tokens * tokens
        ),
        name="attend",
    )(side, qkv)


def attend_back_kernel(width, scale, side_ref, qkv_ref, grad_ref, norm_ref, out_ref,
                       q_s, k_s, kn_s, g_s, v_s, qt_s, gt_s, dq_s, dkv_s):
    bands, packed, _ = qkv_ref.shape
    band_tokens = packed * 2 // 3
    band_rows = band_tokens // width
    side_now = side_ref[0]

    def variant(side):
        tokens = side * side
        used = side // band_rows
        own = band_rows * side
        lanes = lane_ids(own)
        low = lanes < 64
        ones_high = jnp.where((lanes >= 64) & (lanes < 67), 1.0, 0.0)
        ones_low = jnp.where(lanes < 3, 1.0, 0.0).astype(BF)

        def gather_band(band, _):
            queries = unpack_pairs(crop(qkv_ref[band, band_tokens:, :].astype(F32), width, side))
            keys = crop(qkv_ref[band, :band_tokens, :].astype(F32), width, side)
            grads = unpack_pairs(crop(grad_ref[0, band].astype(F32), width, side))
            rows = pl.ds(pl.multiple_of(band * own, 16), own)
            mixed = norm_ref[rows, :]
            delta = jnp.sum(jnp.where(low, grads * mixed, 0.0), axis=1, keepdims=True)
            log_total = mixed[:, 64:65]
            scaled = queries * (scale * LOG2E)
            head = scaled.astype(BF).astype(F32)
            turned = swap_halves(keys)
            q_s[rows, :128] = jnp.where(low, head, swap_halves(scaled - head)).astype(BF)
            q_s[rows, 128:] = extras(-log_total, lanes, 0).astype(BF)
            k_s[rows, :128] = jnp.where(low, keys, turned).astype(BF)
            k_s[rows, 128:] = ones_low
            kn_s[rows, :] = jnp.where(low, keys, 0.0).astype(BF)
            g_s[rows, :] = jnp.where(low, grads, extras(-delta, lanes, 64)).astype(BF)
            v_s[rows, :] = jnp.where(low, turned, ones_high).astype(BF)
            dq_s[rows, :] = jnp.where(low, queries, swap_halves(grads))
            return 0

        lax.fori_loop(0, used, gather_band, 0)
        step = block_of(tokens, (512, 256))
        for first in range(0, tokens, step):
            turned = dq_s[first : first + step, :].T.astype(BF)
            qt_s[:, first : first + step] = turned[:64]
            gt_s[:, first : first + step] = turned[64:]
        dkv_s[...] = jnp.zeros_like(dkv_s)
        bq = block_of(tokens, (512, 768, 256))
        bk = block_of(tokens, (512, 768, 256))

        def main(qi, _):
            rows = pl.ds(pl.multiple_of(qi * bq, 256), bq)
            queries = q_s[rows, :]
            grads = g_s[rows, :]
            grads_t = gt_s[:, rows]
            queries_t = qt_s[:, rows]
            total = jnp.zeros((bq, 128), F32)
            for first in range(0, tokens, bk):
                probs = jnp.exp2(dot_nt(queries, k_s[first : first + bk, :]))
                slopes = dot_nt(grads, v_s[first : first + bk, :])
                grad_scores = (probs * slopes).astype(BF)
                dkv_s[64:, first : first + bk] += dot_nn(grads_t, probs.astype(BF))
                dkv_s[:64, first : first + bk] += dot_nn(queries_t, grad_scores)
                total = total + dot_nn(grad_scores, kn_s[first : first + bk, :])
            dq_s[rows, :] = total
            return 0

        lax.fori_loop(0, tokens // bq, main, 0)
        for first in range(0, tokens, step):
            turned = dkv_s[:, first : first + step].T
            k_s[first : first + step, :128] = jnp.where(
                lane_ids(step) < 64, turned * scale, turned
            ).astype(BF)

        def spread_band(band, _):
            rows = pl.ds(pl.multiple_of(band * own, 16), own)
            out_ref[band, :band_tokens] = uncrop(k_s[rows, :128], width, side)
            pairs = pack_pairs(dq_s[rows, :] * scale, lanes)
            out_ref[band, band_tokens:] = uncrop(pairs, width, side).astype(BF)
            return 0

        lax.fori_loop(0, used, spread_band, 0)
        if used < bands:
            out_ref[used:] = jnp.zeros((bands - used,) + out_ref.shape[1:], BF)

    for side in (width, width * 3 // 4, width // 2):
        pl.when(side_now == side)(partial(variant, side))


def attend_back(side, qkv, grads, spot, norms, width, scale):
    bands, packed, _ = qkv.shape
    tokens = bands * packed * 2 // 3
    vm = pl.BlockSpec(memory_space=pltpu.VMEM)
    return pl.pallas_call(
        partial(attend_back_kernel, width, scale),
        out_shape=jax.ShapeDtypeStruct((bands, packed, 128), BF),
        grid=(1,),
        in_specs=[
            pl.BlockSpec(memory_space=pltpu.SMEM),
            vm,
            pl.BlockSpec((1,) + grads.shape[1:], lambda at: (spot, 0, 0, 0)),
            vm,
        ],
        out_specs=vm,
        scratch_shapes=[
            pltpu.VMEM((tokens, 256), BF),
            pltpu.VMEM((tokens, 256), BF),
            pltpu.VMEM((tokens, 128), BF),
            pltpu.VMEM((tokens, 128), BF),
            pltpu.VMEM((tokens, 128), BF),
            pltpu.VMEM((64, tokens), BF),
            pltpu.VMEM((64, tokens), BF),
            pltpu.VMEM((tokens, 128), F32),
            pltpu.VMEM((128, tokens), F32),
        ],
        compiler_params=pltpu.CompilerParams(vmem_limit_bytes=56 << 20),
        cost_estimate=pl.CostEstimate(
            flops=10 * 256 * tokens * tokens, bytes_accessed=10 << 20, transcendentals=tokens * tokens
        ),
        name="attend_back",
    )(side, qkv, grads, norms)


def dot_tn(lhs, rhs):
    return lax.dot_general(lhs, rhs, (((0,), (0,)), ((), ())), preferred_element_type=F32)


def row_of(table, at):
    ids = lax.broadcasted_iota(jnp.int32, table.shape, 0)
    return jnp.sum(jnp.where(ids == at, table, 0.0), axis=0, keepdims=True)


def put_row(table_ref, at, row):
    ids = lax.broadcasted_iota(jnp.int32, table_ref.shape, 0)
    table_ref[...] = jnp.where(ids == at, row, table_ref[...])


def col_sum(field):
    return jnp.sum(field, axis=0, keepdims=True)


def pixel_inside(shape, first_row, side, width):
    token = lax.broadcasted_iota(jnp.int32, shape, 0)
    row = first_row + lax.shift_right_logical(token, int(math.log2(width)))
    return (row >= 0) & (row < side) & ((token & (width - 1)) < side)


def moments(avg_ref, at):
    table = avg_ref[...]
    mean = row_of(table, 2 * at)
    return mean, lax.rsqrt(row_of(table, 2 * at + 1) - mean * mean + GN_EPS)


def put_taps(taps_s, first, field, width, flipped):
    channels = field.shape[1]
    column = lax.broadcasted_iota(jnp.int32, field.shape, 0) & (width - 1)
    count = field.shape[0]
    left = jnp.where(column == 0, 0.0, pltpu.roll(field, 1, 0))
    right = jnp.where(column == width - 1, 0.0, pltpu.roll(field, count - 1, 0))
    order = (right, field, left) if flipped else (left, field, right)
    for at, part in enumerate(order):
        taps_s[first : first + count, at * channels : (at + 1) * channels] = part.astype(BF)


VMEM_WHOLE = pl.BlockSpec(memory_space=pltpu.VMEM)
SMEM_WHOLE = pl.BlockSpec(memory_space=pltpu.SMEM)


def image_block(tokens, channels):
    return pl.BlockSpec((1, tokens, channels), lambda at: (at, 0, 0))


def edge_block(width, channels):
    return pl.BlockSpec((2, 1, width, channels), lambda at: (0, at, 0, 0))


def table_block(channels, rows=8):
    return pl.BlockSpec((rows, channels), lambda at: (0, 0))


def fixed_block(shape):
    return pl.BlockSpec(shape, lambda at: (0,) * len(shape), pipeline_mode=pl.Buffered(1))


def conv_forward_kernel(width, base_given, *refs):
    if base_given:
        (place, sides, field_ref, halo_ref, avg_ref, gain_ref, bias_ref, weight_ref, shift_ref,
         base_ref, out_ref, edge_ref, stats_ref, taps_s) = refs
    else:
        (place, sides, field_ref, halo_ref, avg_ref, gain_ref, bias_ref, weight_ref, shift_ref,
         out_ref, edge_ref, stats_ref, taps_s) = refs
    at = pl.program_id(0)
    _, tokens, channels = field_ref.shape
    first_row = place[0]
    side = sides[at]
    mean, inv_std = moments(avg_ref, at)
    slope = inv_std * gain_ref[...]
    offset = bias_ref[...] - mean * slope

    def active(field, row):
        normed = field.astype(F32) * slope + offset
        inside = pixel_inside(normed.shape, row, side, width)
        return jnp.where(inside, normed * jax.nn.sigmoid(normed), 0.0)

    rows = tokens // width
    put_taps(taps_s, 0, active(halo_ref[0, 0], first_row - 1), width, False)
    put_taps(taps_s, width, active(field_ref[0], first_row), width, False)
    put_taps(taps_s, width + tokens, active(halo_ref[1, 0], first_row + rows), width, False)
    deep = 3 * channels
    total = dot_nn(taps_s[:tokens], weight_ref[:deep])
    for tap in (1, 2):
        total = total + dot_nn(
            taps_s[tap * width : tap * width + tokens], weight_ref[tap * deep : (tap + 1) * deep]
        )
    total = total + row_of(shift_ref[...], at)
    inside = pixel_inside(total.shape, first_row, side, width)
    if base_given:
        total = total + jnp.where(inside, base_ref[0].astype(F32), 0.0)
    out_ref[0] = total
    edge_ref[0, 0] = total[:width].astype(BF)
    edge_ref[1, 0] = total[tokens - width :].astype(BF)
    masked = jnp.where(inside, total, 0.0)

    @pl.when(at == 0)
    def _():
        stats_ref[...] = jnp.zeros_like(stats_ref)

    put_row(stats_ref, 2 * at, col_sum(masked))
    put_row(stats_ref, 2 * at + 1, col_sum(masked * masked))


def conv_forward(place, sides, field, halo, avg, gain, bias, weight, shift, base, width):
    images, tokens, channels = field.shape
    ins = [place, sides, field, halo, avg, gain, bias, weight, shift]
    specs = [
        SMEM_WHOLE,
        SMEM_WHOLE,
        image_block(tokens, channels),
        edge_block(width, channels),
        table_block(channels),
        table_block(channels, 1),
        table_block(channels, 1),
        fixed_block(weight.shape),
        table_block(channels),
    ]
    if base is not None:
        ins.append(base)
        specs.append(image_block(tokens, channels))
    return pl.pallas_call(
        partial(conv_forward_kernel, width, base is not None),
        grid=(images,),
        out_shape=(
            jax.ShapeDtypeStruct(field.shape, F32),
            jax.ShapeDtypeStruct((2, images, width, channels), BF),
            jax.ShapeDtypeStruct((8, channels), F32),
        ),
        in_specs=specs,
        out_specs=(
            image_block(tokens, channels),
            edge_block(width, channels),
            table_block(channels),
        ),
        scratch_shapes=[pltpu.VMEM((tokens + 2 * width, 3 * channels), BF)],
        compiler_params=pltpu.CompilerParams(vmem_limit_bytes=56 << 20),
        name="conv_forward",
    )(*ins)


def conv_backward_kernel(width, added, *refs):
    refs = list(refs)
    (place, sides, grad_ref, grad_halo, field_ref, field_halo, avg_ref, back_avg, gain_ref) = refs[:9]
    refs = refs[9:]
    if added:
        add_ref, add_halo = refs[:2]
        refs = refs[2:]
    (weight_ref, prior_ref, prior_avg, prior_gain, prior_bias) = refs[:5]
    refs = refs[5:]
    if added:
        kept_ref = refs[0]
        refs = refs[1:]
    (out_ref, edge_ref, stats_ref, sums_ref, weight_grad, taps_s, act_s, total_s) = refs
    at = pl.program_id(0)
    last = pl.num_programs(0) - 1
    _, tokens, channels = grad_ref.shape
    first_row = place[0]
    side = sides[at]
    mean, inv_std = moments(avg_ref, at)
    back = back_avg[...]
    back_mean, back_cross = row_of(back, 2 * at), row_of(back, 2 * at + 1)
    gain = gain_ref[...]
    grad_slope = inv_std * gain
    field_slope = inv_std * inv_std * back_cross
    offset = inv_std * back_mean - mean * field_slope

    def through(grads, field, extra, row):
        moved = grads.astype(F32) * grad_slope - field.astype(F32) * field_slope - offset
        if extra is not None:
            moved = moved + extra.astype(F32)
        return jnp.where(pixel_inside(moved.shape, row, side, width), moved, 0.0)

    rows = tokens // width
    own = through(grad_ref[0], field_ref[0], add_ref[0] if added else None, first_row)
    put_taps(taps_s, width, own, width, True)
    for end, row, first in ((0, first_row - 1, 0), (1, first_row + rows, width + tokens)):
        put_taps(
            taps_s,
            first,
            through(grad_halo[end, 0], field_halo[end, 0], add_halo[end, 0] if added else None, row),
            width,
            True,
        )
    if added:
        kept_ref[0] = own

    @pl.when(at == 0)
    def _():
        stats_ref[...] = jnp.zeros_like(stats_ref)
        sums_ref[...] = jnp.zeros_like(sums_ref)
        total_s[...] = jnp.zeros_like(total_s)

    put_row(sums_ref, at, col_sum(own))
    prior_mean, prior_std = moments(prior_avg, at)
    centred = (prior_ref[0].astype(F32) - prior_mean) * prior_std
    normed = centred * prior_gain[...] + prior_bias[...]
    gate = jax.nn.sigmoid(normed)
    inside = pixel_inside(normed.shape, first_row, side, width)
    act_s[...] = jnp.where(inside, normed * gate, 0.0).T.astype(BF)
    act_t = act_s[...]
    moved = None
    for down in range(3):
        lines = pl.ds((2 - down) * width, tokens)
        for across in range(3):
            tap = 3 * down + across
            low = taps_s[lines, across * channels : (across + 1) * channels]
            part = slice(tap * channels, (tap + 1) * channels)
            term = dot_nt(low, weight_ref[part])
            moved = term if moved is None else moved + term
            total_s[part] += dot_nn(act_t, low)
    grads = jnp.where(inside, moved * (gate + normed * gate * (1.0 - gate)), 0.0)
    out_ref[0] = grads
    edge_ref[0, 0] = grads[:width].astype(BF)
    edge_ref[1, 0] = grads[tokens - width :].astype(BF)
    put_row(stats_ref, 2 * at, col_sum(grads))
    put_row(stats_ref, 2 * at + 1, col_sum(grads * centred))

    @pl.when(at == last)
    def _():
        weight_grad[...] = total_s[...].astype(BF)


def conv_backward(place, sides, grads, grad_halo, field, field_halo, avg, back_avg, gain, extra,
                  extra_halo, weight, prior, prior_avg, prior_gain, prior_bias, width):
    images, tokens, channels = grads.shape
    added = extra is not None
    tok = image_block(tokens, channels)
    edge = edge_block(width, channels)
    table = table_block(channels)
    vector = table_block(channels, 1)
    ins = [place, sides, grads, grad_halo, field, field_halo, avg, back_avg, gain]
    specs = [SMEM_WHOLE, SMEM_WHOLE, tok, edge, tok, edge, table, table, vector]
    if added:
        ins += [extra, extra_halo]
        specs += [tok, edge]
    ins += [weight, prior, prior_avg, prior_gain, prior_bias]
    specs += [fixed_block(weight.shape), tok, table, vector, vector]
    outs = [
        jax.ShapeDtypeStruct(grads.shape, F32),
        jax.ShapeDtypeStruct((2, images, width, channels), BF),
        jax.ShapeDtypeStruct((8, channels), F32),
        jax.ShapeDtypeStruct((8, channels), F32),
        jax.ShapeDtypeStruct(weight.shape, BF),
    ]
    out_specs = [tok, edge, table, table, fixed_block(weight.shape)]
    if added:
        outs.insert(0, jax.ShapeDtypeStruct(grads.shape, F32))
        out_specs.insert(0, tok)
    return pl.pallas_call(
        partial(conv_backward_kernel, width, added),
        grid=(images,),
        out_shape=outs,
        in_specs=specs,
        out_specs=out_specs,
        scratch_shapes=[
            pltpu.VMEM((tokens + 2 * width, 3 * channels), BF),
            pltpu.VMEM((channels, tokens), BF),
            pltpu.VMEM(weight.shape, F32),
        ],
        compiler_params=pltpu.CompilerParams(vmem_limit_bytes=60 << 20),
        name="conv_backward",
    )(*ins)


def layer_stats(field):
    centre = jnp.mean(field, axis=-1, keepdims=True)
    centred = field - centre
    inv_std = lax.rsqrt(jnp.mean(centred * centred, axis=-1, keepdims=True) + LN_EPS)
    return centred * inv_std, inv_std


def layer_back(grads, gain, centred, inv_std):
    scaled = grads * gain
    return inv_std * (
        scaled
        - jnp.mean(scaled, axis=-1, keepdims=True)
        - centred * jnp.mean(scaled * centred, axis=-1, keepdims=True)
    )


def entry_kernel(field_ref, avg_ref, gain_ref, bias_ref, proj_ref, proj_bias, ln_gain, ln_bias, qkv_ref,
                 stream_ref, sent_ref):
    at = pl.program_id(0)
    _, tokens, channels = field_ref.shape
    half = tokens // 2
    mean, inv_std = moments(avg_ref, at)
    slope = inv_std * gain_ref[...]
    flat = (field_ref[0] * slope + (bias_ref[...] - mean * slope)).astype(BF)
    stream = dot_nn(flat, proj_ref[...]) + proj_bias[...]
    stream_ref[0] = stream
    centred, _ = layer_stats(stream)
    joint = dot_nn((centred * ln_gain[...] + ln_bias[...]).astype(BF), qkv_ref[...])
    low = lane_ids(half) < 64
    for head in range(HEADS):
        sent_ref[0, head, :tokens] = joint[:, head * 128 : head * 128 + 128].astype(BF)
        first = 2 * channels + (head // 2) * 128
        upper, lower = joint[:half, first : first + 128], joint[half:, first : first + 128]
        if head % 2 == 0:
            pairs = jnp.where(low, upper, swap_halves(lower))
        else:
            pairs = jnp.where(low, swap_halves(upper), lower)
        sent_ref[0, head, tokens:] = pairs.astype(BF)


def entry(field, avg, gain, bias, proj, proj_bias, ln_gain, ln_bias, qkv):
    images, tokens, channels = field.shape
    vector = table_block(channels, 1)
    return pl.pallas_call(
        entry_kernel,
        grid=(images,),
        out_shape=(
            jax.ShapeDtypeStruct(field.shape, F32),
            jax.ShapeDtypeStruct((images, HEADS, tokens * 3 // 2, 128), BF),
        ),
        in_specs=[
            image_block(tokens, channels),
            table_block(channels),
            vector,
            vector,
            fixed_block(proj.shape),
            vector,
            vector,
            vector,
            fixed_block(qkv.shape),
        ],
        out_specs=(
            image_block(tokens, channels),
            pl.BlockSpec((1, HEADS, tokens * 3 // 2, 128), lambda at: (at, 0, 0, 0)),
        ),
        compiler_params=pltpu.CompilerParams(vmem_limit_bytes=48 << 20),
        name="entry",
    )(field, avg, gain, bias, proj, proj_bias, ln_gain, ln_bias, qkv)


def join_heads(pairs_ref, at):
    half = pairs_ref.shape[-2]
    low = lane_ids(half) < 64
    upper, lower = [], []
    for head in range(0, HEADS, 2):
        one, two = pairs_ref[at, head].astype(F32), pairs_ref[at, head + 1].astype(F32)
        upper.append(jnp.where(low, one, swap_halves(two)))
        lower.append(jnp.where(low, swap_halves(one), two))
    return jnp.concatenate(
        [jnp.concatenate(upper, axis=1), jnp.concatenate(lower, axis=1)], axis=0
    ).astype(BF)


def split_heads(field, out_ref, at):
    half = field.shape[0] // 2
    low = lane_ids(half) < 64
    for head in range(HEADS):
        first = (head // 2) * 128
        upper, lower = field[:half, first : first + 128], field[half:, first : first + 128]
        if head % 2 == 0:
            pairs = jnp.where(low, upper, swap_halves(lower))
        else:
            pairs = jnp.where(low, swap_halves(upper), lower)
        out_ref[at, head] = pairs.astype(BF)


def feed_pieces(channels, wide, hidden, bands):
    size = channels // bands
    geglu = [(at * size, size) for at in range(wide // channels)]
    first = wide // bands
    return (
        geglu,
        [(first, hidden // bands)],
        [(first + hidden // bands, size)],
        [(first + hidden // bands + size, size)],
    )


def feed_kernel(width, bands, per_band, place, sides, *refs):
    given = refs[:per_band]
    (stream_ref, residual_ref, cot_ref, cross_ref, attn_ref, attn_bias, ln_gain, ln_bias,
     geglu_ref, geglu_bias, feed_ref, feed_bias, proj_ref, proj_bias,
     out_ref, three_ref, back_ref, grads_ref, sums_ref, cross_sum, pair_sums, geglu_s, feed_s, proj_s, attn_s,
     mixed_s, sent_s, out_send, out_recv, back_send, back_recv) = refs[per_band:]
    at = pl.program_id(0)
    images = pl.num_programs(0)
    last = images - 1
    me = lax.axis_index("rows")

    def move(src, dst, send, recv, target):
        @pl.when(target != me)
        def _():
            pltpu.make_async_remote_copy(
                src_ref=src, dst_ref=dst, send_sem=send, recv_sem=recv, device_id={"rows": target},
                device_id_type=pl.DeviceIdType.MESH,
            ).start()

        @pl.when(target == me)
        def _():
            pltpu.make_async_copy(src, dst, recv).start()

    def arrived(dst, send, recv, source):
        @pl.when(source != me)
        def _():
            pltpu.make_async_remote_copy(
                src_ref=dst, dst_ref=dst, send_sem=send, recv_sem=recv, device_id={"rows": source},
                device_id_type=pl.DeviceIdType.MESH,
            ).wait_recv()

        @pl.when(source == me)
        def _():
            pltpu.make_async_copy(dst, dst, recv).wait()

    def left(src, send, recv, target):
        @pl.when(target != me)
        def _():
            pltpu.make_async_remote_copy(
                src_ref=src, dst_ref=src, send_sem=send, recv_sem=recv, device_id={"rows": target},
                device_id_type=pl.DeviceIdType.MESH,
            ).wait_send()

    @pl.when(at == 0)
    def _():
        barrier = pltpu.get_barrier_semaphore()
        for away in range(1, bands):
            pl.semaphore_signal(
                barrier, inc=1, device_id={"rows": lax.rem(me + away, bands)},
                device_id_type=pl.DeviceIdType.MESH,
            )
        pl.semaphore_wait(barrier, bands - 1)
        for spot in range(per_band):
            item = me * per_band + spot
            head, image = item // images, lax.rem(item, images)
            for away in range(bands):
                band = lax.rem(me + away, bands)
                move(
                    given[spot].at[band], mixed_s.at[image, head], out_send.at[spot, away],
                    out_recv.at[image, head], band,
                )

    for head in range(HEADS):
        arrived(
            mixed_s.at[at, head], out_send.at[0, 0], out_recv.at[at, head], (head * images + at) // per_band
        )
    _, tokens, channels = stream_ref.shape
    hidden = feed_ref.shape[0]
    side = sides[at]
    inside = pixel_inside((tokens, channels), place[0], side, width)

    @pl.when(at == 0)
    def _():
        for ref in (sums_ref, cross_sum, pair_sums, geglu_s, feed_s, proj_s, attn_s):
            ref[...] = jnp.zeros_like(ref)

    mixed = join_heads(mixed_s, at)
    three = stream_ref[0] + dot_nn(mixed, attn_ref[...]) + (attn_bias[...] + row_of(cross_ref[...], at))
    centred, inv_std = layer_stats(three)
    feed_in = (centred * ln_gain[...] + ln_bias[...]).astype(BF)
    grad_out = jnp.where(inside, cot_ref[0].astype(F32), 0.0)
    branch = grad_out.astype(BF)
    grad_four = dot_nt(branch, proj_ref[...])
    low_feed = grad_four.astype(BF)
    four = three + feed_bias[...]
    grad_in = jnp.zeros((tokens, channels), F32)
    step = 512
    for first in range(0, hidden, step):
        own = slice(first, first + step)
        gates = slice(hidden + first, hidden + first + step)
        value = dot_nn(feed_in, geglu_ref[:, own]) + geglu_bias[:, own]
        gate = dot_nn(feed_in, geglu_ref[:, gates]) + geglu_bias[:, gates]
        back = dot_nt(low_feed, feed_ref[own])
        below = 0.5 + 0.5 * lax.erf(gate * math.sqrt(0.5))
        bell = jnp.exp(gate * gate * -0.5) * (1.0 / math.sqrt(2.0 * math.pi))
        act = gate * below
        gated = (value * act).astype(BF)
        four = four + dot_nn(gated, feed_ref[own])
        feed_s[own] += dot_tn(gated, low_feed)
        grad_value = back * act
        grad_gate = back * value * (below + gate * bell)
        pair_sums[:, own] += col_sum(grad_value)
        pair_sums[:, gates] += col_sum(grad_gate)
        low_value, low_gate = grad_value.astype(BF), grad_gate.astype(BF)
        geglu_s[:, own] += dot_tn(feed_in, low_value)
        geglu_s[:, gates] += dot_tn(feed_in, low_gate)
        grad_in = grad_in + dot_nt(low_value, geglu_ref[:, own]) + dot_nt(low_gate, geglu_ref[:, gates])
    last_in = four.astype(BF)
    proj_s[...] += dot_tn(last_in, branch)
    output = residual_ref[0] + dot_nn(last_in, proj_ref[...]) + proj_bias[...]
    out_ref[0] = jnp.where(inside, output, 0.0).astype(BF)
    grad_three = grad_four + layer_back(grad_in, ln_gain[...], centred, inv_std)
    three_ref[0] = grad_three
    low_attn = grad_three.astype(BF)
    attn_s[...] += dot_tn(mixed, low_attn)
    split_heads(dot_nt(low_attn, attn_ref[...]), sent_s, at)
    for head in range(HEADS):
        item = head * images + at
        move(
            sent_s.at[at, head], back_ref.at[lax.rem(item, per_band), me], back_send.at[at, head],
            back_recv.at[lax.rem(item, per_band), me], item // per_band,
        )
    put_row(cross_sum, at, col_sum(grad_three))
    ids = lax.broadcasted_iota(jnp.int32, sums_ref.shape, 0)
    for row, total in enumerate(
        (col_sum(grad_out), col_sum(grad_four), col_sum(grad_in * centred), col_sum(grad_in))
    ):
        sums_ref[...] += jnp.where(ids == row, total, 0.0)

    @pl.when(at == last)
    def _():
        for spot in range(per_band):
            for away in range(bands):
                band = lax.rem(me + away, bands)
                left(given[spot].at[band], out_send.at[spot, away], out_recv.at[0, 0], band)
                arrived(back_ref.at[spot, band], back_send.at[0, 0], back_recv.at[spot, band], band)
        for image in range(sent_s.shape[0]):
            for head in range(HEADS):
                left(
                    sent_s.at[image, head], back_send.at[image, head], back_recv.at[0, 0],
                    (head * sent_s.shape[0] + image) // per_band,
                )
        halving = len(grads_ref.shape) == 5
        for band in range(bands):
            if halving:
                apart = jnp.bitwise_xor(me, band)
                own = (apart & 1, (apart >> 1) & 1, apart >> 2)
            else:
                own = (band,)
            pieces = feed_pieces(channels, 2 * hidden, hidden, bands)
            for total, parts in zip((geglu_s, feed_s, proj_s, attn_s), pieces):
                for at_col, (first, size) in enumerate(parts):
                    grads_ref[own + (pl.ds(first, size),)] = total[
                        band * size : (band + 1) * size, at_col * channels : (at_col + 1) * channels
                    ].astype(BF)


def feed(place, sides, mixed, stream, residual, cot, cross, attn, attn_bias, ln_gain, ln_bias, geglu,
         geglu_bias, feed_out, feed_bias, proj, proj_bias, width, bands, halving):
    images, tokens, channels = stream.shape
    tok = image_block(tokens, channels)
    vector = table_block(channels, 1)
    table = table_block(channels)
    half = tokens // 2
    per_band = len(mixed)
    anywhere = pl.BlockSpec(memory_space=pl.ANY)
    wide = geglu.shape[1]
    weights = (geglu, feed_out, proj, attn)
    rows = sum(w.size for w in weights) // channels // bands
    lead = (2, 2, 2) if halving else (bands,)
    grads = lead + (rows, channels)
    return pl.pallas_call(
        partial(feed_kernel, width, bands, per_band),
        grid=(images,),
        out_shape=(
            jax.ShapeDtypeStruct(stream.shape, BF),
            jax.ShapeDtypeStruct(stream.shape, F32),
            jax.ShapeDtypeStruct((per_band, bands, half, 128), BF),
        )
        + (
            jax.ShapeDtypeStruct(grads, BF),
            jax.ShapeDtypeStruct((8, channels), F32),
            jax.ShapeDtypeStruct((8, channels), F32),
            jax.ShapeDtypeStruct((1, wide), F32),
        ),
        in_specs=[
            SMEM_WHOLE,
            SMEM_WHOLE,
        ]
        + [anywhere] * per_band
        + [
            tok,
            tok,
            tok,
            table,
            fixed_block(attn.shape),
            vector,
            vector,
            vector,
            fixed_block(geglu.shape),
            table_block(wide, 1),
            fixed_block(feed_out.shape),
            vector,
            fixed_block(proj.shape),
            vector,
        ],
        out_specs=(tok, tok, anywhere)
        + (fixed_block(grads), table, table, table_block(wide, 1)),
        scratch_shapes=[pltpu.VMEM(w.shape, F32) for w in weights]
        + [pltpu.VMEM((images, HEADS, half, 128), BF)] * 2
        + [
            pltpu.SemaphoreType.DMA((per_band, bands)),
            pltpu.SemaphoreType.DMA((images, HEADS)),
            pltpu.SemaphoreType.DMA((images, HEADS)),
            pltpu.SemaphoreType.DMA((per_band, bands)),
        ],
        compiler_params=pltpu.CompilerParams(
            vmem_limit_bytes=62 << 20, collective_id=5, has_side_effects=True
        ),
        name="feed",
    )(place, sides, *mixed, stream, residual, cot, cross, attn, attn_bias, ln_gain, ln_bias, geglu,
      geglu_bias, feed_out, feed_bias, proj, proj_bias)


def leave_kernel(width, place, sides, *refs):
    (packed_ref, stream_ref, three_ref, field_ref, avg_ref, gain_ref, bias_ref, proj_ref, ln_gain, ln_bias,
     qkv_ref, out_ref, edge_ref, stats_ref, sums_ref, grad_qkv, grad_proj, qkv_s, proj_s) = refs
    at = pl.program_id(0)
    last = pl.num_programs(0) - 1
    _, tokens, channels = stream_ref.shape
    inside = pixel_inside((tokens, channels), place[0], sides[at], width)

    @pl.when(at == 0)
    def _():
        for ref in (stats_ref, sums_ref, qkv_s, proj_s):
            ref[...] = jnp.zeros_like(ref)

    queries = join_heads(packed_ref.at[:, :, tokens:, :], 0)
    joint = jnp.concatenate([packed_ref[0, head, :tokens] for head in range(HEADS)] + [queries], axis=1)
    centred, inv_std = layer_stats(stream_ref[0])
    attn_in = (centred * ln_gain[...] + ln_bias[...]).astype(BF)
    qkv_s[...] += dot_tn(attn_in, joint)
    grads = dot_nt(joint, qkv_ref[...])
    grad_stream = three_ref[0] + layer_back(grads, ln_gain[...], centred, inv_std)
    low_in = grad_stream.astype(BF)
    mean, deviation = moments(avg_ref, at)
    normed = (field_ref[0] - mean) * deviation
    flat = (normed * gain_ref[...] + bias_ref[...]).astype(BF)
    proj_s[...] += dot_tn(flat, low_in)
    moved = jnp.where(inside, dot_nt(low_in, proj_ref[...]), 0.0)
    out_ref[0] = moved
    edge_ref[0, 0] = moved[:width].astype(BF)
    edge_ref[1, 0] = moved[tokens - width :].astype(BF)
    put_row(stats_ref, 2 * at, col_sum(moved))
    put_row(stats_ref, 2 * at + 1, col_sum(moved * normed))
    ids = lax.broadcasted_iota(jnp.int32, sums_ref.shape, 0)
    for row, total in enumerate((col_sum(grads * centred), col_sum(grads), col_sum(grad_stream))):
        sums_ref[...] += jnp.where(ids == row, total, 0.0)

    @pl.when(at == last)
    def _():
        grad_qkv[...] = qkv_s[...].astype(BF)
        grad_proj[...] = proj_s[...].astype(BF)


def leave(place, sides, packed, stream, three, field, avg, gain, bias, proj, ln_gain, ln_bias, qkv, width):
    images, tokens, channels = stream.shape
    tok = image_block(tokens, channels)
    vector = table_block(channels, 1)
    table = table_block(channels)
    return pl.pallas_call(
        partial(leave_kernel, width),
        grid=(images,),
        out_shape=(
            jax.ShapeDtypeStruct(stream.shape, F32),
            jax.ShapeDtypeStruct((2, images, width, channels), BF),
            jax.ShapeDtypeStruct((8, channels), F32),
            jax.ShapeDtypeStruct((8, channels), F32),
            jax.ShapeDtypeStruct(qkv.shape, BF),
            jax.ShapeDtypeStruct(proj.shape, BF),
        ),
        in_specs=[
            SMEM_WHOLE,
            SMEM_WHOLE,
            pl.BlockSpec((1,) + packed.shape[1:], lambda at: (at, 0, 0, 0)),
            tok,
            tok,
            tok,
            table,
            vector,
            vector,
            fixed_block(proj.shape),
            vector,
            vector,
            fixed_block(qkv.shape),
        ],
        out_specs=(
            tok,
            edge_block(width, channels),
            table,
            table,
            fixed_block(qkv.shape),
            fixed_block(proj.shape),
        ),
        scratch_shapes=[pltpu.VMEM(qkv.shape, F32), pltpu.VMEM(proj.shape, F32)],
        compiler_params=pltpu.CompilerParams(vmem_limit_bytes=56 << 20),
        name="leave",
    )(place, sides, packed, stream, three, field, avg, gain, bias, proj, ln_gain, ln_bias, qkv)


def exchange_kernel(count, bands, sent_ref, weight_ref, scale_ref, *refs):
    edges, avg_ref, halos = refs[:count], refs[count], refs[count + 1 : 2 * count + 1]
    slots, send_sem, recv_sem, edge_send, edge_recv = refs[2 * count + 1 :]
    me = lax.axis_index("rows")
    barrier = pltpu.get_barrier_semaphore()
    for away in range(1, bands):
        pl.semaphore_signal(
            barrier,
            inc=1,
            device_id={"rows": lax.rem(me + away, bands)},
            device_id_type=pl.DeviceIdType.MESH,
        )
    slots[me] = sent_ref[...]
    pl.semaphore_wait(barrier, bands - 1)
    copies = []
    for at in range(count):
        for end, away in ((0, bands - 1), (1, 1)):
            copies.append(
                pltpu.make_async_remote_copy(
                    src_ref=edges[at].at[end],
                    dst_ref=halos[at].at[1 - end],
                    send_sem=edge_send.at[at, end],
                    recv_sem=edge_recv.at[at, 1 - end],
                    device_id={"rows": lax.rem(me + away, bands)},
                    device_id_type=pl.DeviceIdType.MESH,
                )
            )
    for away in range(1, bands):
        copies.append(
            pltpu.make_async_remote_copy(
                src_ref=sent_ref,
                dst_ref=slots.at[me],
                send_sem=send_sem.at[away],
                recv_sem=recv_sem.at[me],
                device_id={"rows": lax.rem(me + away, bands)},
                device_id_type=pl.DeviceIdType.MESH,
            )
        )
    for copy in copies[2 * count :] + copies[: 2 * count]:
        copy.start()
    for copy in copies:
        copy.wait_send()
    for away in range(1, bands):
        source = lax.rem(me + away, bands)
        pltpu.make_async_remote_copy(
            src_ref=sent_ref,
            dst_ref=slots.at[source],
            send_sem=send_sem.at[away],
            recv_sem=recv_sem.at[source],
            device_id={"rows": source},
            device_id_type=pl.DeviceIdType.MESH,
        ).wait_recv()
    total = slots[0]
    for at in range(1, bands):
        total = total + slots[at]
    channels = total.shape[1]
    size = channels // GROUPS
    rows = lax.broadcasted_iota(jnp.int32, (channels, channels), 0) // size
    cols = lax.broadcasted_iota(jnp.int32, (channels, channels), 1) // size
    same = jnp.where(rows == cols, 1.0, 0.0)
    avg_ref[...] = jnp.dot(
        total * weight_ref[...], same, precision=HIGH, preferred_element_type=F32
    ) * scale_ref[...]
    for copy in copies[: 2 * count]:
        copy.wait_recv()


def exchange(sums, weight, scale, edges, bands):
    count = len(edges)
    hbm = pl.BlockSpec(memory_space=pl.ANY)
    return pl.pallas_call(
        partial(exchange_kernel, count, bands),
        out_shape=(jax.ShapeDtypeStruct(sums.shape, F32),)
        + tuple(jax.ShapeDtypeStruct(edge.shape, edge.dtype) for edge in edges),
        in_specs=[VMEM_WHOLE] * 3 + [hbm] * count,
        out_specs=(VMEM_WHOLE,) + (hbm,) * count,
        scratch_shapes=[
            pltpu.VMEM((bands,) + sums.shape, F32),
            pltpu.SemaphoreType.DMA((bands,)),
            pltpu.SemaphoreType.DMA((bands,)),
            pltpu.SemaphoreType.DMA((max(count, 1), 2)),
            pltpu.SemaphoreType.DMA((max(count, 1), 2)),
        ],
        compiler_params=pltpu.CompilerParams(collective_id=count, has_side_effects=True),
        name="exchange",
    )(sums, weight, scale, *edges)

def rounded(field):
    return field.astype(BF)


def reduce_kernel(chunks, shapes, bands, groups, *refs):
    count = len(shapes)
    parts, table_ref = refs[:count], refs[count]
    outs, gathered = refs[count + 1 : 2 * count + 1], refs[2 * count + 1]
    refs = refs[2 * count + 2 :]
    pairs, crossed, summed, pieces = (refs[at * count : (at + 1) * count] for at in range(4))
    (slots, pair_send, pair_recv, cross_send, cross_recv, piece_send, piece_recv, back_send, back_recv,
     table_send, table_recv, far_send, far_recv) = refs[4 * count :]
    chips = bands // 2
    me = lax.axis_index("rows")
    group = lax.axis_index("heads")
    core, chip = lax.rem(me, 2), me // 2
    row_peers = [lax.rem(me + away, bands) for away in range(1, bands)]
    far_peers = [lax.rem(group + away, groups) for away in range(1, groups)]
    barrier = pltpu.get_barrier_semaphore()
    for axis, peers in (("rows", row_peers), ("heads", far_peers)):
        for peer in peers:
            pl.semaphore_signal(
                barrier, inc=1, device_id={axis: peer}, device_id_type=pl.DeviceIdType.MESH
            )
    pl.semaphore_wait(barrier, bands + groups - 2)

    def copy(src, dst, send, recv, axis, peer):
        return pltpu.make_async_remote_copy(
            src_ref=src,
            dst_ref=dst,
            send_sem=send,
            recv_sem=recv,
            device_id={axis: peer},
            device_id_type=pl.DeviceIdType.MESH,
        )

    def rows_of(band, size):
        return pl.ds(pl.multiple_of(band * size, 16), size)

    near = [
        copy(table_ref, slots.at[away], table_send.at[away], table_recv.at[away], "rows", peer)
        for away, peer in enumerate(row_peers)
    ]
    for item in near:
        item.start()
    stage_one = []
    for at, (which, first, wide) in enumerate(chunks):
        size = shapes[which][0] // bands
        cols = pl.ds(first, wide)
        own = []
        for spot in range(chips):
            own.append(
                copy(
                    parts[which].at[rows_of(2 * spot + 1 - core, size), cols],
                    pairs[which].at[spot, :, cols],
                    pair_send.at[at, spot],
                    pair_recv.at[at, spot],
                    "rows",
                    me + 1 - 2 * core,
                )
            )
        for item in own:
            item.start()
        stage_one.append(own)
    for item in near:
        item.wait_recv()
    total = table_ref[...]
    for away in range(bands - 1):
        total = total + slots[away]
    gathered[group] = total
    far = [
        copy(gathered.at[group], gathered.at[group], far_send.at[away], far_recv.at[away], "heads", peer)
        for away, peer in enumerate(far_peers)
    ]
    for item in far:
        item.start()
    def to_owner(at):
        which, first, wide = chunks[at]
        size = shapes[which][0] // bands
        cols = pl.ds(first, wide)
        for item in stage_one[at]:
            item.wait_recv()
        own = []
        for away in range(1, chips):
            spot = lax.rem(chip + away, chips)
            pairs[which][spot, :, cols] = (
                pairs[which][spot, :, cols].astype(F32)
                + parts[which][rows_of(2 * spot + core, size), cols].astype(F32)
            ).astype(BF)
            item = copy(
                pairs[which].at[spot, :, cols],
                crossed[which].at[away - 1, :, cols],
                cross_send.at[at, away - 1],
                cross_recv.at[at, away - 1],
                "rows",
                2 * spot + core,
            )
            item.start()
            own.append(item)
        stage_two.append(own)

    def to_groups(at):
        which, first, wide = chunks[at]
        size = shapes[which][0] // bands
        piece = size // groups
        cols = pl.ds(first, wide)
        for item in stage_two[at]:
            item.wait_recv()
        total = pairs[which][chip, :, cols].astype(F32) + parts[which][rows_of(me, size), cols].astype(F32)
        for away in range(chips - 1):
            total = total + crossed[which][away, :, cols].astype(F32)
        summed[which][:, cols] = total.astype(BF)
        own = []
        for away, peer in enumerate(far_peers):
            item = copy(
                summed[which].at[rows_of(peer, piece), cols],
                pieces[which].at[away, :, cols],
                piece_send.at[at, away],
                piece_recv.at[at, away],
                "heads",
                peer,
            )
            item.start()
            own.append(item)
        stage_three.append(own)

    def back_round(at):
        which, first, wide = chunks[at]
        piece = shapes[which][0] // bands // groups
        cols = pl.ds(first, wide)
        for item in stage_three[at]:
            item.wait_recv()
        mine = rows_of(group, piece)
        total = summed[which][mine, cols].astype(F32)
        for away in range(groups - 1):
            total = total + pieces[which][away, :, cols].astype(F32)
        outs[which][mine, cols] = total.astype(BF)
        own = []
        for away, peer in enumerate(far_peers):
            item = copy(
                outs[which].at[mine, cols],
                outs[which].at[mine, cols],
                back_send.at[at, away],
                back_recv.at[at, away],
                "heads",
                peer,
            )
            item.start()
            own.append(item)
        stage_four.append(own)

    stage_two, stage_three, stage_four = [], [], []
    steps = len(chunks)
    for at in range(steps + 3):
        if at < steps:
            to_owner(at)
        if 2 <= at + 1 and 0 <= at - 1 < steps:
            to_groups(at - 1)
        if 0 <= at - 3 < steps:
            back_round(at - 3)
    for away in range(groups - 1):
        source = lax.rem(group - (away + 1) + groups, groups)
        copy(
            gathered.at[source], gathered.at[source], far_send.at[away], far_recv.at[away], "heads", source
        ).wait_recv()
        for at, (which, first, wide) in enumerate(chunks):
            piece = shapes[which][0] // bands // groups
            theirs = outs[which].at[rows_of(source, piece), pl.ds(first, wide)]
            copy(theirs, theirs, back_send.at[at, away], back_recv.at[at, away], "heads", source).wait_recv()
    for item in near + far + sum(stage_one + stage_two + stage_three + stage_four, []):
        item.wait_send()


def reduce_fits(shapes, bands, groups):
    return bands % 2 == 0 and all(rows % (16 * bands * groups) == 0 for rows, _ in shapes)


def reduce_parts(parts, table, bands, groups):
    shapes = [part.shape for part in parts]
    chunks = []
    for which, (rows, cols) in enumerate(shapes):
        wide = cols if rows * cols < 1 << 19 else 512 if cols > 512 else 128
        chunks += [(which, first, wide) for first in range(0, cols, wide)]
    chips = bands // 2

    def scratch(lead, split):
        return [
            pltpu.VMEM(lead + (rows // bands // split, cols), BF) for rows, cols in shapes
        ]

    def sems(count):
        return [pltpu.SemaphoreType.DMA((len(chunks), count))] * 2

    return pl.pallas_call(
        partial(reduce_kernel, chunks, shapes, bands, groups),
        out_shape=tuple(jax.ShapeDtypeStruct((rows // bands, cols), BF) for rows, cols in shapes)
        + (jax.ShapeDtypeStruct((groups,) + table.shape, F32),),
        in_specs=[VMEM_WHOLE] * (len(parts) + 1),
        out_specs=(VMEM_WHOLE,) * (len(parts) + 1),
        scratch_shapes=scratch((chips,), 1)
        + scratch((chips - 1,), 1)
        + scratch((), 1)
        + scratch((groups - 1,), groups)
        + [pltpu.VMEM((bands - 1,) + table.shape, F32)]
        + sems(chips)
        + sems(chips - 1)
        + sems(groups - 1)
        + sems(groups - 1)
        + [pltpu.SemaphoreType.DMA((bands - 1,))] * 2
        + [pltpu.SemaphoreType.DMA((groups - 1,))] * 2,
        compiler_params=pltpu.CompilerParams(
            vmem_limit_bytes=56 << 20, collective_id=8, has_side_effects=True
        ),
        name="reduce_parts",
    )(*parts, table)


def halve_rows(packed, step):
    pairs = [(band, band ^ (1 << step)) for band in range(8)]
    return rounded(packed[0].astype(F32) + lax.ppermute(packed[1], "rows", pairs).astype(F32))


def sum_groups(part, step, groups):
    odd = lax.rem(lax.axis_index("heads"), 2)
    near = [(at, at ^ 1) for at in range(groups)]
    far = [(at, at ^ 2) for at in range(groups)]
    if step == 0:
        half = part.shape[0] // 2
        kept = lax.dynamic_slice_in_dim(part, odd * half, half, 0)
        sent = lax.dynamic_slice_in_dim(part, (1 - odd) * half, half, 0)
        return rounded(kept.astype(F32) + lax.ppermute(sent, "heads", near).astype(F32))
    if step == 1:
        return rounded(part.astype(F32) + lax.ppermute(part, "heads", far).astype(F32))
    other = lax.ppermute(part, "heads", near)
    return jnp.where(odd == 0, jnp.concatenate([part, other]), jnp.concatenate([other, part]))


def finish_kernel(width, place, sides, kept_ref, grad_ref, field_ref, avg_ref, back_avg, gain_ref, out_ref):
    at = pl.program_id(0)
    mean, inv_std = moments(avg_ref, at)
    back = back_avg[...]
    field_slope = inv_std * inv_std * row_of(back, 2 * at + 1)
    offset = inv_std * row_of(back, 2 * at) - mean * field_slope
    moved = grad_ref[0] * (inv_std * gain_ref[...]) - field_ref[0].astype(F32) * field_slope - offset
    inside = pixel_inside(moved.shape, place[0], sides[at], width)
    out_ref[0] = jnp.where(inside, kept_ref[0] + moved, 0.0)


def finish(place, sides, kept, grads, field, avg, back_avg, gain, width):
    images, tokens, channels = kept.shape
    tok = image_block(tokens, channels)
    table = table_block(channels)
    return pl.pallas_call(
        partial(finish_kernel, width),
        grid=(images,),
        out_shape=jax.ShapeDtypeStruct(kept.shape, F32),
        in_specs=[SMEM_WHOLE, SMEM_WHOLE, tok, tok, tok, table, table, table_block(channels, 1)],
        out_specs=tok,
        compiler_params=pltpu.CompilerParams(vmem_limit_bytes=32 << 20),
        name="finish",
    )(place, sides, kept, grads, field, avg, back_avg, gain)


def time_features(time_steps, dims):
    half_dim = dims // 2
    frequency = jnp.exp(-math.log(10000.0) * jnp.arange(half_dim, dtype=jnp.float32) / half_dim)
    angles = time_steps.astype(jnp.float32)[:, None] * frequency[None, :]
    return jnp.concatenate([jnp.cos(angles), jnp.sin(angles)], axis=-1)


def pad_rows(table):
    return jnp.pad(table, ((0, 8 - table.shape[0]), (0, 0)))


def to_items(sent, bands):
    images, heads = sent.shape[:2]
    per_band = heads * images // bands
    if bands == heads:
        parts = [sent[at] for at in range(images)]
    else:
        items = jnp.swapaxes(sent, 0, 1).reshape((bands, per_band) + sent.shape[2:])
        parts = [items[:, at] for at in range(per_band)]
    return [lax.all_to_all(part, "rows", split_axis=0, concat_axis=0, tiled=True) for part in parts]


def from_items(results, images, bands):
    back = [
        lax.all_to_all(result, "rows", split_axis=0, concat_axis=0, tiled=True)
        for result in results
    ]
    if bands == HEADS:
        return jnp.stack(back)
    joint = jnp.stack(back, axis=1)
    return jnp.swapaxes(joint.reshape((HEADS, images) + joint.shape[2:]), 0, 1)


def per_device(
    images,
    image_sides,
    labels,
    timesteps,
    cotangent,
    first_gain,
    first_bias,
    conv_one,
    time_proj,
    time_bias,
    second_gain,
    second_bias,
    conv_two,
    conv_bias,
    third_gain,
    third_bias,
    proj_in,
    proj_in_bias,
    attn_gain,
    attn_bias,
    qkv_proj,
    attn_out,
    attn_out_bias,
    class_table,
    cross_value,
    cross_out,
    feed_gain,
    feed_bias,
    geglu_proj,
    geglu_bias,
    feed_out,
    feed_out_bias,
    proj_out,
    proj_out_bias,
):
    image_count, band_rows, width, channels = images.shape
    tokens = band_rows * width
    head_dim = channels // HEADS
    score_scale = head_dim ** (-0.5)
    bands = lax.axis_size("rows")
    groups = lax.axis_size("heads")
    halving = bands == 8 and groups == 4
    me = lax.axis_index("rows")
    first_image = lax.axis_index("heads") * image_count
    sides = lax.dynamic_slice_in_dim(image_sides, first_image, image_count)
    place = jnp.stack([me * band_rows, me]).astype(jnp.int32)

    def vector(entries):
        return entries.astype(F32).reshape(1, -1)

    counts = 1.0 / (sides * sides * (channels // GROUPS)).astype(F32)
    scale = jnp.broadcast_to(pad_rows(jnp.repeat(counts, 2)[:, None]), (8, channels))
    ones = jnp.ones((1, channels), F32)
    field = images.reshape(image_count, tokens, channels)
    cot = cotangent.reshape(image_count, tokens, channels)

    def edges_of(whole):
        return jnp.stack([whole[:, 0], whole[:, -1]])

    hot = rounded(
        (labels[:, None] == jnp.arange(class_table.shape[0], dtype=jnp.int32)[None, :]).astype(F32)
    )
    context = jnp.dot(hot, class_table, preferred_element_type=F32)
    value = rounded(jnp.dot(rounded(context), cross_value, preferred_element_type=F32))
    cross = jnp.dot(value, cross_out, preferred_element_type=F32)
    cross = pad_rows(lax.dynamic_slice_in_dim(cross, first_image, image_count))
    embed = rounded(jax.nn.silu(time_features(timesteps, time_proj.shape[0])))
    shift = jnp.dot(embed, time_proj, preferred_element_type=F32) + time_bias.astype(F32)
    shift = pad_rows(lax.dynamic_slice_in_dim(shift, first_image, image_count))

    row_ids = me * band_rows + jnp.arange(band_rows, dtype=jnp.int32)
    col_ids = jnp.arange(width, dtype=jnp.int32)
    limit = sides[:, None, None]
    inside = ((row_ids[None, :, None] < limit) & (col_ids[None, None, :] < limit))[..., None]
    start = jnp.where(inside, images.astype(F32), 0.0)
    sums = jnp.stack([jnp.sum(start, axis=(1, 2)), jnp.sum(start * start, axis=(1, 2))], axis=1)
    sums = pad_rows(sums.reshape(2 * image_count, channels))

    avg_one, halo_images, halo_cot = exchange(
        sums, ones, scale, (edges_of(images), edges_of(cotangent)), bands
    )
    hidden, edge, sums = conv_forward(
        place, sides, field, halo_images, avg_one, vector(first_gain), vector(first_bias), conv_one,
        shift, None, width,
    )
    avg_two, halo_hidden = exchange(sums, ones, scale, (edge,), bands)
    residual, edge, sums = conv_forward(
        place, sides, hidden, halo_hidden, avg_two, vector(second_gain), vector(second_bias), conv_two,
        jnp.broadcast_to(vector(conv_bias), (8, channels)), field, width,
    )
    avg_three, halo_residual = exchange(sums, ones, scale, (edge,), bands)
    split = qkv_proj.reshape(channels, 3, HEADS, head_dim)
    turned_qkv = jnp.concatenate(
        [
            jnp.stack([split[:, 1], split[:, 2]], axis=2).reshape(channels, 2 * channels),
            qkv_proj[:, :channels],
        ],
        axis=1,
    )
    stream, sent = entry(
        residual, avg_three, vector(third_gain), vector(third_bias), proj_in, vector(proj_in_bias),
        vector(attn_gain), vector(attn_bias), turned_qkv,
    )
    chunks = to_items(sent, bands)
    first_item = me * len(chunks)
    item_sides = [
        lax.dynamic_slice_in_dim(sides, lax.rem(first_item + at, image_count), 1)
        for at in range(len(chunks))
    ]
    attended = [attend(side, chunk, width, score_scale) for side, chunk in zip(item_sides, chunks)]
    mixed = [pairs for pairs, _ in attended]
    (
        output, three, grad_chunks, feed_grads, feed_sums, cross_sum, pair_sums,
    ) = feed(
        place, sides, mixed, stream, residual, cot, cross, attn_out, vector(attn_out_bias),
        vector(feed_gain), vector(feed_bias), geglu_proj, vector(geglu_bias), feed_out,
        vector(feed_out_bias), proj_out, vector(proj_out_bias), width, bands, halving,
    )
    halved = feed_grads
    results = []
    for spot, (side, chunk, (_, norms)) in enumerate(zip(item_sides, chunks, attended)):
        if halving and spot in (1, 3):
            halved, norms = lax.optimization_barrier((halve_rows(halved, spot // 2), norms))
        results.append(attend_back(side, chunk, grad_chunks, spot, norms, width, score_scale))
    grad_qkv = from_items(results, image_count, bands)
    if halving:
        halved, grad_qkv = lax.optimization_barrier((halve_rows(halved, 2), grad_qkv))
        early = halved
    else:
        early = feed_grads.reshape((bands,) + feed_grads.shape[-2:])
        early = lax.psum_scatter(early, "rows", scatter_dimension=0, tiled=True)[0]
        early = lax.psum(early, "heads")
    moved, edge, third_sums, leave_sums, grad_qkv_proj, grad_proj_in = leave(
        place, sides, grad_qkv, stream, three, residual, avg_three, vector(third_gain),
        vector(third_bias), proj_in, vector(attn_gain), vector(attn_bias), turned_qkv, width,
    )
    if halving:
        early, third_sums = lax.optimization_barrier((sum_groups(early, 0, groups), third_sums))
    back_three, halo_moved = exchange(third_sums, vector(third_gain), scale, (edge,), bands)
    grad_residual, moved, edge, second_sums, residual_sums, grad_conv_two = conv_backward(
        place, sides, moved, halo_moved, residual, halo_residual, avg_three, back_three,
        vector(third_gain), cot, halo_cot, conv_two, hidden, avg_two, vector(second_gain),
        vector(second_bias), width,
    )
    if halving:
        early, second_sums = lax.optimization_barrier((sum_groups(early, 1, groups), second_sums))
    back_two, halo_moved = exchange(second_sums, vector(second_gain), scale, (edge,), bands)
    moved, _, first_sums, hidden_sums, grad_conv_one = conv_backward(
        place, sides, moved, halo_moved, hidden, halo_hidden, avg_two, back_two, vector(second_gain),
        None, None, conv_one, field, avg_one, vector(first_gain), vector(first_bias), width,
    )
    if halving:
        early, first_sums = lax.optimization_barrier((sum_groups(early, 2, groups), first_sums))
    (back_one,) = exchange(first_sums, vector(first_gain), scale, (), bands)
    grad_images = finish(
        place, sides, grad_residual, moved, field, avg_one, back_one, vector(first_gain), width
    ).reshape(images.shape)

    def own(whole, axis=0):
        size = whole.shape[axis] // bands
        return lax.dynamic_slice_in_dim(whole, me * size, size, axis)

    def reduced(part):
        part = lax.psum_scatter(part, "rows", scatter_dimension=0, tiled=True)
        return lax.psum(part, "heads").astype(F32)

    used = 2 * image_count
    table = jnp.concatenate(
        [
            cross_sum[:image_count],
            hidden_sums[:image_count],
            jnp.stack(
                [
                    jnp.sum(first_sums[1:used:2], axis=0),
                    jnp.sum(first_sums[0:used:2], axis=0),
                    jnp.sum(second_sums[1:used:2], axis=0),
                    jnp.sum(second_sums[0:used:2], axis=0),
                    jnp.sum(third_sums[1:used:2], axis=0),
                    jnp.sum(third_sums[0:used:2], axis=0),
                    jnp.sum(residual_sums[:image_count], axis=0),
                ]
            ),
            leave_sums[:3],
            feed_sums[:4],
            pair_sums.reshape(-1, channels),
        ]
    )
    table = jnp.pad(table, ((0, -table.shape[0] % 8), (0, 0)))
    late = (grad_conv_two, grad_conv_one, grad_qkv_proj, grad_proj_in)
    if reduce_fits([part.shape for part in late], bands, groups):
        grad_images, table = lax.optimization_barrier((grad_images, table))
        *late, table = reduce_parts(late, table, bands, groups)
        late = [part.astype(F32) for part in late]
    else:
        table = lax.all_gather(lax.psum(table, "rows"), "heads")
        late = [reduced(part) for part in late]
    rows_conv_two, rows_conv_one, rows_qkv, rows_proj_in = late
    rows_early = early.astype(F32)
    pieces = feed_pieces(channels, geglu_proj.shape[1], feed_out.shape[0], bands)
    rows_geglu = jnp.concatenate(
        [rows_early[first : first + size] for first, size in pieces[0]], axis=1
    )
    rows_feed, rows_proj_out, rows_attn_out = (
        rows_early[first : first + size] for ((first, size),) in pieces[1:]
    )
    all_cross = table[:, :image_count].reshape(-1, channels)
    all_shift = table[:, image_count : 2 * image_count].reshape(-1, channels)
    joint = jnp.sum(table[:, 2 * image_count :], axis=0)
    grad_cross_out = jnp.dot(own(value.astype(F32), 1).T, all_cross, precision=HIGH)
    grad_value = jnp.dot(all_cross, cross_out.astype(F32).T, precision=HIGH)
    grad_cross_value = jnp.dot(own(context, 1).T, grad_value, precision=HIGH)
    grad_context = jnp.dot(grad_value, own(cross_value).astype(F32).T, precision=HIGH)
    grad_class_table = jnp.dot(hot.astype(F32).T, grad_context, precision=HIGH)
    grad_time_proj = jnp.dot(own(embed.astype(F32), 1).T, all_shift, precision=HIGH)
    singles = [own(joint[at]) for at in range(14)]
    grad_geglu_bias = own(joint[14 : 14 + geglu_bias.shape[0] // channels].reshape(-1))
    keys_values = rows_qkv[:, : 2 * channels].reshape(-1, HEADS, 2, head_dim)
    rows_qkv = jnp.concatenate(
        [
            rows_qkv[:, 2 * channels :],
            keys_values[:, :, 0].reshape(-1, channels),
            keys_values[:, :, 1].reshape(-1, channels),
        ],
        axis=1,
    )
    return (
        output.reshape(images.shape),
        grad_images,
        singles[0],
        singles[1],
        rows_conv_one,
        grad_time_proj,
        own(jnp.sum(all_shift, axis=0)),
        singles[2],
        singles[3],
        rows_conv_two,
        singles[6],
        singles[4],
        singles[5],
        rows_proj_in,
        singles[9],
        singles[7],
        singles[8],
        rows_qkv,
        rows_attn_out,
        own(jnp.sum(all_cross, axis=0)),
        grad_class_table,
        grad_cross_value,
        grad_cross_out,
        singles[12],
        singles[13],
        rows_geglu,
        grad_geglu_bias,
        rows_feed,
        singles[11],
        rows_proj_out,
        singles[10],
    )


def solution(mesh):
    return jax.shard_map(
        per_device,
        mesh=mesh,
        in_specs=(
            P("heads", "rows", None, None),
            P(),
            P(),
            P(),
            P("heads", "rows", None, None),
            P(),
            P(),
            P(),
            P(),
            P(),
            P(),
            P(),
            P(),
            P(),
            P(),
            P(),
            P(),
            P(),
            P(),
            P(),
            P(),
            P(),
            P(),
            P(),
            P(),
            P(),
            P(),
            P(),
            P(),
            P(),
            P(),
            P(),
            P(),
            P(),
        ),
        out_specs=(
            P("heads", "rows", None, None),
            P("heads", "rows", None, None),
            P("rows"),
            P("rows"),
            P("rows", None),
            P("rows", None),
            P("rows"),
            P("rows"),
            P("rows"),
            P("rows", None),
            P("rows"),
            P("rows"),
            P("rows"),
            P("rows", None),
            P("rows"),
            P("rows"),
            P("rows"),
            P("rows", None),
            P("rows", None),
            P("rows"),
            P(None, "rows"),
            P("rows", None),
            P("rows", None),
            P("rows"),
            P("rows"),
            P("rows", None),
            P("rows"),
            P("rows", None),
            P("rows"),
            P("rows", None),
            P("rows"),
        ),
        check_vma=False,
    )
```

time: 1310 us -> 863 us (0.66); the launches traced: 1310 us -> 847 us
  Pallas kernels: 166 us -> 591 us
  blocking collectives: 276 us -> 0 us
  matrix products: 281 us -> 9.73 us
  other arithmetic: 173 us -> 35.4 us
  local copies, waits for them, and re-layouts: 181 us -> 64.5 us
  waiting for transfers between devices: 150 us -> 66.8 us
  between operations: 16.6 us -> 2.17 us
    pallas_call x0 -> x15, Pallas kernels: none -> 386 us  [the longest x1 100 us: reduce_parts(): pl.pallas_call(partial(reduce_kernel, chunks, shapes, bands, groups), out...]
    dot_general x35 -> x10, matrix products: 281 us -> 9.73 us  [the longest x1 1.8 us: per_device(): grad_cross_value = jnp.dot(own(context, 1).T, grad_value, precision=HIGH)]
    psum x7 -> x0, blocking collectives: 199 us -> none  [the longest x6 103 us: group_sums(): lax.psum((jnp.sum(first_term.reshape(shaped), axis=(1, 3)), jnp.sum(secon...]
    psum x1 -> x0, waiting for transfers between devices: 87.4 us -> none  [reduced(): return lax.psum(part, 'heads').astype(jnp.float32)]
    all_to_all x3 -> x0, blocking collectives: 63.6 us -> none  [to_items(): lax.all_to_all(items[:, at], 'rows', split_axis=0, concat_axis=0, tiled=T...]
    reduce_sum x26 -> x10, other arithmetic: 60.2 us -> 3.66 us  [the longest x1 0.95 us: per_device(): joint = jnp.sum(table[:, 2 * image_count:], axis=0)]
    unnamed x337 -> x161, local copies, waits for them, and re-layouts: 79.2 us -> 24 us
    ppermute x8 -> x6, waiting for transfers between devices: 4.27 us -> 37.6 us  [the longest x3 37.6 us: halve_rows(): lax.ppermute(packed[1], 'rows', pairs).astype(F32)]
  transfers between devices with their start and end apart: 30 -> 14, of which waited for: 10 -> 3; matrix products, arithmetic and copies ran while one was open for 23% -> 3% of each run, Pallas kernels for 13% -> 35%
where the time goes in v2:
time: 863 us; the launch traced here: 847 us
  Pallas kernels  591 us (68%)
  starting transfers between devices  77.4 us (9%)
  waiting for transfers between devices  66.8 us (8%)
  local copies, waits for them, and re-layouts  64.5 us (7%)
  other arithmetic  35.4 us (4%)
  matrix products  9.73 us (1%)
    pallas_call x4, Pallas kernels, attend_back(): pl.pallas_call(partial(attend_back_kernel, width, scale), out_shape=jax.S...  138 us
    pallas_call x1, Pallas kernels, reduce_parts(): pl.pallas_call(partial(reduce_kernel, chunks, shapes, bands, groups), out...  100 us
    pallas_call x1, Pallas kernels, feed(): pl.pallas_call(partial(feed_kernel, width, bands, per_band), grid=(images...  83 us
    pallas_call x6, Pallas kernels, exchange(): pl.pallas_call(partial(exchange_kernel, count, bands), out_shape=(jax.Sha...  74.6 us
    pallas_call x4, Pallas kernels, attend(): pl.pallas_call(partial(attend_kernel, width, scale), out_shape=(jax.Shape...  66.7 us
    pallas_call x2, Pallas kernels, conv_backward(): pl.pallas_call(partial(conv_backward_kernel, width, added), grid=(images,...  64.4 us
    ppermute x1, starting transfers between devices, sum_groups(): lax.ppermute(sent, 'heads', near).astype(F32)  40.7 us
    ppermute x3, waiting for transfers between devices, halve_rows(): lax.ppermute(packed[1], 'rows', pairs).astype(F32)  37.6 us
  transfers between devices with their start and end apart: 14, of which 3 were waited for; matrix products, arithmetic and copies ran while one was open for 3% of the time, Pallas kernels for 35%

profile of v2, /device:TPU:0, one launch (start us, length us, event | category | flops | bytes accessed | tf_op | source)
XLA Modules:
  0.0 846.9 jit_solution(13490107150737394323)
XLA Ops:
  19.3 19.3 %exchange.6 = (f32[8,512]{1,0:T(8,128)}, bf16[2,4,64,512]{3,2,1,0:T(8,128)(2,1)}, bf16[2,4,64,512]{3,2,1,0:T(8,128)(2,1)}) custom-call(f32[8,512]{1,0:T(8,128)} %reshape.277.sent_ref, f32[1,512]{1,0:T(1,128)} %broadcast_in_dim.24.weight_ref, f32[8,512]{1,0:T(8,128)} %broadcast_in_dim.44.scale_ref, bf16[2,4,64,512]{3,2,1,0:T(8,128)(2,1)} %get-tuple-element.211.refs_0_, ...), custom_call_target="tpu_custom_call" | custom-call | tf_op jit(solution)/shard_map/exchange/pallas_call | solution.py:1080
  38.6 15.5 %conv_forward.2 = (f32[4,512,512]{2,1,0:T(8,128)}, bf16[2,4,64,512]{3,2,1,0:T(8,128)(2,1)}, f32[8,512]{1,0:T(8,128)}) custom-call(s32[2]{0:T(128)} %pad_add_fusion.refs_0_.place, s32[4]{0:T(128)} %copy-done.21, bf16[4,512,512]{2,1,0:T(8,128)(2,1)} %bitcast.121, bf16[2,4,64,512]{3,2,1,0:T(8,128)(2,1)} %get-tuple-element.100.refs_3_, ...), custom_call_target="tpu_custom_call" | custom-call | tf_op jit(solution)/shard_map/conv_forward/pallas_call | solution.py:448
  54.1 12.1 %exchange.7 = (f32[8,512]{1,0:T(8,128)}, bf16[2,4,64,512]{3,2,1,0:T(8,128)(2,1)}) custom-call(f32[8,512]{1,0:T(8,128)} %get-tuple-element.103.sent_ref, f32[1,512]{1,0:T(1,128)} %broadcast_in_dim.24.weight_ref, f32[8,512]{1,0:T(8,128)} %broadcast_in_dim.44.scale_ref, bf16[2,4,64,512]{3,2,1,0:T(8,128)(2,1)} %get-tuple-element.104.refs_0_), custom_call_target="tpu_custom_call" | custom-call | tf_op jit(solution)/shard_map/exchange/pallas_call | solution.py:1080
  66.8 15.7 %conv_forward.3 = (f32[4,512,512]{2,1,0:T(8,128)}, bf16[2,4,64,512]{3,2,1,0:T(8,128)(2,1)}, f32[8,512]{1,0:T(8,128)}) custom-call(s32[2]{0:T(128)} %pad_add_fusion.refs_0_.place, s32[4]{0:T(128)} %copy-done.21, f32[4,512,512]{2,1,0:T(8,128)} %get-tuple-element.102.refs_2_.refs_12_.refs_4_, bf16[2,4,64,512]{3,2,1,0:T(8,128)(2,1)} %get-tuple-element.105.refs_3_.refs_5_, ...), custom_call_target="tpu_custom_call" | custom-call | tf_op jit(solution)/shard_map/conv_forward/pallas_call | solution.py:448
  82.6 12.1 %exchange.8 = (f32[8,512]{1,0:T(8,128)}, bf16[2,4,64,512]{3,2,1,0:T(8,128)(2,1)}) custom-call(f32[8,512]{1,0:T(8,128)} %get-tuple-element.108.sent_ref, f32[1,512]{1,0:T(1,128)} %broadcast_in_dim.24.weight_ref, f32[8,512]{1,0:T(8,128)} %broadcast_in_dim.44.scale_ref, bf16[2,4,64,512]{3,2,1,0:T(8,128)(2,1)} %get-tuple-element.109.refs_0_), custom_call_target="tpu_custom_call" | custom-call | tf_op jit(solution)/shard_map/exchange/pallas_call | solution.py:1080
  95.5 9.5 %entry.1 = (f32[4,512,512]{2,1,0:T(8,128)}, bf16[4,8,768,128]{3,2,1,0:T(8,128)(2,1)}) custom-call(f32[4,512,512]{2,1,0:T(8,128)} %get-tuple-element.107.field_ref.refs_5_.refs_3_.refs_4_, f32[8,512]{1,0:T(8,128)S(1)} %copy-done.17, f32[1,512]{1,0:T(1,128)S(1)} %bitcast.129, f32[1,512]{1,0:T(1,128)S(1)} %bitcast.133, bf16[512,512]{1,0:T(8,128)(2,1)S(1)} %copy-done.7, ...), custom_call_target="tpu_custom_call" | custom-call | tf_op jit(solution)/shard_map/entry/pallas_call | solution.py:635
  105.0 5.6 slice_bitcast_fusion.2
  121.1 14.3 %all-to-all-done.qkv_ref = bf16[8,768,128]{2,1,0:T(8,128)(2,1)S(1)} async-done(((bf16[8,768,128]{2,1,0:T(8,128)(2,1)}), bf16[8,768,128]{2,1,0:T(8,128)(2,1)S(1)}, u32[]{:S(2)}, u32[]{:S(2)}) %all-to-all-start) | async-done | bytes 1572896 | tf_op jit(solution)/shard_map/all_to_all | solution.py:1379
  135.4 4.3 all-to-all-start.1
  145.8 14.9 %all-to-all-done.1.qkv_ref = bf16[8,768,128]{2,1,0:T(8,128)(2,1)} async-done(((bf16[8,768,128]{2,1,0:T(8,128)(2,1)}), bf16[8,768,128]{2,1,0:T(8,128)(2,1)}, u32[]{:S(2)}, u32[]{:S(2)}) %all-to-all-start.1) | async-done | bytes 1572896 | tf_op jit(solution)/shard_map/all_to_all | solution.py:1379
  164.3 27.7 %attend.5 = (bf16[8,256,128]{2,1,0:T(8,128)(2,1)S(1)}, f32[4096,128]{1,0:T(8,128)S(1)}) custom-call(s32[1]{0:T(128)} %get-tuple-element.208.side_ref, bf16[8,768,128]{2,1,0:T(8,128)(2,1)} %all-to-all-done.1.qkv_ref), custom_call_target="tpu_custom_call" | custom-call | flops 17179869184 | bytes 8388608 | tf_op jit(solution)/shard_map/attend/pallas_call | solution.py:179
  200.8 26.7 %attend.6 = (bf16[8,256,128]{2,1,0:T(8,128)(2,1)S(1)}, f32[4096,128]{1,0:T(8,128)S(1)}) custom-call(s32[1]{0:T(128)} %get-tuple-element.210.side_ref, bf16[8,768,128]{2,1,0:T(8,128)(2,1)S(1)} %copy-done.11), custom_call_target="tpu_custom_call" | custom-call | flops 17179869184 | bytes 8388608 | tf_op jit(solution)/shard_map/attend/pallas_call | solution.py:179
  229.5 8.4 attend.7
  240.1 83.0 %feed.1 = (bf16[4,512,512]{2,1,0:T(8,128)(2,1)}, f32[4,512,512]{2,1,0:T(8,128)}, bf16[4,8,256,128]{3,2,1,0:T(8,128)(2,1)}, bf16[2,2,2,896,512]{4,3,2,1,0:T(8,128...) custom-call(s32[2]{0:T(128)} %pad_add_fusion.refs_0_.place, s32[4]{0:T(128)} %copy-done.21, ...), custom_call_target="tpu_custom_call" | custom-call | tf_op jit(solution)/shard_map/feed/pallas_call | solution.py:871
  323.1 10.0 %attend_back.4 = bf16[8,768,128]{2,1,0:T(8,128)(2,1)} custom-call(s32[1]{0:T(128)} %get-tuple-element.209.side_ref, bf16[8,768,128]{2,1,0:T(8,128)(2,1)} %copy-done.8, bf16[4,8,256,128]{3,2,1,0:T(8,128)(2,1)} %get-tuple-element.123.grad_ref, f32[4096,128]{1,0:T(8,128)} %copy-done.29), custom_call_target="tpu_custom_call" | custom-call | flops 42949672960 | bytes 10485760 | tf_op jit(solution)/shard_map/attend_back/pallas_call | solution.py:293
  339.4 53.2 %attend_back.6 = bf16[8,768,128]{2,1,0:T(8,128)(2,1)} custom-call(s32[1]{0:T(128)} %get-tuple-element.210.side_ref, bf16[8,768,128]{2,1,0:T(8,128)(2,1)} %copy-done.10, bf16[4,8,256,128]{3,2,1,0:T(8,128)(2,1)} %get-tuple-element.123.grad_ref, f32[4096,128]{1,0:T(8,128)} %copy-done.30), custom_call_target="tpu_custom_call" | custom-call | flops 42949672960 | bytes 10485760 | tf_op jit(solution)/shard_map/attend_back/pallas_call | solution.py:293
  392.6 4.3 fusion
  401.7 4.3 all-to-all-start.6
  406.0 53.7 %attend_back.5 = bf16[8,768,128]{2,1,0:T(8,128)(2,1)} custom-call(s32[1]{0:T(128)} %get-tuple-element.208.side_ref, bf16[8,768,128]{2,1,0:T(8,128)(2,1)} %all-to-all-done.1.qkv_ref, bf16[4,8,256,128]{3,2,1,0:T(8,128)(2,1)} %get-tuple-element.123.grad_ref, f32[4096,128]{1,0:T(8,128)} %copy-done.27), custom_call_target="tpu_custom_call" | custom-call | flops 42949672960 | bytes 10485760 | tf_op jit(solution)/shard_map/attend_back/pallas_call | solution.py:293
  461.7 4.3 all-to-all-start.5
  466.1 21.3 %attend_back.7 = bf16[8,768,128]{2,1,0:T(8,128)(2,1)} custom-call(s32[1]{0:T(128)} %get-tuple-element.207.side_ref, bf16[8,768,128]{2,1,0:T(8,128)(2,1)} %copy-done.9, bf16[4,8,256,128]{3,2,1,0:T(8,128)(2,1)} %get-tuple-element.123.grad_ref, f32[4096,128]{1,0:T(8,128)} %copy-done.28), custom_call_target="tpu_custom_call" | custom-call | flops 42949672960 | bytes 10485760 | tf_op jit(solution)/shard_map/attend_back/pallas_call | solution.py:293
  487.4 4.5 all-to-all-start.7
  494.0 37.6 %collective-permute-done.2 = bf16[896,512]{1,0:T(8,128)(2,1)} collective-permute-done((bf16[896,512]{1,0:T(8,128)(2,1)S(1)}, bf16[896,512]{1,0:T(8,128)(2,1)}, u32[]{:S(2)}, u32[]{:S(2)}) %collective-permute-start.2) | collective-permute-done | bytes 917536 | tf_op jit(solution)/shard_map/ppermute | solution.py:1316
  533.1 6.5 pad_maximum_fusion.refs_0_
  539.6 40.7 %collective-permute-start.3 = (bf16[448,512]{1,0:T(8,128)(2,1)S(1)}, bf16[448,512]{1,0:T(8,128)(2,1)S(1)}, u32[]{:S(2)}, u32[]{:S(2)}) collective-permute-start(bf16[448,512]{1,0:T(8,128)(2,1)S(1)} %constant_dynamic-slice_fusion.16), channel_id=1, source_target_pairs={{0,1},{1,0},{2,3},{3,2},{4,5},{5,4},{6,7},{7,6},{8,9},{9,8},{10,11... | collective-permute-start | bytes 1376264 | tf_op jit(solution)/shard_map/ppermute | solution.py:1327
  580.3 19.4 %leave.1 = (f32[4,512,512]{2,1,0:T(8,128)}, bf16[2,4,64,512]{3,2,1,0:T(8,128)(2,1)}, f32[8,512]{1,0:T(8,128)}, f32[8,512]{1,0:T(8,128)}, bf16[512,1536]{1,0:T(8,128)(2,1)}, /*index=5*/bf16[512,512]{1,0:T(8,128)(2,1)}) custom-call(s32[2]{0:T(128)} %pad_add_fusion.refs_0_.place, s32[4]{0:T(128)} %copy-done.21, ...), custom_call_target="tpu_custom_call" | custom-call | tf_op jit(solution)/shard_map/leave/pallas_call | solution.py:970
  600.0 12.1 %exchange.9 = (f32[8,512]{1,0:T(8,128)}, bf16[2,4,64,512]{3,2,1,0:T(8,128)(2,1)}) custom-call(f32[8,512]{1,0:T(8,128)} %get-tuple-element.133.sent_ref, f32[1,512]{1,0:T(1,128)} %bitcast.131, f32[8,512]{1,0:T(8,128)} %broadcast_in_dim.44.scale_ref, bf16[2,4,64,512]{3,2,1,0:T(8,128)(2,1)} %get-tuple-element.134.refs_0_), custom_call_target="tpu_custom_call" | custom-call | tf_op jit(solution)/shard_map/exchange/pallas_call | solution.py:1080
  612.2 32.7 %conv_backward.2 = (f32[4,512,512]{2,1,0:T(8,128)}, f32[4,512,512]{2,1,0:T(8,128)}, bf16[2,4,64,512]{3,2,1,0:T(8,128)(2,1)}, f32[8,512]{1,0:T(8,128)}, f32[8,512]{1,0:T(8,128)}, /*index=5*/bf16[4608,512]{1,0:T(8,128)(2,1)}) custom-call(s32[2]{0:T(128)} %pad_add_fusion.refs_0_.place, s32[4]{0:T(128)} %copy-done.21, ...), custom_call_target="tpu_custom_call" | custom-call | tf_op jit(solution)/shard_map/conv_backward/pallas_call | solution.py:576
  648.8 12.1 %exchange.10 = (f32[8,512]{1,0:T(8,128)}, bf16[2,4,64,512]{3,2,1,0:T(8,128)(2,1)}) custom-call(f32[8,512]{1,0:T(8,128)} %get-tuple-element.143.sent_ref, f32[1,512]{1,0:T(1,128)} %bitcast.150, f32[8,512]{1,0:T(8,128)} %broadcast_in_dim.44.scale_ref, bf16[2,4,64,512]{3,2,1,0:T(8,128)(2,1)} %get-tuple-element.144.refs_0_), custom_call_target="tpu_custom_call" | custom-call | tf_op jit(solution)/shard_map/exchange/pallas_call | solution.py:1080
  660.9 31.7 %conv_backward.3 = (f32[4,512,512]{2,1,0:T(8,128)}, bf16[2,4,64,512]{3,2,1,0:T(8,128)(2,1)}, f32[8,512]{1,0:T(8,128)}, f32[8,512]{1,0:T(8,128)}, bf16[4608,512]{1,0:T(8,128)(2,1)}) custom-call(s32[2]{0:T(128)} %pad_add_fusion.refs_0_.place, s32[4]{0:T(128)} %copy-done.21, f32[4,512,512]{2,1,0:T(8,128)} %get-tuple-element.140.refs_2_, ...), custom_call_target="tpu_custom_call" | custom-call | tf_op jit(solution)/shard_map/conv_backward/pallas_call | solution.py:576
  695.3 6.8 exchange.11.back_avg
  713.3 100.3 %reduce_parts.1 = (bf16[576,512]{1,0:T(8,128)(2,1)}, bf16[576,512]{1,0:T(8,128)(2,1)}, bf16[64,1536]{1,0:T(8,128)(2,1)}, bf16[64,512]{1,0:T(8,128)(2,1)}, f32[4,32,512]{2,1,0:T(8,128)}) custom-call(bf16[4608,512]{1,0:T(8,128)(2,1)} %get-tuple-element.158.refs_0_, bf16[4608,512]{1,0:T(8,128)(2,1)} %get-tuple-element.159.refs_1_, ...), custom_call_target="tpu_custom_call" | custom-call | tf_op jit(solution)/shard_map/reduce_parts/pallas_call | solution.py:1290
  (310 shorter events, 120.1 us)
Async XLA Ops:
  0.7 13.6 %copy-start = (bf16[1024,512]{1,0:T(8,128)(2,1)S(1)}, bf16[1024,512]{1,0:T(8,128)(2,1)}, u32[]{:S(2)}) copy-start(bf16[1024,512]{1,0:T(8,128)(2,1)} %param.42) | copy-start | bytes 3145732
  6.4 88.3 %copy-start.20 = (f32[512]{0:T(512)}, f32[512]{0:T(512)S(1)}, u32[]{:S(2)}) copy-start(f32[512]{0:T(512)S(1)} %reshape.326) | copy-start | bytes 6148
  6.4 88.3 %copy-start.24 = (f32[512]{0:T(512)}, f32[512]{0:T(512)S(1)}, u32[]{:S(2)}) copy-start(f32[512]{0:T(512)S(1)} %reshape.328) | copy-start | bytes 6148
  6.5 88.3 %copy-start.25 = (f32[512]{0:T(512)}, f32[512]{0:T(512)S(1)}, u32[]{:S(2)}) copy-start(f32[512]{0:T(512)S(1)} %reshape.332) | copy-start | bytes 6148
  6.5 88.2 %copy-start.26 = (f32[512]{0:T(512)}, f32[512]{0:T(512)S(1)}, u32[]{:S(2)}) copy-start(f32[512]{0:T(512)S(1)} %reshape.334) | copy-start | bytes 6148
  16.9 77.9 %copy-start.4 = (bf16[512,1536]{1,0:T(8,128)(2,1)}, bf16[512,1536]{1,0:T(8,128)(2,1)S(1)}, u32[]{:S(2)}) copy-start(bf16[512,1536]{1,0:T(8,128)(2,1)S(1)} %pad_maximum_fusion.1.qkv_ref.refs_10_) | copy-start | bytes 4718596
  38.6 27.6 %copy-start.68 = (bf16[512]{0:T(512)(128)(2,1)S(1)}, bf16[512]{0:T(512)(128)(2,1)}, u32[]{:S(2)}) copy-start(bf16[512]{0:T(512)(128)(2,1)} %param.47) | copy-start | bytes 3076
  66.8 27.9 %copy-start.7 = (bf16[512,512]{1,0:T(8,128)(2,1)S(1)}, bf16[512,512]{1,0:T(8,128)(2,1)}, u32[]{:S(2)}) copy-start(bf16[512,512]{1,0:T(8,128)(2,1)} %refs_7_.5) | copy-start | bytes 1572868
  110.7 24.7 %all-to-all-start = ((bf16[8,768,128]{2,1,0:T(8,128)(2,1)}), bf16[8,768,128]{2,1,0:T(8,128)(2,1)S(1)}, u32[]{:S(2)}, u32[]{:S(2)}) async-start(bf16[8,768,128]{2,1,0:T(8,128)(2,1)} %get-tuple-element.180), calls=%async_computation | async-start | bytes 3145728 | tf_op jit(solution)/shard_map/all_to_all | solution.py:1379
  135.4 25.3 %all-to-all-start.1 = ((bf16[8,768,128]{2,1,0:T(8,128)(2,1)}), bf16[8,768,128]{2,1,0:T(8,128)(2,1)}, u32[]{:S(2)}, u32[]{:S(2)}) async-start(bf16[8,768,128]{2,1,0:T(8,128)(2,1)} %get-tuple-element.179), calls=%async_computation.1 | async-start | bytes 3145728 | tf_op jit(solution)/shard_map/all_to_all | solution.py:1379
  160.7 33.4 %all-to-all-start.2 = ((bf16[8,768,128]{2,1,0:T(8,128)(2,1)}), bf16[8,768,128]{2,1,0:T(8,128)(2,1)S(1)}, u32[]{:S(2)}, u32[]{:S(2)}) async-start(bf16[8,768,128]{2,1,0:T(8,128)(2,1)} %get-tuple-element.178), calls=%async_computation.2 | async-start | bytes 3145728 | tf_op jit(solution)/shard_map/all_to_all | solution.py:1379
  195.3 34.3 %all-to-all-start.3 = ((bf16[8,768,128]{2,1,0:T(8,128)(2,1)}), bf16[8,768,128]{2,1,0:T(8,128)(2,1)S(1)}, u32[]{:S(2)}, u32[]{:S(2)}) async-start(bf16[8,768,128]{2,1,0:T(8,128)(2,1)} %get-tuple-element.177), calls=%async_computation.3 | async-start | bytes 3145728 | tf_op jit(solution)/shard_map/all_to_all | solution.py:1379
  333.0 68.6 %all-to-all-start.4 = ((bf16[8,768,128]{2,1,0:T(8,128)(2,1)}), bf16[8,768,128]{2,1,0:T(8,128)(2,1)S(1)}, u32[]{:S(2)}, u32[]{:S(2)}) async-start(bf16[8,768,128]{2,1,0:T(8,128)(2,1)} %attend_back.4), calls=%async_computation.4 | async-start | bytes 3145728 | tf_op jit(solution)/shard_map/all_to_all | solution.py:1384
  338.9 53.7 %collective-permute-start = (bf16[2,2,896,512]{3,2,1,0:T(8,128)(2,1)S(1)}, bf16[2,2,896,512]{3,2,1,0:T(8,128)(2,1)}, u32[]{:S(2)}, u32[]{:S(2)}) collective-permute-start(bf16[2,2,896,512]{3,2,1,0:T(8,128)(2,1)S(1)} %slice_bitcast_fusion), channel_id=1, source_target_pairs={{0,4},{4,0},{8,12},{12,8},{16,20},{20,16},{24,28},{28,24},{1,5},{5... | collective-permute-start | bytes 11010056 | tf_op jit(solution)/shard_map/ppermute | solution.py:1316
  400.1 59.6 %collective-permute-start.1 = (bf16[2,896,512]{2,1,0:T(8,128)(2,1)}, bf16[2,896,512]{2,1,0:T(8,128)(2,1)}, u32[]{:S(2)}, u32[]{:S(2)}) collective-permute-start(bf16[2,896,512]{2,1,0:T(8,128)(2,1)} %slice_bitcast_fusion.1), channel_id=1, source_target_pairs={{0,8},{4,12},{8,0},{12,4},{16,24},{20,28},{24,16},{28,20},{1,9},{5... | collective-permute-start | bytes 5505032 | tf_op jit(solution)/shard_map/ppermute | solution.py:1316
  401.7 58.0 %copy-start.33 = (bf16[8,768,128]{2,1,0:T(8,128)(2,1)}, bf16[8,768,128]{2,1,0:T(8,128)(2,1)S(1)}, u32[]{:S(2)}) copy-start(bf16[8,768,128]{2,1,0:T(8,128)(2,1)S(1)} %all-to-all-done.4) | copy-start | bytes 4718596
  401.7 60.1 %all-to-all-start.6 = ((bf16[8,768,128]{2,1,0:T(8,128)(2,1)}), bf16[8,768,128]{2,1,0:T(8,128)(2,1)}, u32[]{:S(2)}, u32[]{:S(2)}) async-start(bf16[8,768,128]{2,1,0:T(8,128)(2,1)} %attend_back.6), calls=%async_computation.6 | async-start | bytes 3145728 | tf_op jit(solution)/shard_map/all_to_all | solution.py:1384
  406.0 53.7 %copy-start.32 = (bf16[2,2,896,512]{3,2,1,0:T(8,128)(2,1)S(1)}, bf16[2,2,896,512]{3,2,1,0:T(8,128)(2,1)}, u32[]{:S(2)}) copy-start(bf16[2,2,896,512]{3,2,1,0:T(8,128)(2,1)} %copy-done.31) | copy-start | bytes 11010052
  461.7 25.6 %all-to-all-start.5 = ((bf16[8,768,128]{2,1,0:T(8,128)(2,1)}), bf16[8,768,128]{2,1,0:T(8,128)(2,1)}, u32[]{:S(2)}, u32[]{:S(2)}) async-start(bf16[8,768,128]{2,1,0:T(8,128)(2,1)} %attend_back.5), calls=%async_computation.5 | async-start | bytes 3145728 | tf_op jit(solution)/shard_map/all_to_all | solution.py:1384
  487.4 45.7 %all-to-all-start.7 = ((bf16[8,768,128]{2,1,0:T(8,128)(2,1)}), bf16[8,768,128]{2,1,0:T(8,128)(2,1)}, u32[]{:S(2)}, u32[]{:S(2)}) async-start(bf16[8,768,128]{2,1,0:T(8,128)(2,1)} %attend_back.7), calls=%async_computation.7 | async-start | bytes 3145728 | tf_op jit(solution)/shard_map/all_to_all | solution.py:1384
  492.0 39.7 %collective-permute-start.2 = (bf16[896,512]{1,0:T(8,128)(2,1)S(1)}, bf16[896,512]{1,0:T(8,128)(2,1)}, u32[]{:S(2)}, u32[]{:S(2)}) collective-permute-start(bf16[896,512]{1,0:T(8,128)(2,1)S(1)} %slice_bitcast_fusion.6), channel_id=1, source_target_pairs={{0,16},{4,20},{8,24},{12,28},{16,0},{20,4},{24,8},{28,12},{1,17},{... | collective-permute-start | bytes 2752520 | tf_op jit(solution)/shard_map/ppermute | solution.py:1316
  539.6 60.1 %collective-permute-start.3 = (bf16[448,512]{1,0:T(8,128)(2,1)S(1)}, bf16[448,512]{1,0:T(8,128)(2,1)S(1)}, u32[]{:S(2)}, u32[]{:S(2)}) collective-permute-start(bf16[448,512]{1,0:T(8,128)(2,1)S(1)} %constant_dynamic-slice_fusion.16), channel_id=1, source_target_pairs={{0,1},{1,0},{2,3},{3,2},{4,5},{5,4},{6,7},{7,6},{8,9},{9,8},{10,11... | collective-permute-start | bytes 1376264 | tf_op jit(solution)/shard_map/ppermute | solution.py:1327
  599.9 45.0 %collective-permute-start.4 = (bf16[448,512]{1,0:T(8,128)(2,1)S(1)}, bf16[448,512]{1,0:T(8,128)(2,1)S(1)}, u32[]{:S(2)}, u32[]{:S(2)}) collective-permute-start(bf16[448,512]{1,0:T(8,128)(2,1)S(1)} %add_convert_fusion.1), channel_id=1, source_target_pairs={{0,2},{1,3},{2,0},{3,1},{4,6},{5,7},{6,4},{7,5},{8,10},{9,11},{10,... | collective-permute-start | bytes 1376264 | tf_op jit(solution)/shard_map/ppermute | solution.py:1329
  612.1 33.0 %copy-start.54 = (f32[8,512]{1,0:T(8,128)S(1)}, f32[8,512]{1,0:T(8,128)}, u32[]{:S(2)}) copy-start(f32[8,512]{1,0:T(8,128)} %get-tuple-element.151) | copy-start | bytes 49156
  612.1 33.0 %copy-start.53 = (f32[8,512]{1,0:T(8,128)S(1)}, f32[8,512]{1,0:T(8,128)}, u32[]{:S(2)}) copy-start(f32[8,512]{1,0:T(8,128)} %get-tuple-element.155) | copy-start | bytes 49156
  612.1 33.6 %copy-start.50 = (f32[1,4096]{1,0:T(1,128)S(1)}, f32[1,4096]{1,0:T(1,128)}, u32[]{:S(2)}) copy-start(f32[1,4096]{1,0:T(1,128)} %get-tuple-element.156) | copy-start | bytes 49156
  612.1 34.3 %copy-start.55 = (f32[8,512]{1,0:T(8,128)S(1)}, f32[8,512]{1,0:T(8,128)}, u32[]{:S(2)}) copy-start(f32[8,512]{1,0:T(8,128)} %get-tuple-element.154) | copy-start | bytes 49156
  612.2 34.3 %copy-start.48 = (f32[8,512]{1,0:T(8,128)S(1)}, f32[8,512]{1,0:T(8,128)}, u32[]{:S(2)}) copy-start(f32[8,512]{1,0:T(8,128)} %get-tuple-element.133.sent_ref) | copy-start | bytes 49156
  645.0 47.5 %copy-start.37 = (bf16[448,512]{1,0:T(8,128)(2,1)}, bf16[448,512]{1,0:T(8,128)(2,1)S(1)}, u32[]{:S(2)}) copy-start(bf16[448,512]{1,0:T(8,128)(2,1)S(1)} %add_convert_fusion) | copy-start | bytes 1376260
  645.0 48.4 %collective-permute-start.5 = (bf16[448,512]{1,0:T(8,128)(2,1)S(1)}, bf16[448,512]{1,0:T(8,128)(2,1)}, u32[]{:S(2)}, u32[]{:S(2)}) collective-permute-start(bf16[448,512]{1,0:T(8,128)(2,1)S(1)} %add_convert_fusion), channel_id=1, source_target_pairs={{0,1},{1,0},{2,3},{3,2},{4,5},{5,4},{6,7},{7,6},{8,9},{9,8},{10,11... | collective-permute-start | bytes 1376264 | tf_op jit(solution)/shard_map/ppermute | solution.py:1330
  692.6 12.0 %copy-start.3 = (bf16[4,8,64,512]{3,2,1,0:T(8,128)(2,1)S(1)}, bf16[4,8,64,512]{3,2,1,0:T(8,128)(2,1)}, u32[]{:S(2)}) copy-start(bf16[4,8,64,512]{3,2,1,0:T(8,128)(2,1)} %param.34) | copy-start | bytes 6291460
  713.3 102.3 %copy-start.36 = (bf16[512,512]{1,0:T(8,128)(2,1)S(1)}, bf16[512,512]{1,0:T(8,128)(2,1)}, u32[]{:S(2)}) copy-start(bf16[512,512]{1,0:T(8,128)(2,1)} %param.59) | copy-start | bytes 1572868
  (58 other events, 261.2 us)
